TPU v7x, 512 devices: a whole 4x8x8 slice. The times are simulated.
512 devices in a mesh: dp: 64 (over z, y), mp: 8 (over x, core).
Axes of the slice: x: 4, y: 8, z: 8, core: 2. Of those that a mesh axis runs over, the one named last changes fastest.
Arguments:
- old_weight: float32 [24576, 3584], P('dp', 'mp'), may hold values from -6 to 6
- old_first: float32 [24576, 3584], P('dp', 'mp'), may hold values from -6 to 6
- old_second: float32 [24576, 3584], P('dp', 'mp'), may hold values from 0.1 to 3
- old_offsets: int32 [25], replicated, may hold values from 0 to 8192, as said below
- activations: bfloat16 [8192, 8192], P(('dp', 'mp')), may hold values from -6 to 6
- upstream: bfloat16 [8192, 3584], P('dp', 'mp'), may hold values from -0.0625 to 0.0625
Outputs:
- new_weight: float32 [8192, 3584], P('dp', 'mp')
- new_first: float32 [8192, 3584], P('dp', 'mp')
- new_second: float32 [8192, 3584], P('dp', 'mp')
- act_grad: bfloat16 [8192, 8192], P('mp', 'dp')
Inputs may be any that keep to these rules, and one draw needn't show every extreme that they name: old_offsets rises from 0 to 8192; shard k holds rows old_offsets[k] to old_offsets[k+1] - 1 in the slots of dp index k; each shard has at most 384 rows, and one has exactly 384.
All inputs are finite; a program needn't handle non-finite values.
Results may differ from a plain program's by a relative error of at most 0.0049.
Values may be sent and summed in bfloat16 or wider, within the bound.
No kernel may reach another device: no remote copies, remote signals or barrier semaphores. Data moves between devices by JAX's collectives and lax.ppermute only.
A program may use at most 64 MiB of HBM per device.

v0:
```python
import jax
import jax.numpy as jnp
from jax import lax
from jax.sharding import PartitionSpec as P

D = 8192
STEP = 24


beta_one = 0.9
beta_two = 0.95
epsilon = 1e-08
learn_rate = 0.05
decay_rate = 0.2


def place_rows(strips, old_offsets, capacity):
    shard_count = old_offsets.shape[0] - 1
    initial = tuple((jnp.zeros((strip.shape[0], D + capacity), strip.dtype) for strip in strips))

    def place_one(index, placed):
        begin = old_offsets[index]
        result = []
        for strip, target in zip(strips, placed):
            block = lax.dynamic_slice_in_dim(strip, index * capacity, capacity, 1)
            result.append(lax.dynamic_update_slice_in_dim(target, block, begin, 1))
        return tuple(result)

    placed = lax.fori_loop(0, shard_count, place_one, initial)
    return tuple((target[:, :D] for target in placed))


def adamw_update(weight, moment_one, moment_two, gradient):
    first_new = beta_one * moment_one + (1.0 - beta_one) * gradient
    second_new = beta_two * moment_two + (1.0 - beta_two) * gradient * gradient
    first_hat = first_new / (1.0 - beta_one**STEP)
    second_hat = second_new / (1.0 - beta_two**STEP)
    weight_new = weight - learn_rate * (
        first_hat / (jnp.sqrt(second_hat) + epsilon) + decay_rate * weight
    )
    return (weight_new, first_new, second_new)


def shards(old_weight, old_first, old_second, old_offsets, activations, upstream):
    groups = lax.axis_size("dp")
    splits = lax.axis_size("mp")
    capacity = old_weight.shape[0]
    new_rows = D // groups
    strips = (
        lax.all_to_all(old_weight.T, "dp", split_axis=0, concat_axis=1, tiled=True),
        lax.all_to_all(old_first.T, "dp", split_axis=0, concat_axis=1, tiled=True),
        lax.all_to_all(old_second.T, "dp", split_axis=0, concat_axis=1, tiled=True),
    )
    placed = place_rows(strips, old_offsets, capacity)
    weight_t, first_t, second_t = lax.all_to_all(
        placed, "dp", split_axis=1, concat_axis=0, tiled=True
    )
    weight = weight_t.T
    moment_one = first_t.T
    moment_two = second_t.T
    weight_half = weight.astype(jnp.bfloat16)
    token_count = activations.shape[0]
    token_rows = lax.all_to_all(activations, "dp", split_axis=1, concat_axis=0, tiled=True)
    gathered = lax.all_gather(token_rows, "mp", axis=0, tiled=True)
    ordered = gathered.reshape(splits, groups, token_count, new_rows).transpose(1, 0, 2, 3)
    ordered = ordered.reshape(splits * groups * token_count, new_rows)
    all_upstream = lax.all_gather(upstream, "dp", axis=0, tiled=True)
    gradient = lax.dot_general(
        ordered, all_upstream, (((0,), (0,)), ((), ())), preferred_element_type=jnp.float32
    )
    partial_sums = lax.dot_general(
        all_upstream, weight_half, (((1,), (1,)), ((), ())), preferred_element_type=jnp.float32
    )
    act_grad = lax.psum_scatter(partial_sums, "mp", scatter_dimension=0, tiled=True).astype(
        jnp.bfloat16
    )
    weight_new, first_new, second_new = adamw_update(weight, moment_one, moment_two, gradient)
    return (weight_new, first_new, second_new, act_grad)


def solution(mesh):
    return jax.shard_map(
        shards,
        mesh=mesh,
        in_specs=(
            P("dp", "mp"),
            P("dp", "mp"),
            P("dp", "mp"),
            P(),
            P(("dp", "mp"), None),
            P("dp", "mp"),
        ),
        out_specs=(P("dp", "mp"), P("dp", "mp"), P("dp", "mp"), P("mp", "dp")),
        check_vma=False,
    )
```

profile of v0, /device:TPU:2, one launch (start us, length us, event | category | flops | bytes accessed | tf_op | source)
XLA Modules:
  0.0 312.7 jit_solution(2772820204538000760)
XLA Ops:
  8.1 0.7 copy_bitcast_fusion
  8.9 16.6 %all-to-all-start.5 = ((bf16[16,64,128]{2,0,1:T(8,128)(2,1)}), bf16[16,64,128]{2,0,1:T(8,128)(2,1)S(1)}, u32[]{:S(2)}, u32[]{:S(2)}) async-start(bf16[16,64,128]{2,0,1:T(8,128)(2,1)} %copy_bitcast_fusion), calls=%async_computation.5 | async-start | bytes 524288 | tf_op jit(solution)/shard_map/all_to_all | solution.py:63
  25.5 2.1 all_to_all.90
  27.6 12.8 %all-to-all-done.5 = bf16[16,64,128]{2,0,1:T(8,128)(2,1)S(1)} async-done(((bf16[16,64,128]{2,0,1:T(8,128)(2,1)}), bf16[16,64,128]{2,0,1:T(8,128)(2,1)S(1)}, u32[]{:S(2)}, u32[]{:S(2)}) %all-to-all-start.5) | async-done | bytes 262176 | tf_op jit(solution)/shard_map/all_to_all | solution.py:63
  40.4 4.6 %all-to-all-start = ((f32[64,7,384]{2,1,0:T(8,128)}), f32[64,7,384]{2,1,0:T(8,128)S(1)}, u32[]{:S(2)}, u32[]{:S(2)}) async-start(f32[64,7,384]{2,1,0:T(8,128)} %all_to_all.90), calls=%async_computation | async-start | bytes 1572864 | tf_op jit(solution)/shard_map/all_to_all | solution.py:50
  45.0 2.1 all_to_all.94
  47.2 22.4 %all-to-all-done = f32[64,7,384]{2,1,0:T(8,128)S(1)} async-done(((f32[64,7,384]{2,1,0:T(8,128)}), f32[64,7,384]{2,1,0:T(8,128)S(1)}, u32[]{:S(2)}, u32[]{:S(2)}) %all-to-all-start) | async-done | bytes 688160 | tf_op jit(solution)/shard_map/all_to_all | solution.py:50
  69.6 6.6 %all-to-all-start.1 = ((f32[64,7,384]{2,1,0:T(8,128)}), f32[64,7,384]{2,1,0:T(8,128)S(1)}, u32[]{:S(2)}, u32[]{:S(2)}) async-start(f32[64,7,384]{2,1,0:T(8,128)} %all_to_all.94), calls=%async_computation.1 | async-start | bytes 1572864 | tf_op jit(solution)/shard_map/all_to_all | solution.py:51
  76.3 1.0 all_to_all.98
  77.3 26.7 %all-to-all-done.1 = f32[64,7,384]{2,1,0:T(8,128)S(1)} async-done(((f32[64,7,384]{2,1,0:T(8,128)}), f32[64,7,384]{2,1,0:T(8,128)S(1)}, u32[]{:S(2)}, u32[]{:S(2)}) %all-to-all-start.1) | async-done | bytes 688160 | tf_op jit(solution)/shard_map/all_to_all | solution.py:51
  104.0 6.8 %all-to-all-start.2 = ((f32[64,7,384]{2,1,0:T(8,128)}), f32[64,7,384]{2,1,0:T(8,128)S(1)}, u32[]{:S(2)}, u32[]{:S(2)}) async-start(f32[64,7,384]{2,1,0:T(8,128)} %all_to_all.98), calls=%async_computation.2 | async-start | bytes 1572864 | tf_op jit(solution)/shard_map/all_to_all | solution.py:52
  111.6 28.5 %all-to-all-done.2 = f32[64,7,384]{2,1,0:T(8,128)S(1)} async-done(((f32[64,7,384]{2,1,0:T(8,128)}), f32[64,7,384]{2,1,0:T(8,128)S(1)}, u32[]{:S(2)}, u32[]{:S(2)}) %all-to-all-start.2) | async-done | bytes 688160 | tf_op jit(solution)/shard_map/all_to_all | solution.py:52
  140.1 91.5 %while.17 = (s32[]{:T(128)}, f32[7,8576]{1,0:T(8,128)S(1)}, f32[7,8576]{1,0:T(8,128)S(1)}, f32[7,8576]{1,0:T(8,128)S(1)}, f32[7,24576]{1,0:T(8,128)S(1)}, /*inde...) while((s32[]{:T(128)}, f32[7,8576]{1,0:T(8,128)S(1)}, ...), condition=%wide.region_1.0_spmd, body=%wide.region_0.0_spmd.sunk | while | flops 9 | bytes 129261 | solution.py:29
  231.7 20.5 %all_to_all.121 = f32[7,64,128]{2,0,1:T(8,128)S(1)} all-to-all(f32[7,64,128]{2,0,1:T(8,128)S(1)} %slice_bitcast_fusion.2), channel_id=1, replica_groups=mesh['dp'=64,'mp'=8] {'dp'}, dimensions={1} | all-to-all | bytes 458752 | tf_op jit(solution)/shard_map/all_to_all | solution.py:55
  252.3 6.4 %convolution_bitcast_fusion = f32[8192,128]{0,1:T(8,128)} fusion(bf16[8192,448]{0,1:T(8,128)(2,1)} %all-gather.5.cloned.1.call-done, f32[448,128]{1,0:T(8,128)S(1)} %all_to_all.105), kind=kOutput, calls=%fused_computation.3 | convolution fusion | flops 939524096 | bytes 11763712 | tf_op jit(solution)/shard_map/dot_general | solution.py:71
  259.5 4.6 %all-to-all-start.4 = ((f32[7,64,128]{2,0,1:T(8,128)}), f32[7,64,128]{2,0,1:T(8,128)S(1)}, u32[]{:S(2)}, u32[]{:S(2)}) async-start(f32[7,64,128]{2,0,1:T(8,128)} %slice_bitcast_fusion.1), calls=%async_computation.4 | async-start | bytes 524288 | tf_op jit(solution)/shard_map/all_to_all | solution.py:55
  264.1 0.7 slice_bitcast_fusion
  264.8 12.9 %all-to-all-done.4 = f32[7,64,128]{2,0,1:T(8,128)S(1)} async-done(((f32[7,64,128]{2,0,1:T(8,128)}), f32[7,64,128]{2,0,1:T(8,128)S(1)}, u32[]{:S(2)}, u32[]{:S(2)}) %all-to-all-start.4) | async-done | bytes 229408 | tf_op jit(solution)/shard_map/all_to_all | solution.py:55
  277.7 4.8 %all-to-all-start.6 = ((f32[7,64,128]{2,0,1:T(8,128)}), f32[7,64,128]{2,0,1:T(8,128)S(1)}, u32[]{:S(2)}, u32[]{:S(2)}) async-start(f32[7,64,128]{2,0,1:T(8,128)} %slice_bitcast_fusion), calls=%async_computation.6 | async-start | bytes 524288 | tf_op jit(solution)/shard_map/all_to_all | solution.py:55
  282.6 13.3 %all-to-all-done.6 = f32[7,64,128]{2,0,1:T(8,128)S(1)} async-done(((f32[7,64,128]{2,0,1:T(8,128)}), f32[7,64,128]{2,0,1:T(8,128)S(1)}, u32[]{:S(2)}, u32[]{:S(2)}) %all-to-all-start.6) | async-done | bytes 229408 | tf_op jit(solution)/shard_map/all_to_all | solution.py:55
  296.0 2.2 copy.31
  298.2 6.0 %bitcast_subtract_fusion = (f32[128,448]{0,1:T(8,128)}, f32[128,448]{0,1:T(8,128)}, f32[128,448]{0,1:T(8,128)}) fusion(f32[448,128]{1,0:T(8,128)S(1)} %all_to_all.105, f32[448,128]{1,0:T(8,128)S(1)} %mul.63, f32[448,128]{1,0:T(8,128)S(1)} %mul.70, bf16[8192,448]{0,1:T(8,128)(2,1)} %all-gather.5.cloned.1.call-done, bf16[8192,128]{1,0:T(8,128)(2,1)S(1)} %bitcast.70), kind=kOutput, calls=%fused_computation.14 | convolution fusion | flops 940269568 | bytes 10813440 | tf_op jit(solution)/shard_map/dot_general | solution.py:68
  304.2 1.1 convert_element_type.7
  305.3 0.8 copy.33
  (171 shorter events, 46.0 us)
Async XLA Ops:
  7.2 1.0 copy-start
  7.2 69.1 %copy-start.2 = (f32[384,448]{0,1:T(8,128)S(1)}, f32[384,448]{0,1:T(8,128)}, u32[]{:S(2)}) copy-start(f32[384,448]{0,1:T(8,128)} %param.10) | copy-start | bytes 2064388
  7.2 132.9 %copy-start.3 = (s32[25]{0:T(128)S(1)}, s32[25]{0:T(128)}, u32[]{:S(2)}) copy-start(s32[25]{0:T(128)} %param.11) | copy-start | bytes 304
  7.2 245.1 %all-gather.5.cloned.1.call-start = ((), (), s32[]{:S(2)}) async-start(), calls=%async_computation.9 | async-start | bytes 7454720 | tf_op jit(solution)/shard_map/all_gather | solution.py:67
  8.9 31.5 %all-to-all-start.5 = ((bf16[16,64,128]{2,0,1:T(8,128)(2,1)}), bf16[16,64,128]{2,0,1:T(8,128)(2,1)S(1)}, u32[]{:S(2)}, u32[]{:S(2)}) async-start(bf16[16,64,128]{2,0,1:T(8,128)(2,1)} %copy_bitcast_fusion), calls=%async_computation.5 | async-start | bytes 524288 | tf_op jit(solution)/shard_map/all_to_all | solution.py:63
  40.4 70.5 %copy-start.1 = (bf16[16,64,128]{2,0,1:T(8,128)(2,1)}, bf16[16,64,128]{2,0,1:T(8,128)(2,1)S(1)}, u32[]{:S(2)}) copy-start(bf16[16,64,128]{2,0,1:T(8,128)(2,1)S(1)} %all-to-all-done.5) | copy-start | bytes 786436
  40.4 29.2 %all-to-all-start = ((f32[64,7,384]{2,1,0:T(8,128)}), f32[64,7,384]{2,1,0:T(8,128)S(1)}, u32[]{:S(2)}, u32[]{:S(2)}) async-start(f32[64,7,384]{2,1,0:T(8,128)} %all_to_all.90), calls=%async_computation | async-start | bytes 1572864 | tf_op jit(solution)/shard_map/all_to_all | solution.py:50
  69.6 34.4 %all-to-all-start.1 = ((f32[64,7,384]{2,1,0:T(8,128)}), f32[64,7,384]{2,1,0:T(8,128)S(1)}, u32[]{:S(2)}, u32[]{:S(2)}) async-start(f32[64,7,384]{2,1,0:T(8,128)} %all_to_all.94), calls=%async_computation.1 | async-start | bytes 1572864 | tf_op jit(solution)/shard_map/all_to_all | solution.py:51
  104.0 36.0 %all-to-all-start.2 = ((f32[64,7,384]{2,1,0:T(8,128)}), f32[64,7,384]{2,1,0:T(8,128)S(1)}, u32[]{:S(2)}, u32[]{:S(2)}) async-start(f32[64,7,384]{2,1,0:T(8,128)} %all_to_all.98), calls=%async_computation.2 | async-start | bytes 1572864 | tf_op jit(solution)/shard_map/all_to_all | solution.py:52
  110.8 185.2 %all-gather.3.cloned.1.call-start = ((), (), s32[]{:S(2)}) async-start(), calls=%async_computation.8 | async-start | bytes 2359296 | tf_op jit(solution)/shard_map/all_gather | solution.py:64
  111.5 192.7 %reduce-scatter.2.cloned.1.call-start = ((), (), s32[]{:S(2)}) async-start(), calls=%async_computation.10 | async-start | bytes 4718592 | tf_op jit(solution)/shard_map/reduce_scatter | solution.py:74
  259.5 18.2 %all-to-all-start.4 = ((f32[7,64,128]{2,0,1:T(8,128)}), f32[7,64,128]{2,0,1:T(8,128)S(1)}, u32[]{:S(2)}, u32[]{:S(2)}) async-start(f32[7,64,128]{2,0,1:T(8,128)} %slice_bitcast_fusion.1), calls=%async_computation.4 | async-start | bytes 524288 | tf_op jit(solution)/shard_map/all_to_all | solution.py:55
  277.7 18.2 %all-to-all-start.6 = ((f32[7,64,128]{2,0,1:T(8,128)}), f32[7,64,128]{2,0,1:T(8,128)S(1)}, u32[]{:S(2)}, u32[]{:S(2)}) async-start(f32[7,64,128]{2,0,1:T(8,128)} %slice_bitcast_fusion), calls=%async_computation.6 | async-start | bytes 524288 | tf_op jit(solution)/shard_map/all_to_all | solution.py:55
Sparse Core Ops, SparseCore 0:
  11.0 149.2 all-gather.4
  162.4 25.8 all-gather.2
  258.9 31.9 reduce-scatter.1
where the time goes:
time: 314 us; the launch traced here: 313 us
  waiting for transfers between devices  118 us (38%)
  local copies, waits for them, and re-layouts  54.2 us (17%)
  loops' own time  48.2 us (15%)
  starting transfers between devices  44.2 us (14%)
  blocking collectives  20.5 us (7%)
  between operations  13.9 us (4%)
  matrix products  12.5 us (4%)
    another operation x1, loops' own time, place_rows(): placed = lax.fori_loop(0, shard_count, place_one, initial)  48.2 us
    dynamic_update_slice x72, local copies, waits for them, and re-layouts, place_one(): result.append(lax.dynamic_update_slice_in_dim(target, block, begin, 1))  28.7 us
    all_to_all x1, waiting for transfers between devices, shards(): lax.all_to_all(old_second.T, 'dp', split_axis=0, concat_axis=1, tiled=True)  28.5 us
    all_to_all x1, waiting for transfers between devices, shards(): lax.all_to_all(old_first.T, 'dp', split_axis=0, concat_axis=1, tiled=True)  26.7 us
    all_to_all x2, waiting for transfers between devices, shards(): lax.all_to_all(placed, 'dp', split_axis=1, concat_axis=0, tiled=True)  26.2 us
    all_to_all x1, waiting for transfers between devices, shards(): lax.all_to_all(old_weight.T, 'dp', split_axis=0, concat_axis=1, tiled=True)  22.4 us
    all_to_all x1, blocking collectives, shards(): lax.all_to_all(placed, 'dp', split_axis=1, concat_axis=0, tiled=True)  20.5 us
    all_to_all x1, starting transfers between devices, shards(): lax.all_to_all(activations, 'dp', split_axis=1, concat_axis=0, tiled=True)  16.6 us
  transfers between devices with their start and end apart: 9, of which 6 were waited for; matrix products, arithmetic and copies ran while one was open for 19% of the time, Pallas kernels for 0%

commit v1 on v0

v1 whole, which is shorter than its diff:
```python
import jax
import jax.numpy as jnp
from jax import lax
from jax.experimental import pallas as pl
from jax.experimental.pallas import tpu as pltpu
from jax.sharding import PartitionSpec as P

D = 8192
STEP = 24
SHARDS = 24
CAP = 384
ROWS = 128
COLS = 448
GROUPS = 64
SPLITS = 8
TOKENS = 16
STRIPS = COLS // 8
LANES = 128

beta_one = 0.9
beta_two = 0.95
epsilon = 1e-08
learn_rate = 0.05
decay_rate = 0.2

f32 = jnp.float32
bf16 = jnp.bfloat16
PARAMS = pltpu.CompilerParams(vmem_limit_bytes=48 * 1024 * 1024)


def pack_kernel(weight_ref, first_ref, second_ref, act_ref, out_ref):
    turned = [r[...].T for r in (weight_ref, first_ref, second_ref)]
    for s in range(GROUPS):
        act = act_ref[:, s * LANES : (s + 1) * LANES].astype(f32)
        if s < STRIPS:
            tiles = [
                t[s * 8 : s * 8 + 8, q * LANES : (q + 1) * LANES]
                for q in range(CAP // LANES)
                for t in turned
            ]
        else:
            tiles = [jnp.zeros((72, LANES), f32)]
        out_ref[s] = jnp.concatenate([act] + tiles, axis=0).astype(bf16)


def pack(weight, first, second, act):
    return pl.pallas_call(
        pack_kernel,
        out_shape=jax.ShapeDtypeStruct((GROUPS, 88, LANES), bf16),
        compiler_params=PARAMS,
        name="pack",
    )(weight, first, second, act)


def place_kernel(offsets_ref, slots_ref, out_ref, rows_ref):
    lane = lax.broadcasted_iota(jnp.int32, (3, 24, LANES), 2)
    for k in range(SHARDS):
        begin = offsets_ref[k]
        block = begin // LANES
        shift = begin % LANES
        slots = slots_ref[k].astype(f32)[16:]
        turned = pltpu.roll(slots, shift, 1).reshape(3, 24, LANES)
        here = pl.ds(block, 3)
        rows_ref[here] = jnp.where(lane >= shift, turned, rows_ref[here])
        after = pl.ds(block + 1, 3)
        rows_ref[after] = jnp.where(lane < shift, turned, rows_ref[after])
    out_ref[...] = rows_ref[:GROUPS].astype(bf16)


def place(offsets, slots):
    return pl.pallas_call(
        place_kernel,
        grid=(1,),
        in_specs=[
            pl.BlockSpec(memory_space=pltpu.SMEM),
            pl.BlockSpec((SHARDS, 88, LANES), lambda i: (0, 0, 0)),
        ],
        out_specs=pl.BlockSpec((GROUPS, 24, LANES), lambda i: (0, 0, 0)),
        out_shape=jax.ShapeDtypeStruct((GROUPS, 24, LANES), bf16),
        scratch_shapes=[pltpu.VMEM((GROUPS + 4, 24, LANES), f32)],
        compiler_params=PARAMS,
        name="place",
    )(offsets, slots)


def sums_kernel(state_ref, up_ref, out_ref, weight_ref):
    @pl.when(pl.program_id(0) == 0)
    def _():
        state = state_ref[:STRIPS].astype(f32)
        weight_ref[...] = state[:, :8].reshape(COLS, ROWS).T.astype(bf16)

    up = jnp.concatenate([up_ref[j] for j in range(8)], axis=1)
    sums = jnp.dot(weight_ref[...], up, preferred_element_type=f32).astype(bf16)
    for j in range(8):
        out_ref[j] = sums[:, j * LANES : (j + 1) * LANES]


def act_sums(state, up):
    return pl.pallas_call(
        sums_kernel,
        grid=(GROUPS // 8,),
        in_specs=[
            pl.BlockSpec((GROUPS, 24, LANES), lambda i: (0, 0, 0)),
            pl.BlockSpec((8, COLS, LANES), lambda i: (i, 0, 0)),
        ],
        out_specs=pl.BlockSpec((8, ROWS, LANES), lambda i: (i, 0, 0)),
        out_shape=jax.ShapeDtypeStruct((GROUPS, ROWS, LANES), bf16),
        scratch_shapes=[pltpu.VMEM((ROWS, COLS), bf16)],
        compiler_params=PARAMS,
        name="act_sums",
    )(state, up)


def total_kernel(parts_ref, out_ref):
    total = parts_ref[0, 0].astype(f32)
    for m in range(1, SPLITS):
        total = total + parts_ref[m, 0].astype(f32)
    out_ref[...] = total.T.astype(bf16)


def act_total(parts):
    return pl.pallas_call(
        total_kernel,
        grid=(8,),
        in_specs=[pl.BlockSpec((SPLITS, 1, ROWS, LANES), lambda i: (0, i, 0, 0))],
        out_specs=pl.BlockSpec((LANES, ROWS), lambda i: (i, 0)),
        out_shape=jax.ShapeDtypeStruct((8 * LANES, ROWS), bf16),
        compiler_params=PARAMS,
        name="act_total",
    )(parts)


def adamw_update(weight, moment_one, moment_two, gradient):
    first_new = beta_one * moment_one + (1.0 - beta_one) * gradient
    second_new = beta_two * moment_two + (1.0 - beta_two) * gradient * gradient
    first_hat = first_new / (1.0 - beta_one**STEP)
    second_hat = second_new / (1.0 - beta_two**STEP)
    weight_new = weight - learn_rate * (
        first_hat / (jnp.sqrt(second_hat) + epsilon) + decay_rate * weight
    )
    return (weight_new, first_new, second_new)


def update_kernel(state_ref, up_ref, act_ref, weight_ref, first_ref, second_ref, grad_ref):
    step = pl.program_id(0)
    up = jnp.concatenate([up_ref[j] for j in range(8)], axis=1)
    act = jnp.concatenate([act_ref[m, j] for j in range(8) for m in range(SPLITS)], axis=0)
    part = jnp.dot(up, act, preferred_element_type=f32)

    @pl.when(step == 0)
    def _():
        grad_ref[...] = part

    @pl.when(step > 0)
    def _():
        grad_ref[...] += part

    @pl.when(step == GROUPS // 8 - 1)
    def _():
        state = state_ref[:STRIPS].astype(f32)
        old = [state[:, a * 8 : a * 8 + 8].reshape(COLS, ROWS) for a in range(3)]
        new = adamw_update(old[0], old[1], old[2], grad_ref[...])
        for ref, value in zip((weight_ref, first_ref, second_ref), new):
            ref[...] = value.T


def update(state, up, act):
    out = jax.ShapeDtypeStruct((ROWS, COLS), f32)
    spec = pl.BlockSpec((ROWS, COLS), lambda i: (0, 0))
    return pl.pallas_call(
        update_kernel,
        grid=(GROUPS // 8,),
        in_specs=[
            pl.BlockSpec((GROUPS, 24, LANES), lambda i: (0, 0, 0)),
            pl.BlockSpec((8, COLS, LANES), lambda i: (i, 0, 0)),
            pl.BlockSpec((SPLITS, 8, TOKENS, LANES), lambda i: (0, i, 0, 0)),
        ],
        out_specs=[spec, spec, spec],
        out_shape=[out, out, out],
        scratch_shapes=[pltpu.VMEM((COLS, ROWS), f32)],
        compiler_params=PARAMS,
        name="update",
    )(state, up, act)


def exchange(x, axis):
    return lax.all_to_all(x, axis, split_axis=0, concat_axis=0, tiled=True)


def shards(old_weight, old_first, old_second, old_offsets, activations, upstream):
    up = lax.all_gather(upstream.T, "dp", axis=0)
    got = exchange(pack(old_weight, old_first, old_second, activations), "dp")
    act = lax.all_gather(got[:, :TOKENS], "mp", axis=0)
    state = exchange(place(old_offsets, got), "dp")
    sums = act_sums(state, up).reshape(SPLITS, 8, ROWS, LANES)
    act_grad = act_total(exchange(sums, "mp"))
    weight, first, second = update(state, up, act)
    return (weight, first, second, act_grad)


def solution(mesh):
    return jax.shard_map(
        shards,
        mesh=mesh,
        in_specs=(
            P("dp", "mp"),
            P("dp", "mp"),
            P("dp", "mp"),
            P(),
            P(("dp", "mp"), None),
            P("dp", "mp"),
        ),
        out_specs=(P("dp", "mp"), P("dp", "mp"), P("dp", "mp"), P("mp", "dp")),
        check_vma=False,
    )
```

time: 314 us -> 202 us (0.64)
  the two profiles are of different devices: /device:TPU:2 before, /device:TPU:1 now
where the time goes in v1:
time: 202 us
  waiting for transfers between devices  78.3 us (39%)
  blocking collectives  76 us (38%)
  Pallas kernels  19.9 us (10%)
  between operations  14.1 us (7%)
  local copies, waits for them, and re-layouts  7.81 us (4%)
  starting transfers between devices  5.39 us (3%)
    all_to_all x2, blocking collectives, exchange(): return lax.all_to_all(x, axis, split_axis=0, concat_axis=0, tiled=True)  76 us
    all_gather x1, waiting for transfers between devices, shards(): up = lax.all_gather(upstream.T, 'dp', axis=0)  50.6 us
    all_gather x1, waiting for transfers between devices, shards(): act = lax.all_gather(got[:, :TOKENS], 'mp', axis=0)  27 us
    pallas_call x1, Pallas kernels, act_sums(): pl.pallas_call(sums_kernel, grid=(GROUPS // 8,), in_specs=[pl.BlockSpec((...  7.96 us
    pallas_call x1, Pallas kernels, update(): pl.pallas_call(update_kernel, grid=(GROUPS // 8,), in_specs=[pl.BlockSpec...  7.55 us
    unnamed x14, local copies, waits for them, and re-layouts  7.09 us
    all_to_all x1, starting transfers between devices, exchange(): return lax.all_to_all(x, axis, split_axis=0, concat_axis=0, tiled=True)  5.32 us
  transfers between devices with their start and end apart: 3, of which 2 were waited for; matrix products, arithmetic and copies ran while one was open for 3% of the time, Pallas kernels for 8%

profile of v1, /device:TPU:1, one launch (start us, length us, event | category | flops | bytes accessed | tf_op | source)
XLA Modules:
  0.0 201.5 jit_solution(17535579887908337790)
XLA Ops:
  7.2 0.0 all-gather.5.cloned.1.call-start
  7.2 0.7 all-gather.5.cloned.1.call-update
  7.9 0.0 all-gather.7.cloned.1.call-start
  8.0 1.4 copy.16.weight_ref
  9.4 1.4 copy.17.first_ref
  10.8 0.3 copy.18.second_ref
  11.0 0.4 pack.1
  11.4 0.0 copy-start.2
  11.4 53.5 %all_to_all.15.slots_ref = bf16[64,88,128]{2,1,0:T(8,128)(2,1)S(1)} all-to-all(bf16[64,88,128]{2,1,0:T(8,128)(2,1)S(1)} %pack.1), channel_id=1, replica_groups=mesh['dp'=64,'mp'=8] {'dp'}, dimensions={0} | all-to-all | bytes 2883584 | tf_op jit(solution)/shard_map/all_to_all | solution.py:187
  65.0 0.7 slice.4
  65.7 0.0 all-gather.7.cloned.1.call-update
  65.7 0.8 place.1
  66.6 22.5 %all_to_all.16.state_ref = bf16[64,24,128]{2,1,0:T(8,128)(2,1)S(1)} all-to-all(bf16[64,24,128]{2,1,0:T(8,128)(2,1)S(1)} %place.1), channel_id=1, replica_groups=mesh['dp'=64,'mp'=8] {'dp'}, dimensions={0} | all-to-all | bytes 786432 | tf_op jit(solution)/shard_map/all_to_all | solution.py:187
  89.1 50.6 %all-gather.5.cloned.1.call-done = bf16[28672,128]{1,0:T(8,128)(2,1)} async-done(((bf16[448,128]{1,0:T(8,128)(2,1)}), bf16[28672,128]{1,0:T(8,128)(2,1)}) %all-gather.5.cloned.1.call-update) | async-done | bytes 7340048 | tf_op jit(solution)/shard_map/all_gather | solution.py:191
  139.7 8.0 %act_sums.1 = bf16[64,128,128]{2,1,0:T(8,128)(2,1)} custom-call(bf16[64,24,128]{2,1,0:T(8,128)(2,1)S(1)} %all_to_all.16.state_ref, bf16[64,448,128]{2,1,0:T(8,128)(2,1)} %bitcast.5), custom_call_target="tpu_custom_call" | custom-call | tf_op jit(solution)/shard_map/act_sums/pallas_call | solution.py:99
  147.7 5.3 %all-to-all-start.2 = ((bf16[8,8,128,128]{3,2,1,0:T(8,128)(2,1)}), bf16[8,8,128,128]{3,2,1,0:T(8,128)(2,1)S(1)}, u32[]{:S(2)}, u32[]{:S(2)}) async-start(bf16[8,8,128,128]{3,2,1,0:T(8,128)(2,1)} %bitcast.3), calls=%async_computation.2 | async-start | bytes 4194304 | tf_op jit(solution)/shard_map/all_to_all | solution.py:187
  153.0 27.0 %all-gather.7.cloned.1.call-done = bf16[512,16,128]{2,1,0:T(8,128)(2,1)} async-done(((bf16[64,16,128]{2,1,0:T(8,128)(2,1)}), bf16[512,16,128]{2,1,0:T(8,128)(2,1)}) %all-gather.7.cloned.1.call-update) | async-done | bytes 2097168 | tf_op jit(solution)/shard_map/all_gather | solution.py:193
  180.0 1.6 copy-done
  181.6 7.5 %update.1 = (f32[128,448]{1,0:T(8,128)S(1)}, f32[128,448]{1,0:T(8,128)S(1)}, f32[128,448]{1,0:T(8,128)S(1)}) custom-call(bf16[64,24,128]{2,1,0:T(8,128)(2,1)S(1)} %all_to_all.16.state_ref, bf16[64,448,128]{2,1,0:T(8,128)(2,1)} %bitcast.6, bf16[8,64,16,128]{3,2,1,0:T(8,128)(2,1)S(1)} %bitcast.4), custom_call_target="tpu_custom_call" | custom-call | tf_op jit(solution)/shard_map/update/pallas_call | solution.py:170
  189.1 0.8 copy.19
  189.9 0.8 copy.20
  190.8 0.8 copy.21
  191.6 0.0 all-to-all-done.2.parts_ref
  191.6 3.1 %act_total.1 = bf16[1024,128]{1,0:T(8,128)(2,1)} custom-call(bf16[8,8,128,128]{3,2,1,0:T(8,128)(2,1)S(1)} %all-to-all-done.2.parts_ref), custom_call_target="tpu_custom_call" | custom-call | tf_op jit(solution)/shard_map/act_total/pallas_call | solution.py:122
  (6 shorter events, 0.0 us)
Async XLA Ops:
  7.2 3.6 %copy-start.3 = (f32[384,448]{0,1:T(8,128)S(1)}, f32[384,448]{0,1:T(8,128)}, u32[]{:S(2)}) copy-start(f32[384,448]{0,1:T(8,128)} %param.8) | copy-start | bytes 2064388
  7.2 132.5 %all-gather.5.cloned.1.call-start = ((), (), s32[]{:S(2)}) async-start(), calls=%async_computation.3 | async-start | bytes 7454720 | tf_op jit(solution)/shard_map/all_gather | solution.py:191
  7.9 3.1 %copy-start.1 = (bf16[16,8192]{1,0:T(8,128)(2,1)S(1)}, bf16[16,8192]{1,0:T(8,128)(2,1)}, u32[]{:S(2)}) copy-start(bf16[16,8192]{1,0:T(8,128)(2,1)} %act_ref.1) | copy-start | bytes 786436
  7.9 172.1 %all-gather.7.cloned.1.call-start = ((), (), s32[]{:S(2)}) async-start(), calls=%async_computation.4 | async-start | bytes 2359296 | tf_op jit(solution)/shard_map/all_gather | solution.py:193
  11.4 54.3 %copy-start.2 = (s32[25]{0:T(128)S(1)}, s32[25]{0:T(128)}, u32[]{:S(2)}) copy-start(s32[25]{0:T(128)} %offsets_ref.1) | copy-start | bytes 304
  147.7 43.9 %all-to-all-start.2 = ((bf16[8,8,128,128]{3,2,1,0:T(8,128)(2,1)}), bf16[8,8,128,128]{3,2,1,0:T(8,128)(2,1)S(1)}, u32[]{:S(2)}, u32[]{:S(2)}) async-start(bf16[8,8,128,128]{3,2,1,0:T(8,128)(2,1)} %bitcast.3), calls=%async_computation.2 | async-start | bytes 4194304 | tf_op jit(solution)/shard_map/all_to_all | solution.py:187
  180.0 1.6 copy-start
Sparse Core Ops, SparseCore 0:
  11.0 128.6 all-gather.4
  142.4 37.5 all-gather.6

commit v2 on v1

--- a/solution.py
+++ b/solution.py
@@ -29,7 +29,7 @@
 
 
 def pack_kernel(weight_ref, first_ref, second_ref, act_ref, out_ref):
-    turned = [r[...].T for r in (weight_ref, first_ref, second_ref)]
+    turned = [r[...] for r in (weight_ref, first_ref, second_ref)]
     for s in range(GROUPS):
         act = act_ref[:, s * LANES : (s + 1) * LANES].astype(f32)
         if s < STRIPS:
@@ -161,12 +161,12 @@
         old = [state[:, a * 8 : a * 8 + 8].reshape(COLS, ROWS) for a in range(3)]
         new = adamw_update(old[0], old[1], old[2], grad_ref[...])
         for ref, value in zip((weight_ref, first_ref, second_ref), new):
-            ref[...] = value.T
+            ref[...] = value
 
 
 def update(state, up, act):
-    out = jax.ShapeDtypeStruct((ROWS, COLS), f32)
-    spec = pl.BlockSpec((ROWS, COLS), lambda i: (0, 0))
+    out = jax.ShapeDtypeStruct((COLS, ROWS), f32)
+    spec = pl.BlockSpec((COLS, ROWS), lambda i: (0, 0))
     return pl.pallas_call(
         update_kernel,
         grid=(GROUPS // 8,),
@@ -189,13 +189,14 @@
 
 def shards(old_weight, old_first, old_second, old_offsets, activations, upstream):
     up = lax.all_gather(upstream.T, "dp", axis=0)
-    got = exchange(pack(old_weight, old_first, old_second, activations), "dp")
-    act = lax.all_gather(got[:, :TOKENS], "mp", axis=0)
+    got = exchange(pack(old_weight.T, old_first.T, old_second.T, activations), "dp")
+    copies = jnp.broadcast_to(got[None, :, :TOKENS], (SPLITS, GROUPS, TOKENS, LANES))
+    act = exchange(copies, "mp")
     state = exchange(place(old_offsets, got), "dp")
     sums = act_sums(state, up).reshape(SPLITS, 8, ROWS, LANES)
     act_grad = act_total(exchange(sums, "mp"))
     weight, first, second = update(state, up, act)
-    return (weight, first, second, act_grad)
+    return (weight.T, first.T, second.T, act_grad)
 
 
 def solution(mesh):

time: 202 us -> 193 us (0.955)
  blocking collectives: 76 us -> 54 us
  starting transfers between devices: 5.39 us -> 23 us
  waiting for transfers between devices: 78.3 us -> 71.3 us
  Pallas kernels: 19.9 us -> 22.1 us
    all_to_all x1 -> x3, waiting for transfers between devices: 0.01 us -> 32 us  [exchange(): return lax.all_to_all(x, axis, split_axis=0, concat_axis=0, tiled=True)]
    all_gather x1 -> x0, waiting for transfers between devices: 27 us -> none  [shards(): act = lax.all_gather(got[:, :TOKENS], 'mp', axis=0)]
    all_to_all x2 -> x1, blocking collectives: 76 us -> 54 us  [exchange(): return lax.all_to_all(x, axis, split_axis=0, concat_axis=0, tiled=True)]
    all_to_all x1 -> x3, starting transfers between devices: 5.32 us -> 22.9 us  [exchange(): return lax.all_to_all(x, axis, split_axis=0, concat_axis=0, tiled=True)]
    all_gather x1, waiting for transfers between devices: 50.6 us -> 38.6 us  [shards(): up = lax.all_gather(upstream.T, 'dp', axis=0)]
    pallas_call x1, Pallas kernels: 3.12 us -> 5.56 us  [act_total(): pl.pallas_call(total_kernel, grid=(8,), in_specs=[pl.BlockSpec((SPLITS, 1...]
    unnamed x14 -> x12, local copies, waits for them, and re-layouts: 7.09 us -> 5.64 us
  transfers between devices with their start and end apart: 3 -> 4, of which waited for: 2 -> 3; matrix products, arithmetic and copies ran while one was open for 3% -> 1% of each run, Pallas kernels for 8% -> 9%
where the time goes in v2:
time: 193 us; the launch traced here: 192 us
  waiting for transfers between devices  71.3 us (37%)
  blocking collectives  54 us (28%)
  starting transfers between devices  23 us (12%)
  Pallas kernels  22.1 us (11%)
  between operations  14.1 us (7%)
  local copies, waits for them, and re-layouts  7.24 us (4%)
    all_to_all x1, blocking collectives, exchange(): return lax.all_to_all(x, axis, split_axis=0, concat_axis=0, tiled=True)  54 us
    all_gather x1, waiting for transfers between devices, shards(): up = lax.all_gather(upstream.T, 'dp', axis=0)  38.6 us
    all_to_all x3, waiting for transfers between devices, exchange(): return lax.all_to_all(x, axis, split_axis=0, concat_axis=0, tiled=True)  32 us
    all_to_all x3, starting transfers between devices, exchange(): return lax.all_to_all(x, axis, split_axis=0, concat_axis=0, tiled=True)  22.9 us
    pallas_call x1, Pallas kernels, update(): pl.pallas_call(update_kernel, grid=(GROUPS // 8,), in_specs=[pl.BlockSpec...  8.17 us
    pallas_call x1, Pallas kernels, act_sums(): pl.pallas_call(sums_kernel, grid=(GROUPS // 8,), in_specs=[pl.BlockSpec((...  6.64 us
    unnamed x12, local copies, waits for them, and re-layouts  5.64 us
    pallas_call x1, Pallas kernels, act_total(): pl.pallas_call(total_kernel, grid=(8,), in_specs=[pl.BlockSpec((SPLITS, 1...  5.56 us
  transfers between devices with their start and end apart: 4, of which 3 were waited for; matrix products, arithmetic and copies ran while one was open for 1% of the time, Pallas kernels for 9%

profile of v2, /device:TPU:1, one launch (start us, length us, event | category | flops | bytes accessed | tf_op | source)
XLA Modules:
  0.0 191.7 jit_solution(17438914967368076925)
XLA Ops:
  7.2 0.0 all-gather.3.cloned.1.call-start
  7.2 0.7 all-gather.3.cloned.1.call-update
  7.9 0.0 copy-start.1
  7.9 1.1 copy-done.1
  9.0 1.1 copy-done.2
  10.1 1.1 copy-done.3
  11.2 0.9 copy-done.4
  12.1 0.2 pack.1
  12.3 0.0 copy-start.5
  12.3 54.0 %all_to_all.20.slots_ref = bf16[64,88,128]{2,1,0:T(8,128)(2,1)S(1)} all-to-all(bf16[64,88,128]{2,1,0:T(8,128)(2,1)S(1)} %pack.1), channel_id=1, replica_groups=mesh['dp'=64,'mp'=8] {'dp'}, dimensions={0} | all-to-all | bytes 2883584 | tf_op jit(solution)/shard_map/all_to_all | solution.py:187
  66.3 1.6 place.1
  67.9 8.7 %all-to-all-start.1 = ((bf16[64,24,128]{2,1,0:T(8,128)(2,1)}), bf16[64,24,128]{2,1,0:T(8,128)(2,1)S(1)}, u32[]{:S(2)}, u32[]{:S(2)}) async-start(bf16[64,24,128]{2,1,0:T(8,128)(2,1)} %place.1), calls=%async_computation.1 | async-start | bytes 786432 | tf_op jit(solution)/shard_map/all_to_all | solution.py:187
  76.6 13.7 %all-to-all-done.1.state_ref = bf16[64,24,128]{2,1,0:T(8,128)(2,1)S(1)} async-done(((bf16[64,24,128]{2,1,0:T(8,128)(2,1)}), bf16[64,24,128]{2,1,0:T(8,128)(2,1)S(1)}, u32[]{:S(2)}, u32[]{:S(2)}) %all-to-all-start.1) | async-done | bytes 393248 | tf_op jit(solution)/shard_map/all_to_all | solution.py:187
  90.4 1.6 broadcast_in_dim.2
  91.9 8.9 %all-to-all-start.2 = ((bf16[8,64,16,128]{3,2,1,0:T(8,128)(2,1)}), bf16[8,64,16,128]{3,2,1,0:T(8,128)(2,1)S(1)}, u32[]{:S(2)}, u32[]{:S(2)}) async-start(bf16[8,64,16,128]{3,2,1,0:T(8,128)(2,1)} %broadcast_in_dim.2), calls=%async_computation.2 | async-start | bytes 4194304 | tf_op jit(solution)/shard_map/all_to_all | solution.py:187
  100.9 38.6 %all-gather.3.cloned.1.call-done = bf16[28672,128]{1,0:T(8,128)(2,1)} async-done(((bf16[448,128]{1,0:T(8,128)(2,1)}), bf16[28672,128]{1,0:T(8,128)(2,1)}) %all-gather.3.cloned.1.call-update) | async-done | bytes 7340048 | tf_op jit(solution)/shard_map/all_gather | solution.py:191
  139.5 6.6 %act_sums.1 = bf16[64,128,128]{2,1,0:T(8,128)(2,1)S(1)} custom-call(bf16[64,24,128]{2,1,0:T(8,128)(2,1)S(1)} %all-to-all-done.1.state_ref, bf16[64,448,128]{2,1,0:T(8,128)(2,1)} %bitcast.13), custom_call_target="tpu_custom_call" | custom-call | tf_op jit(solution)/shard_map/act_sums/pallas_call | solution.py:99
  146.2 0.0 copy-start
  146.2 1.4 copy-done
  147.6 0.0 all-to-all-done.2.act_ref
  147.6 5.3 %all-to-all-start.3 = ((bf16[8,8,128,128]{3,2,1,0:T(8,128)(2,1)}), bf16[8,8,128,128]{3,2,1,0:T(8,128)(2,1)}, u32[]{:S(2)}, u32[]{:S(2)}) async-start(bf16[8,8,128,128]{3,2,1,0:T(8,128)(2,1)} %bitcast.9), calls=%async_computation.3 | async-start | bytes 4194304 | tf_op jit(solution)/shard_map/all_to_all | solution.py:187
  152.9 8.2 %update.1 = (f32[448,128]{1,0:T(8,128)}, f32[448,128]{1,0:T(8,128)}, f32[448,128]{1,0:T(8,128)}) custom-call(bf16[64,24,128]{2,1,0:T(8,128)(2,1)S(1)} %all-to-all-done.1.state_ref, bf16[64,448,128]{2,1,0:T(8,128)(2,1)} %bitcast.14, bf16[8,64,16,128]{3,2,1,0:T(8,128)(2,1)S(1)} %all-to-all-done.2.act_ref), custom_call_target="tpu_custom_call" | custom-call | tf_op jit(solution)/shard_map/update/pallas_call | solution.py:170
  161.1 18.3 %all-to-all-done.3.parts_ref = bf16[8,8,128,128]{3,2,1,0:T(8,128)(2,1)} async-done(((bf16[8,8,128,128]{3,2,1,0:T(8,128)(2,1)}), bf16[8,8,128,128]{3,2,1,0:T(8,128)(2,1)}, u32[]{:S(2)}, u32[]{:S(2)}) %all-to-all-start.3) | async-done | bytes 2097184 | tf_op jit(solution)/shard_map/all_to_all | solution.py:187
  179.3 5.6 %act_total.1 = bf16[1024,128]{1,0:T(8,128)(2,1)} custom-call(bf16[8,8,128,128]{3,2,1,0:T(8,128)(2,1)} %all-to-all-done.3.parts_ref), custom_call_target="tpu_custom_call" | custom-call | tf_op jit(solution)/shard_map/act_total/pallas_call | solution.py:122
  (5 shorter events, 0.0 us)
Async XLA Ops:
  7.2 132.3 %all-gather.3.cloned.1.call-start = ((), (), s32[]{:S(2)}) async-start(), calls=%async_computation.4 | async-start | bytes 7454720 | tf_op jit(solution)/shard_map/all_gather | solution.py:191
  7.9 1.1 copy-start.1
  9.0 1.1 copy-start.2
  10.1 1.1 copy-start.3
  11.2 0.9 copy-start.4
  12.3 54.0 %copy-start.5 = (s32[25]{0:T(128)S(1)}, s32[25]{0:T(128)}, u32[]{:S(2)}) copy-start(s32[25]{0:T(128)} %offsets_ref.1) | copy-start | bytes 304
  67.9 22.4 %all-to-all-start.1 = ((bf16[64,24,128]{2,1,0:T(8,128)(2,1)}), bf16[64,24,128]{2,1,0:T(8,128)(2,1)S(1)}, u32[]{:S(2)}, u32[]{:S(2)}) async-start(bf16[64,24,128]{2,1,0:T(8,128)(2,1)} %place.1), calls=%async_computation.1 | async-start | bytes 786432 | tf_op jit(solution)/shard_map/all_to_all | solution.py:187
  91.9 55.6 %all-to-all-start.2 = ((bf16[8,64,16,128]{3,2,1,0:T(8,128)(2,1)}), bf16[8,64,16,128]{3,2,1,0:T(8,128)(2,1)S(1)}, u32[]{:S(2)}, u32[]{:S(2)}) async-start(bf16[8,64,16,128]{3,2,1,0:T(8,128)(2,1)} %broadcast_in_dim.2), calls=%async_computation.2 | async-start | bytes 4194304 | tf_op jit(solution)/shard_map/all_to_all | solution.py:187
  146.2 1.4 copy-start
  147.6 31.8 %all-to-all-start.3 = ((bf16[8,8,128,128]{3,2,1,0:T(8,128)(2,1)}), bf16[8,8,128,128]{3,2,1,0:T(8,128)(2,1)}, u32[]{:S(2)}, u32[]{:S(2)}) async-start(bf16[8,8,128,128]{3,2,1,0:T(8,128)(2,1)} %bitcast.9), calls=%async_computation.3 | async-start | bytes 4194304 | tf_op jit(solution)/shard_map/all_to_all | solution.py:187
Sparse Core Ops, SparseCore 0:
  11.0 128.4 all-gather.2

commit v3 on v2

v3 whole, which is shorter than its diff:
```python
import jax
import jax.numpy as jnp
from jax import lax
from jax.experimental import pallas as pl
from jax.experimental.pallas import tpu as pltpu
from jax.sharding import Mesh
from jax.sharding import PartitionSpec as P

D = 8192
STEP = 24
SHARDS = 24
CAP = 384
ROWS = 128
COLS = 448
GROUPS = 64
SPLITS = 8
TOKENS = 16
SIDE = 8
STRIPS = COLS // 8
LANES = 128

beta_one = 0.9
beta_two = 0.95
epsilon = 1e-08
learn_rate = 0.05
decay_rate = 0.2

f32 = jnp.float32
bf16 = jnp.bfloat16
PARAMS = pltpu.CompilerParams(vmem_limit_bytes=48 * 1024 * 1024)


def pack_kernel(weight_ref, first_ref, second_ref, out_ref):
    for s in range(STRIPS):
        tiles = [
            r[s * 8 : s * 8 + 8, q * LANES : (q + 1) * LANES]
            for q in range(CAP // LANES)
            for r in (weight_ref, first_ref, second_ref)
        ]
        out_ref[s] = jnp.concatenate(tiles, axis=0).astype(bf16)
    out_ref[STRIPS:] = jnp.zeros((GROUPS - STRIPS, 72, LANES), bf16)


def pack(weight, first, second):
    return pl.pallas_call(
        pack_kernel,
        out_shape=jax.ShapeDtypeStruct((GROUPS, 72, LANES), bf16),
        compiler_params=PARAMS,
        name="pack",
    )(weight, first, second)


def place_kernel(offsets_ref, slots_ref, out_ref, rows_ref):
    lane = lax.broadcasted_iota(jnp.int32, (3, 24, LANES), 2)
    for k in range(SHARDS):
        begin = offsets_ref[k]
        block = begin // LANES
        shift = begin % LANES
        slots = slots_ref[k].astype(f32)
        turned = pltpu.roll(slots, shift, 1).reshape(3, 24, LANES)
        here = pl.ds(block, 3)
        rows_ref[here] = jnp.where(lane >= shift, turned, rows_ref[here])
        after = pl.ds(block + 1, 3)
        rows_ref[after] = jnp.where(lane < shift, turned, rows_ref[after])
    for z in range(SIDE):
        rows = rows_ref[z * SIDE : (z + 1) * SIDE]
        weights = rows[:, :8].reshape(64, LANES)
        for y in range(SIDE):
            both = jnp.concatenate([weights, rows[y, 8:]], axis=0)
            out_ref[z * SIDE + y] = both.astype(bf16)


def place(offsets, slots):
    return pl.pallas_call(
        place_kernel,
        grid=(1,),
        in_specs=[
            pl.BlockSpec(memory_space=pltpu.SMEM),
            pl.BlockSpec((SHARDS, 72, LANES), lambda i: (0, 0, 0)),
        ],
        out_specs=pl.BlockSpec((GROUPS, 80, LANES), lambda i: (0, 0, 0)),
        out_shape=jax.ShapeDtypeStruct((GROUPS, 80, LANES), bf16),
        scratch_shapes=[pltpu.VMEM((GROUPS + 4, 24, LANES), f32)],
        compiler_params=PARAMS,
        name="place",
    )(offsets, slots)


def own_core(up_ref, core):
    parts = [jnp.where(core == 0, up_ref[z, 0], up_ref[z, 1]) for z in range(SIDE)]
    return jnp.concatenate(parts, axis=1)


def sums_kernel(place_ref, state_ref, up_ref, out_ref):
    up = own_core(up_ref, place_ref[1])
    state = state_ref[:STRIPS].astype(f32)
    for y in range(SIDE):
        weight = state[:, y * 8 : y * 8 + 8].reshape(COLS, ROWS).T.astype(bf16)
        sums = jnp.dot(weight, up, preferred_element_type=f32).astype(bf16)
        for z in range(SIDE):
            out_ref[z, y] = sums[:, z * LANES : (z + 1) * LANES]


def act_sums(place, state, up):
    return pl.pallas_call(
        sums_kernel,
        in_specs=[
            pl.BlockSpec(memory_space=pltpu.SMEM),
            pl.BlockSpec(memory_space=pltpu.VMEM),
            pl.BlockSpec(memory_space=pltpu.VMEM),
        ],
        out_shape=jax.ShapeDtypeStruct((SIDE, SIDE, ROWS, LANES), bf16),
        compiler_params=PARAMS,
        name="act_sums",
    )(place, state, up)


def total_kernel(parts_ref, out_ref):
    total = parts_ref[0, 0].astype(f32)
    for m in range(1, SPLITS):
        total = total + parts_ref[m, 0].astype(f32)
    out_ref[0] = total.T.astype(bf16)


def act_total(parts):
    return pl.pallas_call(
        total_kernel,
        grid=(SIDE,),
        in_specs=[pl.BlockSpec((SPLITS, 1, ROWS, LANES), lambda i: (0, i, 0, 0))],
        out_specs=pl.BlockSpec((1, LANES, ROWS), lambda i: (i, 0, 0)),
        out_shape=jax.ShapeDtypeStruct((SIDE, LANES, ROWS), bf16),
        compiler_params=PARAMS,
        name="act_total",
    )(parts)


def grad_kernel(place_ref, up_ref, act_ref, out_ref):
    up = own_core(up_ref, place_ref[1])
    act = jnp.concatenate(
        [act_ref[m, z, 0] for z in range(SIDE) for m in range(SPLITS)], axis=0
    )
    out_ref[0] = jnp.dot(up, act, preferred_element_type=f32)


def grad_parts(place, up, act):
    return pl.pallas_call(
        grad_kernel,
        grid=(SIDE,),
        in_specs=[
            pl.BlockSpec(memory_space=pltpu.SMEM),
            pl.BlockSpec((SIDE, 2, COLS, LANES), lambda i: (0, 0, 0, 0)),
            pl.BlockSpec((SPLITS, SIDE, 1, TOKENS, LANES), lambda i: (0, 0, i, 0, 0)),
        ],
        out_specs=pl.BlockSpec((1, COLS, ROWS), lambda i: (i, 0, 0)),
        out_shape=jax.ShapeDtypeStruct((SIDE, COLS, ROWS), f32),
        compiler_params=PARAMS,
        name="grad_parts",
    )(place, up, act)


def adamw_update(weight, moment_one, moment_two, gradient):
    first_new = beta_one * moment_one + (1.0 - beta_one) * gradient
    second_new = beta_two * moment_two + (1.0 - beta_two) * gradient * gradient
    first_hat = first_new / (1.0 - beta_one**STEP)
    second_hat = second_new / (1.0 - beta_two**STEP)
    weight_new = weight - learn_rate * (
        first_hat / (jnp.sqrt(second_hat) + epsilon) + decay_rate * weight
    )
    return (weight_new, first_new, second_new)


def update_kernel(place_ref, state_ref, grad_ref, weight_ref, first_ref, second_ref):
    mine = place_ref[0]
    state = state_ref[:STRIPS].astype(f32)
    weight = state[:, :8]
    for y in range(1, SIDE):
        weight = jnp.where(mine == y, state[:, y * 8 : y * 8 + 8], weight)
    old = [t.reshape(COLS, ROWS) for t in (weight, state[:, 64:72], state[:, 72:])]
    new = adamw_update(old[0], old[1], old[2], grad_ref[...])
    for ref, value in zip((weight_ref, first_ref, second_ref), new):
        ref[...] = value


def update(place, state, grad):
    out = jax.ShapeDtypeStruct((COLS, ROWS), f32)
    return pl.pallas_call(
        update_kernel,
        in_specs=[
            pl.BlockSpec(memory_space=pltpu.SMEM),
            pl.BlockSpec(memory_space=pltpu.VMEM),
            pl.BlockSpec(memory_space=pltpu.VMEM),
        ],
        out_shape=[out, out, out],
        compiler_params=PARAMS,
        name="update",
    )(place, state, grad)


def exchange(x, axis):
    return lax.all_to_all(x, axis, split_axis=0, concat_axis=0, tiled=True)


def shards(old_weight, old_first, old_second, old_offsets, activations, upstream):
    here = jnp.stack([lax.axis_index("y"), lax.axis_index("c")])
    up = lax.all_gather(upstream.T, ("z", "c"), axis=0).reshape(SIDE, 2, COLS, LANES)
    blocks = activations.reshape(TOKENS, SIDE, SIDE, LANES).transpose(1, 2, 0, 3)
    mine = exchange(blocks, "z")
    act = lax.all_gather(mine, ("x", "c"), axis=0)
    got = exchange(pack(old_weight.T, old_first.T, old_second.T), ("z", "y"))
    state = exchange(place(old_offsets, got), ("z", "y"))
    sums = act_sums(here, state, up)
    total = act_total(exchange(sums, ("x", "c")))
    act_grad = exchange(total, "y").reshape(SIDE * LANES, ROWS)
    parts = grad_parts(here, up, act)
    grad = lax.psum_scatter(parts, "y", scatter_dimension=0)
    weight, first, second = update(here, state, grad)
    return (weight.T, first.T, second.T, act_grad)


def solution(mesh):
    grid = Mesh(mesh.devices.reshape(SIDE, SIDE, SPLITS // 2, 2), ("z", "y", "x", "c"))
    dp, mp = ("z", "y"), ("x", "c")
    return jax.shard_map(
        shards,
        mesh=grid,
        in_specs=(P(dp, mp), P(dp, mp), P(dp, mp), P(), P(dp + mp, None), P(dp, mp)),
        out_specs=(P(dp, mp), P(dp, mp), P(dp, mp), P(mp, dp)),
        check_vma=False,
    )
```

time: 193 us -> 183 us (0.948)
  blocking collectives: 54 us -> 105 us
  waiting for transfers between devices: 71.3 us -> 31 us
  starting transfers between devices: 23 us -> 11.2 us
  Pallas kernels: 22.1 us -> 12.2 us
    all_to_all x1 -> x4, blocking collectives: 54 us -> 105 us  [exchange(): return lax.all_to_all(x, axis, split_axis=0, concat_axis=0, tiled=True)]
    all_to_all x3 -> x1, waiting for transfers between devices: 32 us -> 0.01 us  [exchange(): return lax.all_to_all(x, axis, split_axis=0, concat_axis=0, tiled=True)]
    all_to_all x3 -> x1, starting transfers between devices: 22.9 us -> 11.1 us  [exchange(): return lax.all_to_all(x, axis, split_axis=0, concat_axis=0, tiled=True)]
    pallas_call x4 -> x5, Pallas kernels: 20.5 us -> 10.2 us  [the longest x1 5.62 us: grad_parts(): pl.pallas_call(grad_kernel, grid=(SIDE,), in_specs=[pl.BlockSpec(memory_s...]
    all_gather x1 -> x2, waiting for transfers between devices: 38.6 us -> 30.2 us  [the longest x1 30.2 us: shards(): act = lax.all_gather(mine, ('x', 'c'), axis=0)]
    unnamed x12 -> x18, local copies, waits for them, and re-layouts: 5.64 us -> 7.21 us
  transfers between devices with their start and end apart: 4 -> 4, of which waited for: 3 -> 1; matrix products, arithmetic and copies ran while one was open for 1% -> 1% of each run, Pallas kernels for 9% -> 6%
where the time goes in v3:
time: 183 us; the launch traced here: 182 us
  blocking collectives  105 us (57%)
  waiting for transfers between devices  31 us (17%)
  between operations  13.9 us (8%)
  Pallas kernels  12.2 us (7%)
  starting transfers between devices  11.2 us (6%)
  local copies, waits for them, and re-layouts  8 us (4%)
    all_to_all x4, blocking collectives, exchange(): return lax.all_to_all(x, axis, split_axis=0, concat_axis=0, tiled=True)  105 us
    all_gather x1, waiting for transfers between devices, shards(): act = lax.all_gather(mine, ('x', 'c'), axis=0)  30.2 us
    all_to_all x1, starting transfers between devices, exchange(): return lax.all_to_all(x, axis, split_axis=0, concat_axis=0, tiled=True)  11.1 us
    unnamed x18, local copies, waits for them, and re-layouts  7.21 us
    pallas_call x1, Pallas kernels, grad_parts(): pl.pallas_call(grad_kernel, grid=(SIDE,), in_specs=[pl.BlockSpec(memory_s...  5.62 us
  transfers between devices with their start and end apart: 4, of which 1 were waited for; matrix products, arithmetic and copies ran while one was open for 1% of the time, Pallas kernels for 6%

profile of v3, /device:TPU:1, one launch (start us, length us, event | category | flops | bytes accessed | tf_op | source)
XLA Modules:
  0.0 181.6 jit_solution(14161533008118865868)
XLA Ops:
  7.2 0.0 all-gather.5.cloned.1.call-start
  7.2 0.7 all-gather.5.cloned.1.call-update
  7.9 0.0 all-gather.7.cloned.1.call-start
  8.0 1.0 copy.14
  9.0 21.0 %all_to_all.25 = bf16[8,8,16,128]{3,1,2,0:T(8,128)(2,1)S(1)} all-to-all(bf16[8,8,16,128]{3,1,2,0:T(8,128)(2,1)S(1)} %copy.12), channel_id=1, replica_groups=mesh['z'=8,'y'=8,'x'=4,'c'=2] {'z'}, dimensions={0} | all-to-all | bytes 524288 | tf_op jit(solution)/shard_map/all_to_all | solution.py:200
  30.1 0.7 copy.13
  30.9 0.1 pack.1
  31.0 38.1 %all_to_all.26.slots_ref = bf16[64,72,128]{2,1,0:T(8,128)(2,1)S(1)} all-to-all(bf16[64,72,128]{2,1,0:T(8,128)(2,1)S(1)} %pack.1), channel_id=1, replica_groups=mesh['z'=8,'y'=8,'x'=4,'c'=2] {'z','y'}, dimensions={0} | all-to-all | bytes 2359296 | tf_op jit(solution)/shard_map/all_to_all | solution.py:200
  69.1 2.0 %place.1 = bf16[64,80,128]{2,1,0:T(8,128)(2,1)} custom-call(s32[25]{0:T(128)S(1)} %copy-done.7, bf16[64,72,128]{2,1,0:T(8,128)(2,1)S(1)} %all_to_all.26.slots_ref), custom_call_target="tpu_custom_call" | custom-call | tf_op jit(solution)/shard_map/place/pallas_call | solution.py:74
  71.1 11.1 %all-to-all-start.1 = ((bf16[64,80,128]{2,1,0:T(8,128)(2,1)}), bf16[64,80,128]{2,1,0:T(8,128)(2,1)S(1)}, u32[]{:S(2)}, u32[]{:S(2)}) async-start(bf16[64,80,128]{2,1,0:T(8,128)(2,1)} %place.1), calls=%async_computation.1 | async-start | bytes 2621440 | tf_op jit(solution)/shard_map/all_to_all | solution.py:200
  82.2 0.0 reduce-scatter.2.cloned.1.call-start
  82.2 0.1 pad_add_fusion.place_ref
  82.3 30.2 %all-gather.7.cloned.1.call-done = bf16[64,8,16,128]{3,2,1,0:T(8,128)(2,1)} async-done(((bf16[8,8,16,128]{3,2,1,0:T(8,128)(2,1)}), bf16[64,8,16,128]{3,2,1,0:T(8,128)(2,1)}) %all-gather.7.cloned.1.call-update) | async-done | bytes 2097168 | tf_op jit(solution)/shard_map/all_gather | solution.py:208
  112.5 1.5 copy-done
  114.0 1.6 copy-done.2
  115.6 5.6 %grad_parts.1 = f32[8,448,128]{2,1,0:T(8,128)} custom-call(s32[2]{0:T(128)S(1)} %pad_add_fusion.place_ref, bf16[8,2,448,128]{3,2,1,0:T(8,128)(2,1)S(1)} %bitcast.18, bf16[8,8,8,16,128]{4,3,2,1,0:T(8,128)(2,1)S(1)} %bitcast.20), custom_call_target="tpu_custom_call" | custom-call | tf_op jit(solution)/shard_map/grad_parts/pallas_call | solution.py:146
  121.3 1.5 copy-done.1
  122.7 1.9 %act_sums.1 = bf16[8,8,128,128]{3,2,1,0:T(8,128)(2,1)S(1)} custom-call(s32[2]{0:T(128)S(1)} %pad_add_fusion.place_ref, bf16[64,80,128]{2,1,0:T(8,128)(2,1)S(1)} %all-to-all-done.1.state_ref, bf16[8,2,448,128]{3,2,1,0:T(8,128)(2,1)S(1)} %bitcast.19), custom_call_target="tpu_custom_call" | custom-call | tf_op jit(solution)/shard_map/act_sums/pallas_call | solution.py:105
  124.6 29.8 %all_to_all.27.parts_ref = bf16[8,8,128,128]{3,2,1,0:T(8,128)(2,1)S(1)} all-to-all(bf16[8,8,128,128]{3,2,1,0:T(8,128)(2,1)S(1)} %act_sums.1), channel_id=1, replica_groups=mesh['z'=8,'y'=8,'x'=4,'c'=2] {'x','c'}, dimensions={0} | all-to-all | bytes 4194304 | tf_op jit(solution)/shard_map/all_to_all | solution.py:200
  154.5 1.0 act_total.1
  155.5 16.3 %all_to_all.28 = bf16[8,128,128]{2,1,0:T(8,128)(2,1)S(1)} all-to-all(bf16[8,128,128]{2,1,0:T(8,128)(2,1)S(1)} %act_total.1), channel_id=1, replica_groups=mesh['z'=8,'y'=8,'x'=4,'c'=2] {'y'}, dimensions={0} | all-to-all | bytes 524288 | tf_op jit(solution)/shard_map/all_to_all | solution.py:200
  171.9 0.9 copy-done.6
  172.8 1.6 update.1
  174.4 0.7 copy.16
  (18 shorter events, 0.1 us)
Async XLA Ops:
  7.2 23.7 %copy-start.5 = (f32[384,448]{0,1:T(8,128)S(1)}, f32[384,448]{0,1:T(8,128)}, u32[]{:S(2)}) copy-start(f32[384,448]{0,1:T(8,128)} %param.8) | copy-start | bytes 2064388
  7.2 23.7 %copy-start.4 = (f32[384,448]{0,1:T(8,128)S(1)}, f32[384,448]{0,1:T(8,128)}, u32[]{:S(2)}) copy-start(f32[384,448]{0,1:T(8,128)} %param.7) | copy-start | bytes 2064388
  7.2 23.7 %copy-start.3 = (f32[384,448]{0,1:T(8,128)S(1)}, f32[384,448]{0,1:T(8,128)}, u32[]{:S(2)}) copy-start(f32[384,448]{0,1:T(8,128)} %param.6) | copy-start | bytes 2064388
  7.2 75.1 %all-gather.5.cloned.1.call-start = ((), (), s32[]{:S(2)}) async-start(), calls=%async_computation.7 | async-start | bytes 1949696 | tf_op jit(solution)/shard_map/all_gather | solution.py:205
  7.9 104.6 %all-gather.7.cloned.1.call-start = ((), (), s32[]{:S(2)}) async-start(), calls=%async_computation.8 | async-start | bytes 2359296 | tf_op jit(solution)/shard_map/all_gather | solution.py:208
  31.0 38.1 %copy-start.7 = (s32[25]{0:T(128)S(1)}, s32[25]{0:T(128)}, u32[]{:S(2)}) copy-start(s32[25]{0:T(128)} %offsets_ref.1) | copy-start | bytes 304
  71.1 50.2 %all-to-all-start.1 = ((bf16[64,80,128]{2,1,0:T(8,128)(2,1)}), bf16[64,80,128]{2,1,0:T(8,128)(2,1)S(1)}, u32[]{:S(2)}, u32[]{:S(2)}) async-start(bf16[64,80,128]{2,1,0:T(8,128)(2,1)} %place.1), calls=%async_computation.1 | async-start | bytes 2621440 | tf_op jit(solution)/shard_map/all_to_all | solution.py:200
  82.2 89.7 %reduce-scatter.2.cloned.1.call-start = ((), (), s32[]{:S(2)}) async-start(), calls=%async_computation.6 | async-start | bytes 2064384 | tf_op jit(solution)/shard_map/reduce_scatter | solution.py:215
  112.5 1.5 copy-start
  114.0 1.6 copy-start.2
  121.2 1.5 copy-start.1
  171.9 0.9 copy-start.6
Sparse Core Ops, SparseCore 0:
  10.2 68.4 all-gather.4
  81.4 31.0 all-gather.6
  121.4 39.7 reduce-scatter.1

commit v4 on v3

--- a/solution.py
+++ b/solution.py
@@ -86,38 +86,58 @@
     )(offsets, slots)
 
 
-def own_core(up_ref, core):
-    parts = [jnp.where(core == 0, up_ref[z, 0], up_ref[z, 1]) for z in range(SIDE)]
-    return jnp.concatenate(parts, axis=1)
-
-
-def sums_kernel(place_ref, state_ref, up_ref, out_ref):
-    up = own_core(up_ref, place_ref[1])
-    state = state_ref[:STRIPS].astype(f32)
-    for y in range(SIDE):
-        weight = state[:, y * 8 : y * 8 + 8].reshape(COLS, ROWS).T.astype(bf16)
-        sums = jnp.dot(weight, up, preferred_element_type=f32).astype(bf16)
-        for z in range(SIDE):
-            out_ref[z, y] = sums[:, z * LANES : (z + 1) * LANES]
-
-
-def act_sums(place, state, up):
-    return pl.pallas_call(
-        sums_kernel,
+def send_kernel(place_ref, act_ref, *out_refs):
+    for s, out_ref in enumerate(out_refs):
+        z = lax.rem(place_ref[0] + s, SIDE)
+        for y in range(SIDE):
+            at = pl.multiple_of((z * SIDE + y) * LANES, LANES)
+            out_ref[y * TOKENS : (y + 1) * TOKENS] = act_ref[:, pl.ds(at, LANES)]
+
+
+def send_blocks(place, act):
+    return pl.pallas_call(
+        send_kernel,
         in_specs=[
             pl.BlockSpec(memory_space=pltpu.SMEM),
             pl.BlockSpec(memory_space=pltpu.VMEM),
-            pl.BlockSpec(memory_space=pltpu.VMEM),
         ],
-        out_shape=jax.ShapeDtypeStruct((SIDE, SIDE, ROWS, LANES), bf16),
+        out_shape=[jax.ShapeDtypeStruct((SIDE * TOKENS, LANES), bf16)] * SIDE,
+        compiler_params=PARAMS,
+        name="send_blocks",
+    )(place, act)
+
+
+def sums_kernel(place_ref, own_ref, other_ref, up_ref, out_ref):
+    core = place_ref[3]
+    halves = []
+    for c in (core, 1 - core):
+        halves.append(jnp.concatenate([up_ref[2 * x + core, c] for x in range(4)], axis=1))
+    up = jnp.concatenate(halves, axis=0)
+    own = own_ref[...].astype(f32)
+    other = other_ref[...].astype(f32)
+    for y in range(SIDE):
+        weight = jnp.concatenate(
+            [w[:, y * 8 : y * 8 + 8].reshape(COLS, ROWS) for w in (own, other)], axis=0
+        )
+        sums = jnp.dot(weight.T.astype(bf16), up, preferred_element_type=f32).astype(bf16)
+        for x in range(4):
+            out_ref[x, y] = sums[:, x * LANES : (x + 1) * LANES]
+
+
+def act_sums(place, own, other, up):
+    vmem = pl.BlockSpec(memory_space=pltpu.VMEM)
+    return pl.pallas_call(
+        sums_kernel,
+        in_specs=[pl.BlockSpec(memory_space=pltpu.SMEM)] + [vmem] * 3,
+        out_shape=jax.ShapeDtypeStruct((SPLITS // 2, SIDE, ROWS, LANES), bf16),
         compiler_params=PARAMS,
         name="act_sums",
-    )(place, state, up)
+    )(place, own, other, up)
 
 
 def total_kernel(parts_ref, out_ref):
     total = parts_ref[0, 0].astype(f32)
-    for m in range(1, SPLITS):
+    for m in range(1, SPLITS // 2):
         total = total + parts_ref[m, 0].astype(f32)
     out_ref[0] = total.T.astype(bf16)
 
@@ -126,7 +146,7 @@
     return pl.pallas_call(
         total_kernel,
         grid=(SIDE,),
-        in_specs=[pl.BlockSpec((SPLITS, 1, ROWS, LANES), lambda i: (0, i, 0, 0))],
+        in_specs=[pl.BlockSpec((SPLITS // 2, 1, ROWS, LANES), lambda i: (0, i, 0, 0))],
         out_specs=pl.BlockSpec((1, LANES, ROWS), lambda i: (i, 0, 0)),
         out_shape=jax.ShapeDtypeStruct((SIDE, LANES, ROWS), bf16),
         compiler_params=PARAMS,
@@ -134,28 +154,33 @@
     )(parts)
 
 
-def grad_kernel(place_ref, up_ref, act_ref, out_ref):
-    up = own_core(up_ref, place_ref[1])
-    act = jnp.concatenate(
-        [act_ref[m, z, 0] for z in range(SIDE) for m in range(SPLITS)], axis=0
-    )
-    out_ref[0] = jnp.dot(up, act, preferred_element_type=f32)
-
-
-def grad_parts(place, up, act):
+def grad_kernel(place_ref, own_ref, other_ref, up_ref, out_ref):
+    up = jnp.concatenate([up_ref[z, place_ref[3]] for z in range(SIDE)], axis=1)
+    for y in range(0, SIDE, 2):
+        act = []
+        for rows in (slice(y * TOKENS, (y + 1) * TOKENS), slice((y + 1) * TOKENS, (y + 2) * TOKENS)):
+            tiles = []
+            for z in range(SIDE):
+                back = lax.rem(place_ref[0] + SIDE - z, SIDE)
+                for m in range(SPLITS):
+                    x = lax.rem(place_ref[2] + 4 - m // 2, 4)
+                    same = place_ref[3] == m % 2
+                    tiles.append(jnp.where(same, own_ref[x, back, rows], other_ref[x, back, rows]))
+            act.append(jnp.concatenate(tiles, axis=0))
+        part = jnp.dot(up, jnp.concatenate(act, axis=1), preferred_element_type=f32)
+        out_ref[y] = part[:, :LANES]
+        out_ref[y + 1] = part[:, LANES:]
+
+
+def grad_parts(place, own, other, up):
+    vmem = pl.BlockSpec(memory_space=pltpu.VMEM)
     return pl.pallas_call(
         grad_kernel,
-        grid=(SIDE,),
-        in_specs=[
-            pl.BlockSpec(memory_space=pltpu.SMEM),
-            pl.BlockSpec((SIDE, 2, COLS, LANES), lambda i: (0, 0, 0, 0)),
-            pl.BlockSpec((SPLITS, SIDE, 1, TOKENS, LANES), lambda i: (0, 0, i, 0, 0)),
-        ],
-        out_specs=pl.BlockSpec((1, COLS, ROWS), lambda i: (i, 0, 0)),
+        in_specs=[pl.BlockSpec(memory_space=pltpu.SMEM)] + [vmem] * 3,
         out_shape=jax.ShapeDtypeStruct((SIDE, COLS, ROWS), f32),
         compiler_params=PARAMS,
         name="grad_parts",
-    )(place, up, act)
+    )(place, own, other, up)
 
 
 def adamw_update(weight, moment_one, moment_two, gradient):
@@ -170,7 +195,7 @@
 
 
 def update_kernel(place_ref, state_ref, grad_ref, weight_ref, first_ref, second_ref):
-    mine = place_ref[0]
+    mine = place_ref[1]
     state = state_ref[:STRIPS].astype(f32)
     weight = state[:, :8]
     for y in range(1, SIDE):
@@ -200,19 +225,27 @@
     return lax.all_to_all(x, axis, split_axis=0, concat_axis=0, tiled=True)
 
 
+def shift(x, axis, by):
+    n = lax.axis_size(axis)
+    return lax.ppermute(x, axis, [(i, (i + by) % n) for i in range(n)])
+
+
 def shards(old_weight, old_first, old_second, old_offsets, activations, upstream):
-    here = jnp.stack([lax.axis_index("y"), lax.axis_index("c")])
+    here = jnp.stack([lax.axis_index(a) for a in ("z", "y", "x", "c")])
     up = lax.all_gather(upstream.T, ("z", "c"), axis=0).reshape(SIDE, 2, COLS, LANES)
-    blocks = activations.reshape(TOKENS, SIDE, SIDE, LANES).transpose(1, 2, 0, 3)
-    mine = exchange(blocks, "z")
-    act = lax.all_gather(mine, ("x", "c"), axis=0)
     got = exchange(pack(old_weight.T, old_first.T, old_second.T), ("z", "y"))
+    sent = send_blocks(here, activations)
+    act = jnp.stack([sent[0]] + [shift(sent[s], "z", s) for s in range(1, SIDE)])
+    got, act = lax.optimization_barrier((got, act))
+    own = jnp.stack([act] + [shift(act, "x", s) for s in range(1, SPLITS // 2)])
     state = exchange(place(old_offsets, got), ("z", "y"))
-    sums = act_sums(here, state, up)
-    total = act_total(exchange(sums, ("x", "c")))
+    parts = grad_parts(here, own, shift(own, "c", 1), up)
+    state, parts = lax.optimization_barrier((state, parts))
+    grad = lax.psum_scatter(parts, "y", scatter_dimension=0)
+    weight = state[:STRIPS, : SIDE * 8]
+    sums = act_sums(here, weight, shift(weight, "c", 1), up)
+    total = act_total(exchange(sums, "x"))
     act_grad = exchange(total, "y").reshape(SIDE * LANES, ROWS)
-    parts = grad_parts(here, up, act)
-    grad = lax.psum_scatter(parts, "y", scatter_dimension=0)
     weight, first, second = update(here, state, grad)
     return (weight.T, first.T, second.T, act_grad)
 

time: 183 us -> 168 us (0.918)
  blocking collectives: 105 us -> 32.7 us
  starting transfers between devices: 11.2 us -> 77.7 us
  waiting for transfers between devices: 31 us -> 23.8 us
    all_to_all x4 -> x2, blocking collectives: 105 us -> 32.7 us  [exchange(): return lax.all_to_all(x, axis, split_axis=0, concat_axis=0, tiled=True)]
    ppermute x0 -> x12, starting transfers between devices: none -> 48.4 us  [shift(): return lax.ppermute(x, axis, [(i, (i + by) % n) for i in range(n)])]
    all_gather x1 -> x0, waiting for transfers between devices: 30.2 us -> none  [shards(): act = lax.all_gather(mine, ('x', 'c'), axis=0)]
    ppermute x0 -> x12, waiting for transfers between devices: none -> 23 us  [shift(): return lax.ppermute(x, axis, [(i, (i + by) % n) for i in range(n)])]
    all_to_all x1 -> x2, starting transfers between devices: 11.1 us -> 29.1 us  [exchange(): return lax.all_to_all(x, axis, split_axis=0, concat_axis=0, tiled=True)]
    pallas_call x1 -> x2, Pallas kernels: 5.62 us -> 3.56 us  [the longest x1 2.93 us: grad_parts(): pl.pallas_call(grad_kernel, in_specs=[pl.BlockSpec(memory_space=pltpu.SME...]
    unnamed x18 -> x24, local copies, waits for them, and re-layouts: 7.21 us -> 6.51 us
  transfers between devices with their start and end apart: 4 -> 16, of which waited for: 1 -> 7; matrix products, arithmetic and copies ran while one was open for 1% -> 0% of each run, Pallas kernels for 6% -> 5%
where the time goes in v4:
time: 168 us; the launch traced here: 166 us
  starting transfers between devices  77.7 us (46%)
  blocking collectives  32.7 us (19%)
  waiting for transfers between devices  23.8 us (14%)
  between operations  14.3 us (9%)
  Pallas kernels  11 us (7%)
  local copies, waits for them, and re-layouts  6.62 us (4%)
    ppermute x12, starting transfers between devices, shift(): return lax.ppermute(x, axis, [(i, (i + by) % n) for i in range(n)])  48.4 us
    all_to_all x2, blocking collectives, exchange(): return lax.all_to_all(x, axis, split_axis=0, concat_axis=0, tiled=True)  32.7 us
    all_to_all x2, starting transfers between devices, exchange(): return lax.all_to_all(x, axis, split_axis=0, concat_axis=0, tiled=True)  29.1 us
    ppermute x12, waiting for transfers between devices, shift(): return lax.ppermute(x, axis, [(i, (i + by) % n) for i in range(n)])  23 us
    unnamed x24, local copies, waits for them, and re-layouts  6.51 us
  transfers between devices with their start and end apart: 16, of which 7 were waited for; matrix products, arithmetic and copies ran while one was open for 0% of the time, Pallas kernels for 5%

profile of v4, /device:TPU:1, one launch (start us, length us, event | category | flops | bytes accessed | tf_op | source)
XLA Modules:
  0.0 166.3 jit_solution(14655154276025001699)
XLA Ops:
  11.6 17.3 %all-to-all-start = ((bf16[64,72,128]{2,1,0:T(8,128)(2,1)}), bf16[64,72,128]{2,1,0:T(8,128)(2,1)S(1)}, u32[]{:S(2)}, u32[]{:S(2)}) async-start(bf16[64,72,128]{2,1,0:T(8,128)(2,1)} %pack.1), calls=%async_computation | async-start | bytes 2359296 | tf_op jit(solution)/shard_map/all_to_all | solution.py:225
  30.3 2.9 %collective-permute-start = (bf16[128,128]{1,0:T(8,128)(2,1)S(1)}, bf16[128,128]{1,0:T(8,128)(2,1)S(1)}, u32[]{:S(2)}, u32[]{:S(2)}) collective-permute-start(bf16[128,128]{1,0:T(8,128)(2,1)S(1)} %get-tuple-element.20), channel_id=1, source_target_pairs={{0,64},{64,128},{128,192},{192,256},{256,320},{320,384},{384,448},... | collective-permute-start | bytes 98312 | tf_op jit(solution)/shard_map/ppermute | solution.py:230
  33.3 4.0 %collective-permute-start.1 = (bf16[128,128]{1,0:T(8,128)(2,1)S(1)}, bf16[128,128]{1,0:T(8,128)(2,1)S(1)}, u32[]{:S(2)}, u32[]{:S(2)}) collective-permute-start(bf16[128,128]{1,0:T(8,128)(2,1)S(1)} %get-tuple-element.21), channel_id=1, source_target_pairs={{0,128},{64,192},{128,256},{192,320},{256,384},{320,448},{384,0},{... | collective-permute-start | bytes 98312 | tf_op jit(solution)/shard_map/ppermute | solution.py:230
  37.3 4.5 %collective-permute-start.2 = (bf16[128,128]{1,0:T(8,128)(2,1)S(1)}, bf16[128,128]{1,0:T(8,128)(2,1)S(1)}, u32[]{:S(2)}, u32[]{:S(2)}) collective-permute-start(bf16[128,128]{1,0:T(8,128)(2,1)S(1)} %get-tuple-element.22), channel_id=1, source_target_pairs={{0,192},{64,256},{128,320},{192,384},{256,448},{320,0},{384,64},{4... | collective-permute-start | bytes 98312 | tf_op jit(solution)/shard_map/ppermute | solution.py:230
  41.8 3.8 %collective-permute-start.3 = (bf16[128,128]{1,0:T(8,128)(2,1)S(1)}, bf16[128,128]{1,0:T(8,128)(2,1)S(1)}, u32[]{:S(2)}, u32[]{:S(2)}) collective-permute-start(bf16[128,128]{1,0:T(8,128)(2,1)S(1)} %get-tuple-element.23), channel_id=1, source_target_pairs={{0,256},{64,320},{128,384},{192,448},{256,0},{320,64},{384,128},{4... | collective-permute-start | bytes 98312 | tf_op jit(solution)/shard_map/ppermute | solution.py:230
  45.6 4.6 %collective-permute-start.4 = (bf16[128,128]{1,0:T(8,128)(2,1)S(1)}, bf16[128,128]{1,0:T(8,128)(2,1)S(1)}, u32[]{:S(2)}, u32[]{:S(2)}) collective-permute-start(bf16[128,128]{1,0:T(8,128)(2,1)S(1)} %get-tuple-element.24), channel_id=1, source_target_pairs={{0,320},{64,384},{128,448},{192,0},{256,64},{320,128},{384,192},{4... | collective-permute-start | bytes 98312 | tf_op jit(solution)/shard_map/ppermute | solution.py:230
  50.2 5.1 %collective-permute-start.5 = (bf16[128,128]{1,0:T(8,128)(2,1)S(1)}, bf16[128,128]{1,0:T(8,128)(2,1)S(1)}, u32[]{:S(2)}, u32[]{:S(2)}) collective-permute-start(bf16[128,128]{1,0:T(8,128)(2,1)S(1)} %get-tuple-element.25), channel_id=1, source_target_pairs={{0,384},{64,448},{128,0},{192,64},{256,128},{320,192},{384,256},{4... | collective-permute-start | bytes 98312 | tf_op jit(solution)/shard_map/ppermute | solution.py:230
  55.3 3.0 %collective-permute-start.6 = (bf16[128,128]{1,0:T(8,128)(2,1)S(1)}, bf16[128,128]{1,0:T(8,128)(2,1)S(1)}, u32[]{:S(2)}, u32[]{:S(2)}) collective-permute-start(bf16[128,128]{1,0:T(8,128)(2,1)S(1)} %get-tuple-element.26), channel_id=1, source_target_pairs={{0,448},{64,0},{128,64},{192,128},{256,192},{320,256},{384,320},{4... | collective-permute-start | bytes 98312 | tf_op jit(solution)/shard_map/ppermute | solution.py:230
  58.3 5.9 %collective-permute-done.2 = bf16[128,128]{1,0:T(8,128)(2,1)S(1)} collective-permute-done((bf16[128,128]{1,0:T(8,128)(2,1)S(1)}, bf16[128,128]{1,0:T(8,128)(2,1)S(1)}, u32[]{:S(2)}, u32[]{:S(2)}) %collective-permute-start.2) | collective-permute-done | bytes 32800 | tf_op jit(solution)/shard_map/ppermute | solution.py:230
  64.3 2.0 %collective-permute-done.3 = bf16[128,128]{1,0:T(8,128)(2,1)S(1)} collective-permute-done((bf16[128,128]{1,0:T(8,128)(2,1)S(1)}, bf16[128,128]{1,0:T(8,128)(2,1)S(1)}, u32[]{:S(2)}, u32[]{:S(2)}) %collective-permute-start.3) | collective-permute-done | bytes 32800 | tf_op jit(solution)/shard_map/ppermute | solution.py:230
  66.4 1.9 %place.1 = bf16[64,80,128]{2,1,0:T(8,128)(2,1)} custom-call(s32[25]{0:T(128)S(1)} %copy-done.7, bf16[64,72,128]{2,1,0:T(8,128)(2,1)S(1)} %all-to-all-done.slots_ref), custom_call_target="tpu_custom_call" | custom-call | tf_op jit(solution)/shard_map/place/pallas_call | solution.py:74
  68.3 11.9 %all-to-all-start.1 = ((bf16[64,80,128]{2,1,0:T(8,128)(2,1)}), bf16[64,80,128]{2,1,0:T(8,128)(2,1)S(1)}, u32[]{:S(2)}, u32[]{:S(2)}) async-start(bf16[64,80,128]{2,1,0:T(8,128)(2,1)} %place.1), calls=%async_computation.1 | async-start | bytes 2621440 | tf_op jit(solution)/shard_map/all_to_all | solution.py:225
  80.2 4.4 %collective-permute-start.9 = (bf16[8,128,128]{2,1,0:T(8,128)(2,1)S(1)}, bf16[8,128,128]{2,1,0:T(8,128)(2,1)S(1)}, u32[]{:S(2)}, u32[]{:S(2)}) collective-permute-start(bf16[8,128,128]{2,1,0:T(8,128)(2,1)S(1)} %bitcast_dynamic-update-slice_fusion), channel_id=1, source_target_pairs={{0,6},{2,0},{4,2},{6,4},{1,7},{3,1},{5,3},{7,5},{8,14},{10,8},{12,... | collective-permute-start | bytes 786440 | tf_op jit(solution)/shard_map/ppermute | solution.py:230
  84.6 2.5 %collective-permute-start.8 = (bf16[8,128,128]{2,1,0:T(8,128)(2,1)S(1)}, bf16[8,128,128]{2,1,0:T(8,128)(2,1)S(1)}, u32[]{:S(2)}, u32[]{:S(2)}) collective-permute-start(bf16[8,128,128]{2,1,0:T(8,128)(2,1)S(1)} %bitcast_dynamic-update-slice_fusion), channel_id=1, source_target_pairs={{0,4},{2,6},{4,0},{6,2},{1,5},{3,7},{5,1},{7,3},{8,12},{10,14},{12... | collective-permute-start | bytes 786440 | tf_op jit(solution)/shard_map/ppermute | solution.py:230
  87.1 2.5 %collective-permute-start.7 = (bf16[8,128,128]{2,1,0:T(8,128)(2,1)S(1)}, bf16[8,128,128]{2,1,0:T(8,128)(2,1)S(1)}, u32[]{:S(2)}, u32[]{:S(2)}) collective-permute-start(bf16[8,128,128]{2,1,0:T(8,128)(2,1)S(1)} %bitcast_dynamic-update-slice_fusion), channel_id=1, source_target_pairs={{0,2},{2,4},{4,6},{6,0},{1,3},{3,5},{5,7},{7,1},{8,10},{10,12},{12... | collective-permute-start | bytes 786440 | tf_op jit(solution)/shard_map/ppermute | solution.py:230
  89.6 3.9 %collective-permute-done.8 = bf16[8,128,128]{2,1,0:T(8,128)(2,1)S(1)} collective-permute-done((bf16[8,128,128]{2,1,0:T(8,128)(2,1)S(1)}, bf16[8,128,128]{2,1,0:T(8,128)(2,1)S(1)}, u32[]{:S(2)}, u32[]{:S(2)}) %collective-permute-start.8) | collective-permute-done | bytes 262176 | tf_op jit(solution)/shard_map/ppermute | solution.py:230
  93.5 6.8 %collective-permute-done.7 = bf16[8,128,128]{2,1,0:T(8,128)(2,1)S(1)} collective-permute-done((bf16[8,128,128]{2,1,0:T(8,128)(2,1)S(1)}, bf16[8,128,128]{2,1,0:T(8,128)(2,1)S(1)}, u32[]{:S(2)}, u32[]{:S(2)}) %collective-permute-start.7) | collective-permute-done | bytes 262176 | tf_op jit(solution)/shard_map/ppermute | solution.py:230
  100.5 3.9 %collective-permute-start.10 = (bf16[4,8,128,128]{3,2,1,0:T(8,128)(2,1)S(1)}, bf16[4,8,128,128]{3,2,1,0:T(8,128)(2,1)S(1)}, u32[]{:S(2)}, u32[]{:S(2)}) collective-permute-start(bf16[4,8,128,128]{3,2,1,0:T(8,128)(2,1)S(1)} %pad_maximum_fusion.own_ref), channel_id=1, source_target_pairs={{0,1},{1,0},{2,3},{3,2},{4,5},{5,4},{6,7},{7,6},{8,9},{9,8},{10,11... | collective-permute-start | bytes 3145736 | tf_op jit(solution)/shard_map/ppermute | solution.py:230
  104.4 2.2 %collective-permute-done.10.other_ref = bf16[4,8,128,128]{3,2,1,0:T(8,128)(2,1)S(1)} collective-permute-done((bf16[4,8,128,128]{3,2,1,0:T(8,128)(2,1)S(1)}, bf16[4,8,128,128]{3,2,1,0:T(8,128)(2,1)S(1)}, u32[]{:S(2)}, u32[]{:S(2)}) %collective-permute-start.10) | collective-permute-done | bytes 1048608 | tf_op jit(solution)/shard_map/ppermute | solution.py:230
  108.1 2.9 %grad_parts.1 = f32[8,448,128]{2,1,0:T(8,128)} custom-call(s32[4]{0:T(128)S(1)} %pad_add_fusion.place_ref, bf16[4,8,128,128]{3,2,1,0:T(8,128)(2,1)S(1)} %pad_maximum_fusion.own_ref, bf16[4,8,128,128]{3,2,1,0:T(8,128)(2,1)S(1)} %collective-permute-done.10.other_ref, bf16[8,2,448,128]{3,2,1,0:T(8,128)(2,1)S(1)} %bitcast.34), custom_call_target="tpu_custom_call" | custom-call | tf_op jit(solution)/shard_map/grad_parts/pallas_call | solution.py:177
  111.3 7.3 %collective-permute-start.11 = (bf16[56,64,128]{2,1,0:T(8,128)(2,1)S(1)}, bf16[56,64,128]{2,1,0:T(8,128)(2,1)S(1)}, u32[]{:S(2)}, u32[]{:S(2)}) collective-permute-start(bf16[56,64,128]{2,1,0:T(8,128)(2,1)S(1)} %slice.3.own_ref), channel_id=1, source_target_pairs={{0,1},{1,0},{2,3},{3,2},{4,5},{5,4},{6,7},{7,6},{8,9},{9,8},{10,11... | collective-permute-start | bytes 2752520 | tf_op jit(solution)/shard_map/ppermute | solution.py:230
  118.7 2.1 %collective-permute-done.11.other_ref = bf16[56,64,128]{2,1,0:T(8,128)(2,1)S(1)} collective-permute-done((bf16[56,64,128]{2,1,0:T(8,128)(2,1)S(1)}, bf16[56,64,128]{2,1,0:T(8,128)(2,1)S(1)}, u32[]{:S(2)}, u32[]{:S(2)}) %collective-permute-start.11) | collective-permute-done | bytes 917536 | tf_op jit(solution)/shard_map/ppermute | solution.py:230
  122.6 18.1 %all_to_all.20.parts_ref = bf16[4,8,128,128]{3,2,1,0:T(8,128)(2,1)S(1)} all-to-all(bf16[4,8,128,128]{3,2,1,0:T(8,128)(2,1)S(1)} %act_sums.1), channel_id=1, replica_groups=mesh['z'=8,'y'=8,'x'=4,'c'=2] {'x'}, dimensions={0} | all-to-all | bytes 2097152 | tf_op jit(solution)/shard_map/all_to_all | solution.py:225
  141.7 14.6 %all_to_all.21 = bf16[8,128,128]{2,1,0:T(8,128)(2,1)S(1)} all-to-all(bf16[8,128,128]{2,1,0:T(8,128)(2,1)S(1)} %act_total.1), channel_id=1, replica_groups=mesh['z'=8,'y'=8,'x'=4,'c'=2] {'y'}, dimensions={0} | all-to-all | bytes 524288 | tf_op jit(solution)/shard_map/all_to_all | solution.py:225
  (47 shorter events, 13.9 us)
Async XLA Ops:
  7.2 1.1 copy-start.2
  8.3 1.1 copy-start.3
  9.4 1.1 copy-start.4
  11.6 18.1 %copy-start.5 = (bf16[16,8192]{1,0:T(8,128)(2,1)S(1)}, bf16[16,8192]{1,0:T(8,128)(2,1)}, u32[]{:S(2)}) copy-start(bf16[16,8192]{1,0:T(8,128)(2,1)} %act_ref.1) | copy-start | bytes 786436
  11.6 54.7 %copy-start.7 = (s32[25]{0:T(128)S(1)}, s32[25]{0:T(128)}, u32[]{:S(2)}) copy-start(s32[25]{0:T(128)} %offsets_ref.1) | copy-start | bytes 304
  11.6 54.7 %all-to-all-start = ((bf16[64,72,128]{2,1,0:T(8,128)(2,1)}), bf16[64,72,128]{2,1,0:T(8,128)(2,1)S(1)}, u32[]{:S(2)}, u32[]{:S(2)}) async-start(bf16[64,72,128]{2,1,0:T(8,128)(2,1)} %pack.1), calls=%async_computation | async-start | bytes 2359296 | tf_op jit(solution)/shard_map/all_to_all | solution.py:225
  28.9 75.5 %all-gather.3.cloned.1.call-start = ((), (), s32[]{:S(2)}) async-start(), calls=%async_computation.6 | async-start | bytes 1949696 | tf_op jit(solution)/shard_map/all_gather | solution.py:235
  30.3 19.8 %collective-permute-start = (bf16[128,128]{1,0:T(8,128)(2,1)S(1)}, bf16[128,128]{1,0:T(8,128)(2,1)S(1)}, u32[]{:S(2)}, u32[]{:S(2)}) collective-permute-start(bf16[128,128]{1,0:T(8,128)(2,1)S(1)} %get-tuple-element.20), channel_id=1, source_target_pairs={{0,64},{64,128},{128,192},{192,256},{256,320},{320,384},{384,448},... | collective-permute-start | bytes 98312 | tf_op jit(solution)/shard_map/ppermute | solution.py:230
  33.3 22.0 %collective-permute-start.1 = (bf16[128,128]{1,0:T(8,128)(2,1)S(1)}, bf16[128,128]{1,0:T(8,128)(2,1)S(1)}, u32[]{:S(2)}, u32[]{:S(2)}) collective-permute-start(bf16[128,128]{1,0:T(8,128)(2,1)S(1)} %get-tuple-element.21), channel_id=1, source_target_pairs={{0,128},{64,192},{128,256},{192,320},{256,384},{320,448},{384,0},{... | collective-permute-start | bytes 98312 | tf_op jit(solution)/shard_map/ppermute | solution.py:230
  37.3 27.0 %collective-permute-start.2 = (bf16[128,128]{1,0:T(8,128)(2,1)S(1)}, bf16[128,128]{1,0:T(8,128)(2,1)S(1)}, u32[]{:S(2)}, u32[]{:S(2)}) collective-permute-start(bf16[128,128]{1,0:T(8,128)(2,1)S(1)} %get-tuple-element.22), channel_id=1, source_target_pairs={{0,192},{64,256},{128,320},{192,384},{256,448},{320,0},{384,64},{4... | collective-permute-start | bytes 98312 | tf_op jit(solution)/shard_map/ppermute | solution.py:230
  41.8 24.5 %collective-permute-start.3 = (bf16[128,128]{1,0:T(8,128)(2,1)S(1)}, bf16[128,128]{1,0:T(8,128)(2,1)S(1)}, u32[]{:S(2)}, u32[]{:S(2)}) collective-permute-start(bf16[128,128]{1,0:T(8,128)(2,1)S(1)} %get-tuple-element.23), channel_id=1, source_target_pairs={{0,256},{64,320},{128,384},{192,448},{256,0},{320,64},{384,128},{4... | collective-permute-start | bytes 98312 | tf_op jit(solution)/shard_map/ppermute | solution.py:230
  45.6 20.7 %collective-permute-start.4 = (bf16[128,128]{1,0:T(8,128)(2,1)S(1)}, bf16[128,128]{1,0:T(8,128)(2,1)S(1)}, u32[]{:S(2)}, u32[]{:S(2)}) collective-permute-start(bf16[128,128]{1,0:T(8,128)(2,1)S(1)} %get-tuple-element.24), channel_id=1, source_target_pairs={{0,320},{64,384},{128,448},{192,0},{256,64},{320,128},{384,192},{4... | collective-permute-start | bytes 98312 | tf_op jit(solution)/shard_map/ppermute | solution.py:230
  50.2 16.1 %collective-permute-start.5 = (bf16[128,128]{1,0:T(8,128)(2,1)S(1)}, bf16[128,128]{1,0:T(8,128)(2,1)S(1)}, u32[]{:S(2)}, u32[]{:S(2)}) collective-permute-start(bf16[128,128]{1,0:T(8,128)(2,1)S(1)} %get-tuple-element.25), channel_id=1, source_target_pairs={{0,384},{64,448},{128,0},{192,64},{256,128},{320,192},{384,256},{4... | collective-permute-start | bytes 98312 | tf_op jit(solution)/shard_map/ppermute | solution.py:230
  55.3 11.0 %collective-permute-start.6 = (bf16[128,128]{1,0:T(8,128)(2,1)S(1)}, bf16[128,128]{1,0:T(8,128)(2,1)S(1)}, u32[]{:S(2)}, u32[]{:S(2)}) collective-permute-start(bf16[128,128]{1,0:T(8,128)(2,1)S(1)} %get-tuple-element.26), channel_id=1, source_target_pairs={{0,448},{64,0},{128,64},{192,128},{256,192},{320,256},{384,320},{4... | collective-permute-start | bytes 98312 | tf_op jit(solution)/shard_map/ppermute | solution.py:230
  68.3 42.9 %all-to-all-start.1 = ((bf16[64,80,128]{2,1,0:T(8,128)(2,1)}), bf16[64,80,128]{2,1,0:T(8,128)(2,1)S(1)}, u32[]{:S(2)}, u32[]{:S(2)}) async-start(bf16[64,80,128]{2,1,0:T(8,128)(2,1)} %place.1), calls=%async_computation.1 | async-start | bytes 2621440 | tf_op jit(solution)/shard_map/all_to_all | solution.py:225
  80.2 76.1 %reduce-scatter.2.cloned.1.call-start = ((), (), s32[]{:S(2)}) async-start(), calls=%async_computation.5 | async-start | bytes 2064384 | tf_op jit(solution)/shard_map/reduce_scatter | solution.py:244
  80.2 9.4 %collective-permute-start.9 = (bf16[8,128,128]{2,1,0:T(8,128)(2,1)S(1)}, bf16[8,128,128]{2,1,0:T(8,128)(2,1)S(1)}, u32[]{:S(2)}, u32[]{:S(2)}) collective-permute-start(bf16[8,128,128]{2,1,0:T(8,128)(2,1)S(1)} %bitcast_dynamic-update-slice_fusion), channel_id=1, source_target_pairs={{0,6},{2,0},{4,2},{6,4},{1,7},{3,1},{5,3},{7,5},{8,14},{10,8},{12,... | collective-permute-start | bytes 786440 | tf_op jit(solution)/shard_map/ppermute | solution.py:230
  84.6 8.9 %collective-permute-start.8 = (bf16[8,128,128]{2,1,0:T(8,128)(2,1)S(1)}, bf16[8,128,128]{2,1,0:T(8,128)(2,1)S(1)}, u32[]{:S(2)}, u32[]{:S(2)}) collective-permute-start(bf16[8,128,128]{2,1,0:T(8,128)(2,1)S(1)} %bitcast_dynamic-update-slice_fusion), channel_id=1, source_target_pairs={{0,4},{2,6},{4,0},{6,2},{1,5},{3,7},{5,1},{7,3},{8,12},{10,14},{12... | collective-permute-start | bytes 786440 | tf_op jit(solution)/shard_map/ppermute | solution.py:230
  87.1 13.3 %collective-permute-start.7 = (bf16[8,128,128]{2,1,0:T(8,128)(2,1)S(1)}, bf16[8,128,128]{2,1,0:T(8,128)(2,1)S(1)}, u32[]{:S(2)}, u32[]{:S(2)}) collective-permute-start(bf16[8,128,128]{2,1,0:T(8,128)(2,1)S(1)} %bitcast_dynamic-update-slice_fusion), channel_id=1, source_target_pairs={{0,2},{2,4},{4,6},{6,0},{1,3},{3,5},{5,7},{7,1},{8,10},{10,12},{12... | collective-permute-start | bytes 786440 | tf_op jit(solution)/shard_map/ppermute | solution.py:230
  100.5 6.2 %collective-permute-start.10 = (bf16[4,8,128,128]{3,2,1,0:T(8,128)(2,1)S(1)}, bf16[4,8,128,128]{3,2,1,0:T(8,128)(2,1)S(1)}, u32[]{:S(2)}, u32[]{:S(2)}) collective-permute-start(bf16[4,8,128,128]{3,2,1,0:T(8,128)(2,1)S(1)} %pad_maximum_fusion.own_ref), channel_id=1, source_target_pairs={{0,1},{1,0},{2,3},{3,2},{4,5},{5,4},{6,7},{7,6},{8,9},{9,8},{10,11... | collective-permute-start | bytes 3145736 | tf_op jit(solution)/shard_map/ppermute | solution.py:230
  106.6 1.5 copy-start
  111.2 9.5 %copy-start.1 = (bf16[7168,128]{1,0:T(8,128)(2,1)S(1)}, bf16[7168,128]{1,0:T(8,128)(2,1)}, u32[]{:S(2)}) copy-start(bf16[7168,128]{1,0:T(8,128)(2,1)} %all-gather.3.cloned.1.call-done) | copy-start | bytes 5505028
  111.3 9.4 %collective-permute-start.11 = (bf16[56,64,128]{2,1,0:T(8,128)(2,1)S(1)}, bf16[56,64,128]{2,1,0:T(8,128)(2,1)S(1)}, u32[]{:S(2)}, u32[]{:S(2)}) collective-permute-start(bf16[56,64,128]{2,1,0:T(8,128)(2,1)S(1)} %slice.3.own_ref), channel_id=1, source_target_pairs={{0,1},{1,0},{2,3},{3,2},{4,5},{5,4},{6,7},{7,6},{8,9},{9,8},{10,11... | collective-permute-start | bytes 2752520 | tf_op jit(solution)/shard_map/ppermute | solution.py:230
  156.3 0.9 copy-start.6
Sparse Core Ops, SparseCore 0:
  31.8 57.2 all-gather.2
  111.3 38.8 reduce-scatter.1

commit v5 on v4

--- a/solution.py
+++ b/solution.py
@@ -64,10 +64,10 @@
         rows_ref[after] = jnp.where(lane < shift, turned, rows_ref[after])
     for z in range(SIDE):
         rows = rows_ref[z * SIDE : (z + 1) * SIDE]
-        weights = rows[:, :8].reshape(64, LANES)
+        weights = rows[:, :8].reshape(64, LANES).astype(bf16)
         for y in range(SIDE):
-            both = jnp.concatenate([weights, rows[y, 8:]], axis=0)
-            out_ref[z * SIDE + y] = both.astype(bf16)
+            out_ref[z * SIDE + y, :64] = weights
+            out_ref[z * SIDE + y, 64:] = rows[y, 8:].astype(bf16)
 
 
 def place(offsets, slots):
@@ -136,18 +136,16 @@
 
 
 def total_kernel(parts_ref, out_ref):
-    total = parts_ref[0, 0].astype(f32)
-    for m in range(1, SPLITS // 2):
-        total = total + parts_ref[m, 0].astype(f32)
-    out_ref[0] = total.T.astype(bf16)
+    for y in range(SIDE):
+        total = parts_ref[0, y].astype(f32)
+        for x in range(1, SPLITS // 2):
+            total = total + parts_ref[x, y].astype(f32)
+        out_ref[y] = total.T.astype(bf16)
 
 
 def act_total(parts):
     return pl.pallas_call(
         total_kernel,
-        grid=(SIDE,),
-        in_specs=[pl.BlockSpec((SPLITS // 2, 1, ROWS, LANES), lambda i: (0, i, 0, 0))],
-        out_specs=pl.BlockSpec((1, LANES, ROWS), lambda i: (i, 0, 0)),
         out_shape=jax.ShapeDtypeStruct((SIDE, LANES, ROWS), bf16),
         compiler_params=PARAMS,
         name="act_total",
@@ -238,6 +236,7 @@
     act = jnp.stack([sent[0]] + [shift(sent[s], "z", s) for s in range(1, SIDE)])
     got, act = lax.optimization_barrier((got, act))
     own = jnp.stack([act] + [shift(act, "x", s) for s in range(1, SPLITS // 2)])
+    own, up = lax.optimization_barrier((own, up))
     state = exchange(place(old_offsets, got), ("z", "y"))
     parts = grad_parts(here, own, shift(own, "c", 1), up)
     state, parts = lax.optimization_barrier((state, parts))
@@ -245,8 +244,10 @@
     weight = state[:STRIPS, : SIDE * 8]
     sums = act_sums(here, weight, shift(weight, "c", 1), up)
     total = act_total(exchange(sums, "x"))
-    act_grad = exchange(total, "y").reshape(SIDE * LANES, ROWS)
-    weight, first, second = update(here, state, grad)
+    last = exchange(total, "y")
+    new = update(here, state, grad)
+    last, (weight, first, second) = lax.optimization_barrier((last, new))
+    act_grad = last.reshape(SIDE * LANES, ROWS)
     return (weight.T, first.T, second.T, act_grad)
 
 

time: 168 us -> 168 us (level)
  the two profiles are of different devices: /device:TPU:1 before, /device:TPU:90 now
where the time goes in v5:
time: 168 us; the launch traced here: 167 us
  starting transfers between devices  78.6 us (47%)
  waiting for transfers between devices  37.8 us (22%)
  blocking collectives  18.5 us (11%)
  between operations  14.3 us (9%)
  Pallas kernels  11 us (7%)
  local copies, waits for them, and re-layouts  6.62 us (4%)
    ppermute x12, starting transfers between devices, shift(): return lax.ppermute(x, axis, [(i, (i + by) % n) for i in range(n)])  45.3 us
    all_to_all x3, starting transfers between devices, exchange(): return lax.all_to_all(x, axis, split_axis=0, concat_axis=0, tiled=True)  33.3 us
    ppermute x12, waiting for transfers between devices, shift(): return lax.ppermute(x, axis, [(i, (i + by) % n) for i in range(n)])  19.5 us
    all_to_all x1, blocking collectives, exchange(): return lax.all_to_all(x, axis, split_axis=0, concat_axis=0, tiled=True)  18.5 us
    reduce_scatter x1, waiting for transfers between devices, shards(): grad = lax.psum_scatter(parts, 'y', scatter_dimension=0)  12.5 us
    unnamed x24, local copies, waits for them, and re-layouts  6.51 us
    all_to_all x3, waiting for transfers between devices, exchange(): return lax.all_to_all(x, axis, split_axis=0, concat_axis=0, tiled=True)  5.16 us
  transfers between devices with their start and end apart: 17, of which 8 were waited for; matrix products, arithmetic and copies ran while one was open for 0% of the time, Pallas kernels for 6%

profile of v5, /device:TPU:90, one launch (start us, length us, event | category | flops | bytes accessed | tf_op | source)
XLA Modules:
  0.0 167.1 jit_solution(13820314009137021978)
XLA Ops:
  11.6 15.6 %all-to-all-start = ((bf16[64,72,128]{2,1,0:T(8,128)(2,1)}), bf16[64,72,128]{2,1,0:T(8,128)(2,1)S(1)}, u32[]{:S(2)}, u32[]{:S(2)}) async-start(bf16[64,72,128]{2,1,0:T(8,128)(2,1)} %pack.1), calls=%async_computation | async-start | bytes 2359296 | tf_op jit(solution)/shard_map/all_to_all | solution.py:223
  28.7 3.4 %collective-permute-start = (bf16[128,128]{1,0:T(8,128)(2,1)S(1)}, bf16[128,128]{1,0:T(8,128)(2,1)S(1)}, u32[]{:S(2)}, u32[]{:S(2)}) collective-permute-start(bf16[128,128]{1,0:T(8,128)(2,1)S(1)} %get-tuple-element.26), channel_id=1, source_target_pairs={{0,64},{64,128},{128,192},{192,256},{256,320},{320,384},{384,448},... | collective-permute-start | bytes 98312 | tf_op jit(solution)/shard_map/ppermute | solution.py:228
  32.0 5.6 %collective-permute-start.1 = (bf16[128,128]{1,0:T(8,128)(2,1)S(1)}, bf16[128,128]{1,0:T(8,128)(2,1)S(1)}, u32[]{:S(2)}, u32[]{:S(2)}) collective-permute-start(bf16[128,128]{1,0:T(8,128)(2,1)S(1)} %get-tuple-element.27), channel_id=1, source_target_pairs={{0,128},{64,192},{128,256},{192,320},{256,384},{320,448},{384,0},{... | collective-permute-start | bytes 98312 | tf_op jit(solution)/shard_map/ppermute | solution.py:228
  37.6 2.6 %collective-permute-start.2 = (bf16[128,128]{1,0:T(8,128)(2,1)S(1)}, bf16[128,128]{1,0:T(8,128)(2,1)S(1)}, u32[]{:S(2)}, u32[]{:S(2)}) collective-permute-start(bf16[128,128]{1,0:T(8,128)(2,1)S(1)} %get-tuple-element.28), channel_id=1, source_target_pairs={{0,192},{64,256},{128,320},{192,384},{256,448},{320,0},{384,64},{4... | collective-permute-start | bytes 98312 | tf_op jit(solution)/shard_map/ppermute | solution.py:228
  40.3 4.9 %collective-permute-start.3 = (bf16[128,128]{1,0:T(8,128)(2,1)S(1)}, bf16[128,128]{1,0:T(8,128)(2,1)S(1)}, u32[]{:S(2)}, u32[]{:S(2)}) collective-permute-start(bf16[128,128]{1,0:T(8,128)(2,1)S(1)} %get-tuple-element.29), channel_id=1, source_target_pairs={{0,256},{64,320},{128,384},{192,448},{256,0},{320,64},{384,128},{4... | collective-permute-start | bytes 98312 | tf_op jit(solution)/shard_map/ppermute | solution.py:228
  45.2 3.6 %collective-permute-start.4 = (bf16[128,128]{1,0:T(8,128)(2,1)S(1)}, bf16[128,128]{1,0:T(8,128)(2,1)S(1)}, u32[]{:S(2)}, u32[]{:S(2)}) collective-permute-start(bf16[128,128]{1,0:T(8,128)(2,1)S(1)} %get-tuple-element.30), channel_id=1, source_target_pairs={{0,320},{64,384},{128,448},{192,0},{256,64},{320,128},{384,192},{4... | collective-permute-start | bytes 98312 | tf_op jit(solution)/shard_map/ppermute | solution.py:228
  48.9 4.5 %collective-permute-start.5 = (bf16[128,128]{1,0:T(8,128)(2,1)S(1)}, bf16[128,128]{1,0:T(8,128)(2,1)S(1)}, u32[]{:S(2)}, u32[]{:S(2)}) collective-permute-start(bf16[128,128]{1,0:T(8,128)(2,1)S(1)} %get-tuple-element.31), channel_id=1, source_target_pairs={{0,384},{64,448},{128,0},{192,64},{256,128},{320,192},{384,256},{4... | collective-permute-start | bytes 98312 | tf_op jit(solution)/shard_map/ppermute | solution.py:228
  53.4 5.2 %collective-permute-done.1 = bf16[128,128]{1,0:T(8,128)(2,1)S(1)} collective-permute-done((bf16[128,128]{1,0:T(8,128)(2,1)S(1)}, bf16[128,128]{1,0:T(8,128)(2,1)S(1)}, u32[]{:S(2)}, u32[]{:S(2)}) %collective-permute-start.1) | collective-permute-done | bytes 32800 | tf_op jit(solution)/shard_map/ppermute | solution.py:228
  58.6 6.1 %collective-permute-start.6 = (bf16[128,128]{1,0:T(8,128)(2,1)S(1)}, bf16[128,128]{1,0:T(8,128)(2,1)S(1)}, u32[]{:S(2)}, u32[]{:S(2)}) collective-permute-start(bf16[128,128]{1,0:T(8,128)(2,1)S(1)} %get-tuple-element.32), channel_id=1, source_target_pairs={{0,448},{64,0},{128,64},{192,128},{256,192},{320,256},{384,320},{4... | collective-permute-start | bytes 98312 | tf_op jit(solution)/shard_map/ppermute | solution.py:228
  66.3 2.0 %place.1 = bf16[64,80,128]{2,1,0:T(8,128)(2,1)} custom-call(s32[25]{0:T(128)S(1)} %copy-done.7, bf16[64,72,128]{2,1,0:T(8,128)(2,1)S(1)} %all-to-all-done.slots_ref), custom_call_target="tpu_custom_call" | custom-call | tf_op jit(solution)/shard_map/place/pallas_call | solution.py:74
  68.3 11.6 %all-to-all-start.1 = ((bf16[64,80,128]{2,1,0:T(8,128)(2,1)}), bf16[64,80,128]{2,1,0:T(8,128)(2,1)S(1)}, u32[]{:S(2)}, u32[]{:S(2)}) async-start(bf16[64,80,128]{2,1,0:T(8,128)(2,1)} %place.1), calls=%async_computation.1 | async-start | bytes 2621440 | tf_op jit(solution)/shard_map/all_to_all | solution.py:223
  79.9 3.4 %collective-permute-start.7 = (bf16[8,128,128]{2,1,0:T(8,128)(2,1)S(1)}, bf16[8,128,128]{2,1,0:T(8,128)(2,1)S(1)}, u32[]{:S(2)}, u32[]{:S(2)}) collective-permute-start(bf16[8,128,128]{2,1,0:T(8,128)(2,1)S(1)} %bitcast_dynamic-update-slice_fusion), channel_id=1, source_target_pairs={{0,2},{2,4},{4,6},{6,0},{1,3},{3,5},{5,7},{7,1},{8,10},{10,12},{12... | collective-permute-start | bytes 786440 | tf_op jit(solution)/shard_map/ppermute | solution.py:228
  83.3 2.9 %collective-permute-start.8 = (bf16[8,128,128]{2,1,0:T(8,128)(2,1)S(1)}, bf16[8,128,128]{2,1,0:T(8,128)(2,1)S(1)}, u32[]{:S(2)}, u32[]{:S(2)}) collective-permute-start(bf16[8,128,128]{2,1,0:T(8,128)(2,1)S(1)} %bitcast_dynamic-update-slice_fusion), channel_id=1, source_target_pairs={{0,4},{2,6},{4,0},{6,2},{1,5},{3,7},{5,1},{7,3},{8,12},{10,14},{12... | collective-permute-start | bytes 786440 | tf_op jit(solution)/shard_map/ppermute | solution.py:228
  86.2 4.2 %collective-permute-start.9 = (bf16[8,128,128]{2,1,0:T(8,128)(2,1)S(1)}, bf16[8,128,128]{2,1,0:T(8,128)(2,1)S(1)}, u32[]{:S(2)}, u32[]{:S(2)}) collective-permute-start(bf16[8,128,128]{2,1,0:T(8,128)(2,1)S(1)} %bitcast_dynamic-update-slice_fusion), channel_id=1, source_target_pairs={{0,6},{2,0},{4,2},{6,4},{1,7},{3,1},{5,3},{7,5},{8,14},{10,8},{12,... | collective-permute-start | bytes 786440 | tf_op jit(solution)/shard_map/ppermute | solution.py:228
  90.4 5.1 %collective-permute-done.8 = bf16[8,128,128]{2,1,0:T(8,128)(2,1)S(1)} collective-permute-done((bf16[8,128,128]{2,1,0:T(8,128)(2,1)S(1)}, bf16[8,128,128]{2,1,0:T(8,128)(2,1)S(1)}, u32[]{:S(2)}, u32[]{:S(2)}) %collective-permute-start.8) | collective-permute-done | bytes 262176 | tf_op jit(solution)/shard_map/ppermute | solution.py:228
  95.5 2.7 %collective-permute-done.9 = bf16[8,128,128]{2,1,0:T(8,128)(2,1)S(1)} collective-permute-done((bf16[8,128,128]{2,1,0:T(8,128)(2,1)S(1)}, bf16[8,128,128]{2,1,0:T(8,128)(2,1)S(1)}, u32[]{:S(2)}, u32[]{:S(2)}) %collective-permute-start.9) | collective-permute-done | bytes 262176 | tf_op jit(solution)/shard_map/ppermute | solution.py:228
  100.3 2.6 %collective-permute-done.10.other_ref = bf16[4,8,128,128]{3,2,1,0:T(8,128)(2,1)S(1)} collective-permute-done((bf16[4,8,128,128]{3,2,1,0:T(8,128)(2,1)S(1)}, bf16[4,8,128,128]{3,2,1,0:T(8,128)(2,1)S(1)}, u32[]{:S(2)}, u32[]{:S(2)}) %collective-permute-start.10) | collective-permute-done | bytes 1048608 | tf_op jit(solution)/shard_map/ppermute | solution.py:228
  104.4 2.9 %grad_parts.1 = f32[8,448,128]{2,1,0:T(8,128)} custom-call(s32[4]{0:T(128)S(1)} %pad_add_fusion.place_ref, bf16[4,8,128,128]{3,2,1,0:T(8,128)(2,1)S(1)} %pad_maximum_fusion.own_ref, bf16[4,8,128,128]{3,2,1,0:T(8,128)(2,1)S(1)} %collective-permute-done.10.other_ref, bf16[8,2,448,128]{3,2,1,0:T(8,128)(2,1)S(1)} %bitcast.34), custom_call_target="tpu_custom_call" | custom-call | tf_op jit(solution)/shard_map/grad_parts/pallas_call | solution.py:175
  107.3 5.2 %all-to-all-done.1.state_ref = bf16[64,80,128]{2,1,0:T(8,128)(2,1)S(1)} async-done(((bf16[64,80,128]{2,1,0:T(8,128)(2,1)}), bf16[64,80,128]{2,1,0:T(8,128)(2,1)S(1)}, u32[]{:S(2)}, u32[]{:S(2)}) %all-to-all-start.1) | async-done | bytes 1310752 | tf_op jit(solution)/shard_map/all_to_all | solution.py:223
  112.6 2.1 %collective-permute-start.11 = (bf16[56,64,128]{2,1,0:T(8,128)(2,1)S(1)}, bf16[56,64,128]{2,1,0:T(8,128)(2,1)S(1)}, u32[]{:S(2)}, u32[]{:S(2)}) collective-permute-start(bf16[56,64,128]{2,1,0:T(8,128)(2,1)S(1)} %slice.3.own_ref), channel_id=1, source_target_pairs={{0,1},{1,0},{2,3},{3,2},{4,5},{5,4},{6,7},{7,6},{8,9},{9,8},{10,11... | collective-permute-start | bytes 2752520 | tf_op jit(solution)/shard_map/ppermute | solution.py:228
  114.7 2.4 %collective-permute-done.11.other_ref = bf16[56,64,128]{2,1,0:T(8,128)(2,1)S(1)} collective-permute-done((bf16[56,64,128]{2,1,0:T(8,128)(2,1)S(1)}, bf16[56,64,128]{2,1,0:T(8,128)(2,1)S(1)}, u32[]{:S(2)}, u32[]{:S(2)}) %collective-permute-start.11) | collective-permute-done | bytes 917536 | tf_op jit(solution)/shard_map/ppermute | solution.py:228
  119.0 18.5 %all_to_all.20.parts_ref = bf16[4,8,128,128]{3,2,1,0:T(8,128)(2,1)S(1)} all-to-all(bf16[4,8,128,128]{3,2,1,0:T(8,128)(2,1)S(1)} %act_sums.1), channel_id=1, replica_groups=mesh['z'=8,'y'=8,'x'=4,'c'=2] {'x'}, dimensions={0} | all-to-all | bytes 2097152 | tf_op jit(solution)/shard_map/all_to_all | solution.py:223
  138.4 6.1 %all-to-all-start.3 = ((bf16[8,128,128]{2,1,0:T(8,128)(2,1)}), bf16[8,128,128]{2,1,0:T(8,128)(2,1)S(1)}, u32[]{:S(2)}, u32[]{:S(2)}) async-start(bf16[8,128,128]{2,1,0:T(8,128)(2,1)} %act_total.1), calls=%async_computation.3 | async-start | bytes 524288 | tf_op jit(solution)/shard_map/all_to_all | solution.py:223
  144.5 12.5 %reduce-scatter.2.cloned.1.call-done = f32[1,448,128]{2,1,0:T(8,128)} async-done(((f32[8,448,128]{2,1,0:T(8,128)}), f32[1,448,128]{2,1,0:T(8,128)}) %reduce-scatter.2.cloned.1.call-update) | async-done | bytes 229392 | tf_op jit(solution)/shard_map/reduce_scatter | solution.py:243
  (48 shorter events, 17.1 us)
Async XLA Ops:
  7.2 1.1 copy-start.2
  8.3 1.1 copy-start.3
  9.4 1.1 copy-start.4
  11.6 16.4 %copy-start.5 = (bf16[16,8192]{1,0:T(8,128)(2,1)S(1)}, bf16[16,8192]{1,0:T(8,128)(2,1)}, u32[]{:S(2)}) copy-start(bf16[16,8192]{1,0:T(8,128)(2,1)} %act_ref.1) | copy-start | bytes 786436
  11.6 54.7 %copy-start.7 = (s32[25]{0:T(128)S(1)}, s32[25]{0:T(128)}, u32[]{:S(2)}) copy-start(s32[25]{0:T(128)} %offsets_ref.1) | copy-start | bytes 304
  11.6 54.7 %all-to-all-start = ((bf16[64,72,128]{2,1,0:T(8,128)(2,1)}), bf16[64,72,128]{2,1,0:T(8,128)(2,1)S(1)}, u32[]{:S(2)}, u32[]{:S(2)}) async-start(bf16[64,72,128]{2,1,0:T(8,128)(2,1)} %pack.1), calls=%async_computation | async-start | bytes 2359296 | tf_op jit(solution)/shard_map/all_to_all | solution.py:223
  27.2 71.1 %all-gather.3.cloned.1.call-start = ((), (), s32[]{:S(2)}) async-start(), calls=%async_computation.6 | async-start | bytes 1949696 | tf_op jit(solution)/shard_map/all_gather | solution.py:233
  28.7 20.2 %collective-permute-start = (bf16[128,128]{1,0:T(8,128)(2,1)S(1)}, bf16[128,128]{1,0:T(8,128)(2,1)S(1)}, u32[]{:S(2)}, u32[]{:S(2)}) collective-permute-start(bf16[128,128]{1,0:T(8,128)(2,1)S(1)} %get-tuple-element.26), channel_id=1, source_target_pairs={{0,64},{64,128},{128,192},{192,256},{256,320},{320,384},{384,448},... | collective-permute-start | bytes 98312 | tf_op jit(solution)/shard_map/ppermute | solution.py:228
  32.0 26.6 %collective-permute-start.1 = (bf16[128,128]{1,0:T(8,128)(2,1)S(1)}, bf16[128,128]{1,0:T(8,128)(2,1)S(1)}, u32[]{:S(2)}, u32[]{:S(2)}) collective-permute-start(bf16[128,128]{1,0:T(8,128)(2,1)S(1)} %get-tuple-element.27), channel_id=1, source_target_pairs={{0,128},{64,192},{128,256},{192,320},{256,384},{320,448},{384,0},{... | collective-permute-start | bytes 98312 | tf_op jit(solution)/shard_map/ppermute | solution.py:228
  37.6 27.1 %collective-permute-start.2 = (bf16[128,128]{1,0:T(8,128)(2,1)S(1)}, bf16[128,128]{1,0:T(8,128)(2,1)S(1)}, u32[]{:S(2)}, u32[]{:S(2)}) collective-permute-start(bf16[128,128]{1,0:T(8,128)(2,1)S(1)} %get-tuple-element.28), channel_id=1, source_target_pairs={{0,192},{64,256},{128,320},{192,384},{256,448},{320,0},{384,64},{4... | collective-permute-start | bytes 98312 | tf_op jit(solution)/shard_map/ppermute | solution.py:228
  40.3 24.5 %collective-permute-start.3 = (bf16[128,128]{1,0:T(8,128)(2,1)S(1)}, bf16[128,128]{1,0:T(8,128)(2,1)S(1)}, u32[]{:S(2)}, u32[]{:S(2)}) collective-permute-start(bf16[128,128]{1,0:T(8,128)(2,1)S(1)} %get-tuple-element.29), channel_id=1, source_target_pairs={{0,256},{64,320},{128,384},{192,448},{256,0},{320,64},{384,128},{4... | collective-permute-start | bytes 98312 | tf_op jit(solution)/shard_map/ppermute | solution.py:228
  45.2 19.6 %collective-permute-start.4 = (bf16[128,128]{1,0:T(8,128)(2,1)S(1)}, bf16[128,128]{1,0:T(8,128)(2,1)S(1)}, u32[]{:S(2)}, u32[]{:S(2)}) collective-permute-start(bf16[128,128]{1,0:T(8,128)(2,1)S(1)} %get-tuple-element.30), channel_id=1, source_target_pairs={{0,320},{64,384},{128,448},{192,0},{256,64},{320,128},{384,192},{4... | collective-permute-start | bytes 98312 | tf_op jit(solution)/shard_map/ppermute | solution.py:228
  48.9 16.0 %collective-permute-start.5 = (bf16[128,128]{1,0:T(8,128)(2,1)S(1)}, bf16[128,128]{1,0:T(8,128)(2,1)S(1)}, u32[]{:S(2)}, u32[]{:S(2)}) collective-permute-start(bf16[128,128]{1,0:T(8,128)(2,1)S(1)} %get-tuple-element.31), channel_id=1, source_target_pairs={{0,384},{64,448},{128,0},{192,64},{256,128},{320,192},{384,256},{4... | collective-permute-start | bytes 98312 | tf_op jit(solution)/shard_map/ppermute | solution.py:228
  58.6 7.7 %collective-permute-start.6 = (bf16[128,128]{1,0:T(8,128)(2,1)S(1)}, bf16[128,128]{1,0:T(8,128)(2,1)S(1)}, u32[]{:S(2)}, u32[]{:S(2)}) collective-permute-start(bf16[128,128]{1,0:T(8,128)(2,1)S(1)} %get-tuple-element.32), channel_id=1, source_target_pairs={{0,448},{64,0},{128,64},{192,128},{256,192},{320,256},{384,320},{4... | collective-permute-start | bytes 98312 | tf_op jit(solution)/shard_map/ppermute | solution.py:228
  68.3 44.2 %all-to-all-start.1 = ((bf16[64,80,128]{2,1,0:T(8,128)(2,1)}), bf16[64,80,128]{2,1,0:T(8,128)(2,1)S(1)}, u32[]{:S(2)}, u32[]{:S(2)}) async-start(bf16[64,80,128]{2,1,0:T(8,128)(2,1)} %place.1), calls=%async_computation.1 | async-start | bytes 2621440 | tf_op jit(solution)/shard_map/all_to_all | solution.py:223
  79.9 77.1 %reduce-scatter.2.cloned.1.call-start = ((), (), s32[]{:S(2)}) async-start(), calls=%async_computation.5 | async-start | bytes 2064384 | tf_op jit(solution)/shard_map/reduce_scatter | solution.py:243
  79.9 10.5 %collective-permute-start.7 = (bf16[8,128,128]{2,1,0:T(8,128)(2,1)S(1)}, bf16[8,128,128]{2,1,0:T(8,128)(2,1)S(1)}, u32[]{:S(2)}, u32[]{:S(2)}) collective-permute-start(bf16[8,128,128]{2,1,0:T(8,128)(2,1)S(1)} %bitcast_dynamic-update-slice_fusion), channel_id=1, source_target_pairs={{0,2},{2,4},{4,6},{6,0},{1,3},{3,5},{5,7},{7,1},{8,10},{10,12},{12... | collective-permute-start | bytes 786440 | tf_op jit(solution)/shard_map/ppermute | solution.py:228
  83.3 12.2 %collective-permute-start.8 = (bf16[8,128,128]{2,1,0:T(8,128)(2,1)S(1)}, bf16[8,128,128]{2,1,0:T(8,128)(2,1)S(1)}, u32[]{:S(2)}, u32[]{:S(2)}) collective-permute-start(bf16[8,128,128]{2,1,0:T(8,128)(2,1)S(1)} %bitcast_dynamic-update-slice_fusion), channel_id=1, source_target_pairs={{0,4},{2,6},{4,0},{6,2},{1,5},{3,7},{5,1},{7,3},{8,12},{10,14},{12... | collective-permute-start | bytes 786440 | tf_op jit(solution)/shard_map/ppermute | solution.py:228
  86.2 12.0 %collective-permute-start.9 = (bf16[8,128,128]{2,1,0:T(8,128)(2,1)S(1)}, bf16[8,128,128]{2,1,0:T(8,128)(2,1)S(1)}, u32[]{:S(2)}, u32[]{:S(2)}) collective-permute-start(bf16[8,128,128]{2,1,0:T(8,128)(2,1)S(1)} %bitcast_dynamic-update-slice_fusion), channel_id=1, source_target_pairs={{0,6},{2,0},{4,2},{6,4},{1,7},{3,1},{5,3},{7,5},{8,14},{10,8},{12,... | collective-permute-start | bytes 786440 | tf_op jit(solution)/shard_map/ppermute | solution.py:228
  98.3 4.6 %collective-permute-start.10 = (bf16[4,8,128,128]{3,2,1,0:T(8,128)(2,1)S(1)}, bf16[4,8,128,128]{3,2,1,0:T(8,128)(2,1)S(1)}, u32[]{:S(2)}, u32[]{:S(2)}) collective-permute-start(bf16[4,8,128,128]{3,2,1,0:T(8,128)(2,1)S(1)} %pad_maximum_fusion.own_ref), channel_id=1, source_target_pairs={{0,1},{1,0},{2,3},{3,2},{4,5},{5,4},{6,7},{7,6},{8,9},{9,8},{10,11... | collective-permute-start | bytes 3145736 | tf_op jit(solution)/shard_map/ppermute | solution.py:228
  102.9 1.5 copy-start
  112.5 4.6 %copy-start.1 = (bf16[7168,128]{1,0:T(8,128)(2,1)S(1)}, bf16[7168,128]{1,0:T(8,128)(2,1)}, u32[]{:S(2)}) copy-start(bf16[7168,128]{1,0:T(8,128)(2,1)} %all-gather.3.cloned.1.call-done) | copy-start | bytes 5505028
  112.6 4.5 %collective-permute-start.11 = (bf16[56,64,128]{2,1,0:T(8,128)(2,1)S(1)}, bf16[56,64,128]{2,1,0:T(8,128)(2,1)S(1)}, u32[]{:S(2)}, u32[]{:S(2)}) collective-permute-start(bf16[56,64,128]{2,1,0:T(8,128)(2,1)S(1)} %slice.3.own_ref), channel_id=1, source_target_pairs={{0,1},{1,0},{2,3},{3,2},{4,5},{5,4},{6,7},{7,6},{8,9},{9,8},{10,11... | collective-permute-start | bytes 2752520 | tf_op jit(solution)/shard_map/ppermute | solution.py:228
  138.4 21.1 %all-to-all-start.3 = ((bf16[8,128,128]{2,1,0:T(8,128)(2,1)}), bf16[8,128,128]{2,1,0:T(8,128)(2,1)S(1)}, u32[]{:S(2)}, u32[]{:S(2)}) async-start(bf16[8,128,128]{2,1,0:T(8,128)(2,1)} %act_total.1), calls=%async_computation.3 | async-start | bytes 524288 | tf_op jit(solution)/shard_map/all_to_all | solution.py:223
  (1 other events, 0.9 us)
Sparse Core Ops, SparseCore 0:
  30.2 53.0 all-gather.2
  112.6 44.3 reduce-scatter.1

commit v6 on v5

--- a/solution.py
+++ b/solution.py
@@ -31,11 +31,12 @@
 
 
 def pack_kernel(weight_ref, first_ref, second_ref, out_ref):
+    held = [r[...].astype(f32) for r in (weight_ref, first_ref, second_ref)]
     for s in range(STRIPS):
         tiles = [
-            r[s * 8 : s * 8 + 8, q * LANES : (q + 1) * LANES]
+            t[s * 8 : s * 8 + 8, q * LANES : (q + 1) * LANES]
             for q in range(CAP // LANES)
-            for r in (weight_ref, first_ref, second_ref)
+            for t in held
         ]
         out_ref[s] = jnp.concatenate(tiles, axis=0).astype(bf16)
     out_ref[STRIPS:] = jnp.zeros((GROUPS - STRIPS, 72, LANES), bf16)
@@ -231,7 +232,8 @@
 def shards(old_weight, old_first, old_second, old_offsets, activations, upstream):
     here = jnp.stack([lax.axis_index(a) for a in ("z", "y", "x", "c")])
     up = lax.all_gather(upstream.T, ("z", "c"), axis=0).reshape(SIDE, 2, COLS, LANES)
-    got = exchange(pack(old_weight.T, old_first.T, old_second.T), ("z", "y"))
+    halves = [t.T.astype(bf16) for t in (old_weight, old_first, old_second)]
+    got = exchange(pack(*halves), ("z", "y"))
     sent = send_blocks(here, activations)
     act = jnp.stack([sent[0]] + [shift(sent[s], "z", s) for s in range(1, SIDE)])
     got, act = lax.optimization_barrier((got, act))

time: 168 us -> 167 us (level)
  the two profiles are of different devices: /device:TPU:90 before, /device:TPU:26 now
where the time goes in v6:
time: 167 us; the launch traced here: 166 us
  starting transfers between devices  82 us (49%)
  waiting for transfers between devices  34.4 us (21%)
  blocking collectives  18.6 us (11%)
  between operations  14.3 us (9%)
  Pallas kernels  11 us (7%)
  local copies, waits for them, and re-layouts  3.42 us (2%)
  other arithmetic  2.59 us (2%)
    ppermute x12, starting transfers between devices, shift(): return lax.ppermute(x, axis, [(i, (i + by) % n) for i in range(n)])  50.1 us
    all_to_all x3, starting transfers between devices, exchange(): return lax.all_to_all(x, axis, split_axis=0, concat_axis=0, tiled=True)  31.9 us
    all_to_all x1, blocking collectives, exchange(): return lax.all_to_all(x, axis, split_axis=0, concat_axis=0, tiled=True)  18.6 us
    ppermute x12, waiting for transfers between devices, shift(): return lax.ppermute(x, axis, [(i, (i + by) % n) for i in range(n)])  16.6 us
    reduce_scatter x1, waiting for transfers between devices, shards(): grad = lax.psum_scatter(parts, 'y', scatter_dimension=0)  11 us
    all_to_all x3, waiting for transfers between devices, exchange(): return lax.all_to_all(x, axis, split_axis=0, concat_axis=0, tiled=True)  6.12 us
  transfers between devices with their start and end apart: 17, of which 9 were waited for; matrix products, arithmetic and copies ran while one was open for 0% of the time, Pallas kernels for 6%

profile of v6, /device:TPU:26, one launch (start us, length us, event | category | flops | bytes accessed | tf_op | source)
XLA Modules:
  0.0 166.3 jit_solution(8074434053962140420)
XLA Ops:
  10.9 16.5 %all-to-all-start = ((bf16[64,72,128]{2,1,0:T(8,128)(2,1)}), bf16[64,72,128]{2,1,0:T(8,128)(2,1)S(1)}, u32[]{:S(2)}, u32[]{:S(2)}) async-start(bf16[64,72,128]{2,1,0:T(8,128)(2,1)} %pack.1), calls=%async_computation | async-start | bytes 2359296 | tf_op jit(solution)/shard_map/all_to_all | solution.py:224
  28.8 3.4 %collective-permute-start = (bf16[128,128]{1,0:T(8,128)(2,1)S(1)}, bf16[128,128]{1,0:T(8,128)(2,1)S(1)}, u32[]{:S(2)}, u32[]{:S(2)}) collective-permute-start(bf16[128,128]{1,0:T(8,128)(2,1)S(1)} %get-tuple-element.26), channel_id=1, source_target_pairs={{0,64},{64,128},{128,192},{192,256},{256,320},{320,384},{384,448},... | collective-permute-start | bytes 98312 | tf_op jit(solution)/shard_map/ppermute | solution.py:229
  32.2 4.3 %collective-permute-start.1 = (bf16[128,128]{1,0:T(8,128)(2,1)S(1)}, bf16[128,128]{1,0:T(8,128)(2,1)S(1)}, u32[]{:S(2)}, u32[]{:S(2)}) collective-permute-start(bf16[128,128]{1,0:T(8,128)(2,1)S(1)} %get-tuple-element.27), channel_id=1, source_target_pairs={{0,128},{64,192},{128,256},{192,320},{256,384},{320,448},{384,0},{... | collective-permute-start | bytes 98312 | tf_op jit(solution)/shard_map/ppermute | solution.py:229
  36.5 4.7 %collective-permute-start.2 = (bf16[128,128]{1,0:T(8,128)(2,1)S(1)}, bf16[128,128]{1,0:T(8,128)(2,1)S(1)}, u32[]{:S(2)}, u32[]{:S(2)}) collective-permute-start(bf16[128,128]{1,0:T(8,128)(2,1)S(1)} %get-tuple-element.28), channel_id=1, source_target_pairs={{0,192},{64,256},{128,320},{192,384},{256,448},{320,0},{384,64},{4... | collective-permute-start | bytes 98312 | tf_op jit(solution)/shard_map/ppermute | solution.py:229
  41.3 4.1 %collective-permute-start.3 = (bf16[128,128]{1,0:T(8,128)(2,1)S(1)}, bf16[128,128]{1,0:T(8,128)(2,1)S(1)}, u32[]{:S(2)}, u32[]{:S(2)}) collective-permute-start(bf16[128,128]{1,0:T(8,128)(2,1)S(1)} %get-tuple-element.29), channel_id=1, source_target_pairs={{0,256},{64,320},{128,384},{192,448},{256,0},{320,64},{384,128},{4... | collective-permute-start | bytes 98312 | tf_op jit(solution)/shard_map/ppermute | solution.py:229
  45.3 4.9 %collective-permute-start.4 = (bf16[128,128]{1,0:T(8,128)(2,1)S(1)}, bf16[128,128]{1,0:T(8,128)(2,1)S(1)}, u32[]{:S(2)}, u32[]{:S(2)}) collective-permute-start(bf16[128,128]{1,0:T(8,128)(2,1)S(1)} %get-tuple-element.30), channel_id=1, source_target_pairs={{0,320},{64,384},{128,448},{192,0},{256,64},{320,128},{384,192},{4... | collective-permute-start | bytes 98312 | tf_op jit(solution)/shard_map/ppermute | solution.py:229
  50.6 11.8 %collective-permute-start.5 = (bf16[128,128]{1,0:T(8,128)(2,1)S(1)}, bf16[128,128]{1,0:T(8,128)(2,1)S(1)}, u32[]{:S(2)}, u32[]{:S(2)}) collective-permute-start(bf16[128,128]{1,0:T(8,128)(2,1)S(1)} %get-tuple-element.31), channel_id=1, source_target_pairs={{0,384},{64,448},{128,0},{192,64},{256,128},{320,192},{384,256},{4... | collective-permute-start | bytes 98312 | tf_op jit(solution)/shard_map/ppermute | solution.py:229
  62.4 2.4 %collective-permute-start.6 = (bf16[128,128]{1,0:T(8,128)(2,1)S(1)}, bf16[128,128]{1,0:T(8,128)(2,1)S(1)}, u32[]{:S(2)}, u32[]{:S(2)}) collective-permute-start(bf16[128,128]{1,0:T(8,128)(2,1)S(1)} %get-tuple-element.32), channel_id=1, source_target_pairs={{0,448},{64,0},{128,64},{192,128},{256,192},{320,256},{384,320},{4... | collective-permute-start | bytes 98312 | tf_op jit(solution)/shard_map/ppermute | solution.py:229
  66.3 2.1 %collective-permute-done.6 = bf16[128,128]{1,0:T(8,128)(2,1)S(1)} collective-permute-done((bf16[128,128]{1,0:T(8,128)(2,1)S(1)}, bf16[128,128]{1,0:T(8,128)(2,1)S(1)}, u32[]{:S(2)}, u32[]{:S(2)}) %collective-permute-start.6) | collective-permute-done | bytes 32800 | tf_op jit(solution)/shard_map/ppermute | solution.py:229
  68.4 1.9 %place.1 = bf16[64,80,128]{2,1,0:T(8,128)(2,1)} custom-call(s32[25]{0:T(128)S(1)} %copy-done.4, bf16[64,72,128]{2,1,0:T(8,128)(2,1)S(1)} %all-to-all-done.slots_ref), custom_call_target="tpu_custom_call" | custom-call | tf_op jit(solution)/shard_map/place/pallas_call | solution.py:75
  70.4 9.7 %all-to-all-start.1 = ((bf16[64,80,128]{2,1,0:T(8,128)(2,1)}), bf16[64,80,128]{2,1,0:T(8,128)(2,1)S(1)}, u32[]{:S(2)}, u32[]{:S(2)}) async-start(bf16[64,80,128]{2,1,0:T(8,128)(2,1)} %place.1), calls=%async_computation.1 | async-start | bytes 2621440 | tf_op jit(solution)/shard_map/all_to_all | solution.py:224
  80.1 3.4 %collective-permute-start.7 = (bf16[8,128,128]{2,1,0:T(8,128)(2,1)S(1)}, bf16[8,128,128]{2,1,0:T(8,128)(2,1)S(1)}, u32[]{:S(2)}, u32[]{:S(2)}) collective-permute-start(bf16[8,128,128]{2,1,0:T(8,128)(2,1)S(1)} %bitcast_dynamic-update-slice_fusion), channel_id=1, source_target_pairs={{0,2},{2,4},{4,6},{6,0},{1,3},{3,5},{5,7},{7,1},{8,10},{10,12},{12... | collective-permute-start | bytes 786440 | tf_op jit(solution)/shard_map/ppermute | solution.py:229
  83.5 2.9 %collective-permute-start.8 = (bf16[8,128,128]{2,1,0:T(8,128)(2,1)S(1)}, bf16[8,128,128]{2,1,0:T(8,128)(2,1)S(1)}, u32[]{:S(2)}, u32[]{:S(2)}) collective-permute-start(bf16[8,128,128]{2,1,0:T(8,128)(2,1)S(1)} %bitcast_dynamic-update-slice_fusion), channel_id=1, source_target_pairs={{0,4},{2,6},{4,0},{6,2},{1,5},{3,7},{5,1},{7,3},{8,12},{10,14},{12... | collective-permute-start | bytes 786440 | tf_op jit(solution)/shard_map/ppermute | solution.py:229
  86.4 4.2 %collective-permute-start.9 = (bf16[8,128,128]{2,1,0:T(8,128)(2,1)S(1)}, bf16[8,128,128]{2,1,0:T(8,128)(2,1)S(1)}, u32[]{:S(2)}, u32[]{:S(2)}) collective-permute-start(bf16[8,128,128]{2,1,0:T(8,128)(2,1)S(1)} %bitcast_dynamic-update-slice_fusion), channel_id=1, source_target_pairs={{0,6},{2,0},{4,2},{6,4},{1,7},{3,1},{5,3},{7,5},{8,14},{10,8},{12,... | collective-permute-start | bytes 786440 | tf_op jit(solution)/shard_map/ppermute | solution.py:229
  90.6 5.1 %collective-permute-done.8 = bf16[8,128,128]{2,1,0:T(8,128)(2,1)S(1)} collective-permute-done((bf16[8,128,128]{2,1,0:T(8,128)(2,1)S(1)}, bf16[8,128,128]{2,1,0:T(8,128)(2,1)S(1)}, u32[]{:S(2)}, u32[]{:S(2)}) %collective-permute-start.8) | collective-permute-done | bytes 262176 | tf_op jit(solution)/shard_map/ppermute | solution.py:229
  95.6 2.7 %collective-permute-done.9 = bf16[8,128,128]{2,1,0:T(8,128)(2,1)S(1)} collective-permute-done((bf16[8,128,128]{2,1,0:T(8,128)(2,1)S(1)}, bf16[8,128,128]{2,1,0:T(8,128)(2,1)S(1)}, u32[]{:S(2)}, u32[]{:S(2)}) %collective-permute-start.9) | collective-permute-done | bytes 262176 | tf_op jit(solution)/shard_map/ppermute | solution.py:229
  100.4 2.6 %collective-permute-done.10.other_ref = bf16[4,8,128,128]{3,2,1,0:T(8,128)(2,1)S(1)} collective-permute-done((bf16[4,8,128,128]{3,2,1,0:T(8,128)(2,1)S(1)}, bf16[4,8,128,128]{3,2,1,0:T(8,128)(2,1)S(1)}, u32[]{:S(2)}, u32[]{:S(2)}) %collective-permute-start.10) | collective-permute-done | bytes 1048608 | tf_op jit(solution)/shard_map/ppermute | solution.py:229
  104.5 2.9 %grad_parts.1 = f32[8,448,128]{2,1,0:T(8,128)} custom-call(s32[4]{0:T(128)S(1)} %pad_add_fusion.place_ref, bf16[4,8,128,128]{3,2,1,0:T(8,128)(2,1)S(1)} %pad_maximum_fusion.own_ref, bf16[4,8,128,128]{3,2,1,0:T(8,128)(2,1)S(1)} %collective-permute-done.10.other_ref, bf16[8,2,448,128]{3,2,1,0:T(8,128)(2,1)S(1)} %bitcast.37), custom_call_target="tpu_custom_call" | custom-call | tf_op jit(solution)/shard_map/grad_parts/pallas_call | solution.py:176
  107.5 6.1 %all-to-all-done.1.state_ref = bf16[64,80,128]{2,1,0:T(8,128)(2,1)S(1)} async-done(((bf16[64,80,128]{2,1,0:T(8,128)(2,1)}), bf16[64,80,128]{2,1,0:T(8,128)(2,1)S(1)}, u32[]{:S(2)}, u32[]{:S(2)}) %all-to-all-start.1) | async-done | bytes 1310752 | tf_op jit(solution)/shard_map/all_to_all | solution.py:224
  113.7 2.1 %collective-permute-start.11 = (bf16[56,64,128]{2,1,0:T(8,128)(2,1)S(1)}, bf16[56,64,128]{2,1,0:T(8,128)(2,1)S(1)}, u32[]{:S(2)}, u32[]{:S(2)}) collective-permute-start(bf16[56,64,128]{2,1,0:T(8,128)(2,1)S(1)} %slice.3.own_ref), channel_id=1, source_target_pairs={{0,1},{1,0},{2,3},{3,2},{4,5},{5,4},{6,7},{7,6},{8,9},{9,8},{10,11... | collective-permute-start | bytes 2752520 | tf_op jit(solution)/shard_map/ppermute | solution.py:229
  115.8 2.4 %collective-permute-done.11.other_ref = bf16[56,64,128]{2,1,0:T(8,128)(2,1)S(1)} collective-permute-done((bf16[56,64,128]{2,1,0:T(8,128)(2,1)S(1)}, bf16[56,64,128]{2,1,0:T(8,128)(2,1)S(1)}, u32[]{:S(2)}, u32[]{:S(2)}) %collective-permute-start.11) | collective-permute-done | bytes 917536 | tf_op jit(solution)/shard_map/ppermute | solution.py:229
  120.1 18.6 %all_to_all.20.parts_ref = bf16[4,8,128,128]{3,2,1,0:T(8,128)(2,1)S(1)} all-to-all(bf16[4,8,128,128]{3,2,1,0:T(8,128)(2,1)S(1)} %act_sums.1), channel_id=1, replica_groups=mesh['z'=8,'y'=8,'x'=4,'c'=2] {'x'}, dimensions={0} | all-to-all | bytes 2097152 | tf_op jit(solution)/shard_map/all_to_all | solution.py:224
  139.5 5.7 %all-to-all-start.3 = ((bf16[8,128,128]{2,1,0:T(8,128)(2,1)}), bf16[8,128,128]{2,1,0:T(8,128)(2,1)S(1)}, u32[]{:S(2)}, u32[]{:S(2)}) async-start(bf16[8,128,128]{2,1,0:T(8,128)(2,1)} %act_total.1), calls=%async_computation.3 | async-start | bytes 524288 | tf_op jit(solution)/shard_map/all_to_all | solution.py:224
  145.3 11.0 %reduce-scatter.2.cloned.1.call-done = f32[1,448,128]{2,1,0:T(8,128)} async-done(((f32[8,448,128]{2,1,0:T(8,128)}), f32[1,448,128]{2,1,0:T(8,128)}) %reduce-scatter.2.cloned.1.call-update) | async-done | bytes 229392 | tf_op jit(solution)/shard_map/reduce_scatter | solution.py:245
  (46 shorter events, 16.6 us)
Async XLA Ops:
  7.2 1.3 copy-start.5
  10.8 17.3 %copy-start.2 = (bf16[16,8192]{1,0:T(8,128)(2,1)S(1)}, bf16[16,8192]{1,0:T(8,128)(2,1)}, u32[]{:S(2)}) copy-start(bf16[16,8192]{1,0:T(8,128)(2,1)} %act_ref.1) | copy-start | bytes 786436
  10.9 57.5 %copy-start.4 = (s32[25]{0:T(128)S(1)}, s32[25]{0:T(128)}, u32[]{:S(2)}) copy-start(s32[25]{0:T(128)} %offsets_ref.1) | copy-start | bytes 304
  10.9 57.5 %all-to-all-start = ((bf16[64,72,128]{2,1,0:T(8,128)(2,1)}), bf16[64,72,128]{2,1,0:T(8,128)(2,1)S(1)}, u32[]{:S(2)}, u32[]{:S(2)}) async-start(bf16[64,72,128]{2,1,0:T(8,128)(2,1)} %pack.1), calls=%async_computation | async-start | bytes 2359296 | tf_op jit(solution)/shard_map/all_to_all | solution.py:224
  27.3 71.1 %all-gather.3.cloned.1.call-start = ((), (), s32[]{:S(2)}) async-start(), calls=%async_computation.6 | async-start | bytes 1949696 | tf_op jit(solution)/shard_map/all_gather | solution.py:234
  28.8 21.8 %collective-permute-start = (bf16[128,128]{1,0:T(8,128)(2,1)S(1)}, bf16[128,128]{1,0:T(8,128)(2,1)S(1)}, u32[]{:S(2)}, u32[]{:S(2)}) collective-permute-start(bf16[128,128]{1,0:T(8,128)(2,1)S(1)} %get-tuple-element.26), channel_id=1, source_target_pairs={{0,64},{64,128},{128,192},{192,256},{256,320},{320,384},{384,448},... | collective-permute-start | bytes 98312 | tf_op jit(solution)/shard_map/ppermute | solution.py:229
  32.2 30.2 %collective-permute-start.1 = (bf16[128,128]{1,0:T(8,128)(2,1)S(1)}, bf16[128,128]{1,0:T(8,128)(2,1)S(1)}, u32[]{:S(2)}, u32[]{:S(2)}) collective-permute-start(bf16[128,128]{1,0:T(8,128)(2,1)S(1)} %get-tuple-element.27), channel_id=1, source_target_pairs={{0,128},{64,192},{128,256},{192,320},{256,384},{320,448},{384,0},{... | collective-permute-start | bytes 98312 | tf_op jit(solution)/shard_map/ppermute | solution.py:229
  36.5 28.4 %collective-permute-start.2 = (bf16[128,128]{1,0:T(8,128)(2,1)S(1)}, bf16[128,128]{1,0:T(8,128)(2,1)S(1)}, u32[]{:S(2)}, u32[]{:S(2)}) collective-permute-start(bf16[128,128]{1,0:T(8,128)(2,1)S(1)} %get-tuple-element.28), channel_id=1, source_target_pairs={{0,192},{64,256},{128,320},{192,384},{256,448},{320,0},{384,64},{4... | collective-permute-start | bytes 98312 | tf_op jit(solution)/shard_map/ppermute | solution.py:229
  41.3 25.0 %collective-permute-start.3 = (bf16[128,128]{1,0:T(8,128)(2,1)S(1)}, bf16[128,128]{1,0:T(8,128)(2,1)S(1)}, u32[]{:S(2)}, u32[]{:S(2)}) collective-permute-start(bf16[128,128]{1,0:T(8,128)(2,1)S(1)} %get-tuple-element.29), channel_id=1, source_target_pairs={{0,256},{64,320},{128,384},{192,448},{256,0},{320,64},{384,128},{4... | collective-permute-start | bytes 98312 | tf_op jit(solution)/shard_map/ppermute | solution.py:229
  45.3 20.9 %collective-permute-start.4 = (bf16[128,128]{1,0:T(8,128)(2,1)S(1)}, bf16[128,128]{1,0:T(8,128)(2,1)S(1)}, u32[]{:S(2)}, u32[]{:S(2)}) collective-permute-start(bf16[128,128]{1,0:T(8,128)(2,1)S(1)} %get-tuple-element.30), channel_id=1, source_target_pairs={{0,320},{64,384},{128,448},{192,0},{256,64},{320,128},{384,192},{4... | collective-permute-start | bytes 98312 | tf_op jit(solution)/shard_map/ppermute | solution.py:229
  50.6 15.7 %collective-permute-start.5 = (bf16[128,128]{1,0:T(8,128)(2,1)S(1)}, bf16[128,128]{1,0:T(8,128)(2,1)S(1)}, u32[]{:S(2)}, u32[]{:S(2)}) collective-permute-start(bf16[128,128]{1,0:T(8,128)(2,1)S(1)} %get-tuple-element.31), channel_id=1, source_target_pairs={{0,384},{64,448},{128,0},{192,64},{256,128},{320,192},{384,256},{4... | collective-permute-start | bytes 98312 | tf_op jit(solution)/shard_map/ppermute | solution.py:229
  62.4 6.0 %collective-permute-start.6 = (bf16[128,128]{1,0:T(8,128)(2,1)S(1)}, bf16[128,128]{1,0:T(8,128)(2,1)S(1)}, u32[]{:S(2)}, u32[]{:S(2)}) collective-permute-start(bf16[128,128]{1,0:T(8,128)(2,1)S(1)} %get-tuple-element.32), channel_id=1, source_target_pairs={{0,448},{64,0},{128,64},{192,128},{256,192},{320,256},{384,320},{4... | collective-permute-start | bytes 98312 | tf_op jit(solution)/shard_map/ppermute | solution.py:229
  70.4 43.2 %all-to-all-start.1 = ((bf16[64,80,128]{2,1,0:T(8,128)(2,1)}), bf16[64,80,128]{2,1,0:T(8,128)(2,1)S(1)}, u32[]{:S(2)}, u32[]{:S(2)}) async-start(bf16[64,80,128]{2,1,0:T(8,128)(2,1)} %place.1), calls=%async_computation.1 | async-start | bytes 2621440 | tf_op jit(solution)/shard_map/all_to_all | solution.py:224
  80.0 76.2 %reduce-scatter.2.cloned.1.call-start = ((), (), s32[]{:S(2)}) async-start(), calls=%async_computation.5 | async-start | bytes 2064384 | tf_op jit(solution)/shard_map/reduce_scatter | solution.py:245
  80.1 10.5 %collective-permute-start.7 = (bf16[8,128,128]{2,1,0:T(8,128)(2,1)S(1)}, bf16[8,128,128]{2,1,0:T(8,128)(2,1)S(1)}, u32[]{:S(2)}, u32[]{:S(2)}) collective-permute-start(bf16[8,128,128]{2,1,0:T(8,128)(2,1)S(1)} %bitcast_dynamic-update-slice_fusion), channel_id=1, source_target_pairs={{0,2},{2,4},{4,6},{6,0},{1,3},{3,5},{5,7},{7,1},{8,10},{10,12},{12... | collective-permute-start | bytes 786440 | tf_op jit(solution)/shard_map/ppermute | solution.py:229
  83.5 12.2 %collective-permute-start.8 = (bf16[8,128,128]{2,1,0:T(8,128)(2,1)S(1)}, bf16[8,128,128]{2,1,0:T(8,128)(2,1)S(1)}, u32[]{:S(2)}, u32[]{:S(2)}) collective-permute-start(bf16[8,128,128]{2,1,0:T(8,128)(2,1)S(1)} %bitcast_dynamic-update-slice_fusion), channel_id=1, source_target_pairs={{0,4},{2,6},{4,0},{6,2},{1,5},{3,7},{5,1},{7,3},{8,12},{10,14},{12... | collective-permute-start | bytes 786440 | tf_op jit(solution)/shard_map/ppermute | solution.py:229
  86.4 12.0 %collective-permute-start.9 = (bf16[8,128,128]{2,1,0:T(8,128)(2,1)S(1)}, bf16[8,128,128]{2,1,0:T(8,128)(2,1)S(1)}, u32[]{:S(2)}, u32[]{:S(2)}) collective-permute-start(bf16[8,128,128]{2,1,0:T(8,128)(2,1)S(1)} %bitcast_dynamic-update-slice_fusion), channel_id=1, source_target_pairs={{0,6},{2,0},{4,2},{6,4},{1,7},{3,1},{5,3},{7,5},{8,14},{10,8},{12,... | collective-permute-start | bytes 786440 | tf_op jit(solution)/shard_map/ppermute | solution.py:229
  98.5 4.6 %collective-permute-start.10 = (bf16[4,8,128,128]{3,2,1,0:T(8,128)(2,1)S(1)}, bf16[4,8,128,128]{3,2,1,0:T(8,128)(2,1)S(1)}, u32[]{:S(2)}, u32[]{:S(2)}) collective-permute-start(bf16[4,8,128,128]{3,2,1,0:T(8,128)(2,1)S(1)} %pad_maximum_fusion.own_ref), channel_id=1, source_target_pairs={{0,1},{1,0},{2,3},{3,2},{4,5},{5,4},{6,7},{7,6},{8,9},{9,8},{10,11... | collective-permute-start | bytes 3145736 | tf_op jit(solution)/shard_map/ppermute | solution.py:229
  103.0 1.5 copy-start
  113.6 4.6 %copy-start.1 = (bf16[7168,128]{1,0:T(8,128)(2,1)S(1)}, bf16[7168,128]{1,0:T(8,128)(2,1)}, u32[]{:S(2)}) copy-start(bf16[7168,128]{1,0:T(8,128)(2,1)} %all-gather.3.cloned.1.call-done) | copy-start | bytes 5505028
  113.7 4.5 %collective-permute-start.11 = (bf16[56,64,128]{2,1,0:T(8,128)(2,1)S(1)}, bf16[56,64,128]{2,1,0:T(8,128)(2,1)S(1)}, u32[]{:S(2)}, u32[]{:S(2)}) collective-permute-start(bf16[56,64,128]{2,1,0:T(8,128)(2,1)S(1)} %slice.3.own_ref), channel_id=1, source_target_pairs={{0,1},{1,0},{2,3},{3,2},{4,5},{5,4},{6,7},{7,6},{8,9},{9,8},{10,11... | collective-permute-start | bytes 2752520 | tf_op jit(solution)/shard_map/ppermute | solution.py:229
  139.5 19.2 %all-to-all-start.3 = ((bf16[8,128,128]{2,1,0:T(8,128)(2,1)}), bf16[8,128,128]{2,1,0:T(8,128)(2,1)S(1)}, u32[]{:S(2)}, u32[]{:S(2)}) async-start(bf16[8,128,128]{2,1,0:T(8,128)(2,1)} %act_total.1), calls=%async_computation.3 | async-start | bytes 524288 | tf_op jit(solution)/shard_map/all_to_all | solution.py:224
  156.2 0.9 copy-start.3
Sparse Core Ops, SparseCore 0:
  30.3 57.3 all-gather.2
  113.7 42.4 reduce-scatter.1

commit v7 on v6

--- a/solution.py
+++ b/solution.py
@@ -52,17 +52,16 @@
 
 
 def place_kernel(offsets_ref, slots_ref, out_ref, rows_ref):
-    lane = lax.broadcasted_iota(jnp.int32, (3, 24, LANES), 2)
+    lane = lax.broadcasted_iota(jnp.int32, (24, LANES), 1)
     for k in range(SHARDS):
         begin = offsets_ref[k]
         block = begin // LANES
         shift = begin % LANES
-        slots = slots_ref[k].astype(f32)
-        turned = pltpu.roll(slots, shift, 1).reshape(3, 24, LANES)
-        here = pl.ds(block, 3)
-        rows_ref[here] = jnp.where(lane >= shift, turned, rows_ref[here])
-        after = pl.ds(block + 1, 3)
-        rows_ref[after] = jnp.where(lane < shift, turned, rows_ref[after])
+        turned = pltpu.roll(slots_ref[k].astype(f32), shift, 1).reshape(3, 24, LANES)
+        rows_ref[block] = jnp.where(lane >= shift, turned[0], rows_ref[block])
+        rows_ref[block + 1] = jnp.where(lane >= shift, turned[1], turned[0])
+        rows_ref[block + 2] = jnp.where(lane >= shift, turned[2], turned[1])
+        rows_ref[block + 3] = turned[2]
     for z in range(SIDE):
         rows = rows_ref[z * SIDE : (z + 1) * SIDE]
         weights = rows[:, :8].reshape(64, LANES).astype(bf16)

time: 167 us -> 167 us (level)
  the two profiles are of different devices: /device:TPU:26 before, /device:TPU:30 now
where the time goes in v7:
time: 167 us; the launch traced here: 166 us
  starting transfers between devices  80.1 us (48%)
  waiting for transfers between devices  37 us (22%)
  blocking collectives  17.9 us (11%)
  between operations  14.3 us (9%)
  Pallas kernels  11 us (7%)
  local copies, waits for them, and re-layouts  3.42 us (2%)
  other arithmetic  2.59 us (2%)
    ppermute x12, starting transfers between devices, shift(): return lax.ppermute(x, axis, [(i, (i + by) % n) for i in range(n)])  48.2 us
    all_to_all x3, starting transfers between devices, exchange(): return lax.all_to_all(x, axis, split_axis=0, concat_axis=0, tiled=True)  31.8 us
    all_to_all x1, blocking collectives, exchange(): return lax.all_to_all(x, axis, split_axis=0, concat_axis=0, tiled=True)  17.9 us
    ppermute x12, waiting for transfers between devices, shift(): return lax.ppermute(x, axis, [(i, (i + by) % n) for i in range(n)])  17.9 us
    reduce_scatter x1, waiting for transfers between devices, shards(): grad = lax.psum_scatter(parts, 'y', scatter_dimension=0)  11.7 us
    all_to_all x3, waiting for transfers between devices, exchange(): return lax.all_to_all(x, axis, split_axis=0, concat_axis=0, tiled=True)  6.7 us
  transfers between devices with their start and end apart: 17, of which 10 were waited for; matrix products, arithmetic and copies ran while one was open for 0% of the time, Pallas kernels for 6%

profile of v7, /device:TPU:30, one launch (start us, length us, event | category | flops | bytes accessed | tf_op | source)
XLA Modules:
  0.0 166.4 jit_solution(4955143930433731435)
XLA Ops:
  10.9 16.5 %all-to-all-start = ((bf16[64,72,128]{2,1,0:T(8,128)(2,1)}), bf16[64,72,128]{2,1,0:T(8,128)(2,1)S(1)}, u32[]{:S(2)}, u32[]{:S(2)}) async-start(bf16[64,72,128]{2,1,0:T(8,128)(2,1)} %pack.1), calls=%async_computation | async-start | bytes 2359296 | tf_op jit(solution)/shard_map/all_to_all | solution.py:223
  28.8 3.4 %collective-permute-start = (bf16[128,128]{1,0:T(8,128)(2,1)S(1)}, bf16[128,128]{1,0:T(8,128)(2,1)S(1)}, u32[]{:S(2)}, u32[]{:S(2)}) collective-permute-start(bf16[128,128]{1,0:T(8,128)(2,1)S(1)} %get-tuple-element.26), channel_id=1, source_target_pairs={{0,64},{64,128},{128,192},{192,256},{256,320},{320,384},{384,448},... | collective-permute-start | bytes 98312 | tf_op jit(solution)/shard_map/ppermute | solution.py:228
  32.2 4.3 %collective-permute-start.1 = (bf16[128,128]{1,0:T(8,128)(2,1)S(1)}, bf16[128,128]{1,0:T(8,128)(2,1)S(1)}, u32[]{:S(2)}, u32[]{:S(2)}) collective-permute-start(bf16[128,128]{1,0:T(8,128)(2,1)S(1)} %get-tuple-element.27), channel_id=1, source_target_pairs={{0,128},{64,192},{128,256},{192,320},{256,384},{320,448},{384,0},{... | collective-permute-start | bytes 98312 | tf_op jit(solution)/shard_map/ppermute | solution.py:228
  36.5 4.7 %collective-permute-start.2 = (bf16[128,128]{1,0:T(8,128)(2,1)S(1)}, bf16[128,128]{1,0:T(8,128)(2,1)S(1)}, u32[]{:S(2)}, u32[]{:S(2)}) collective-permute-start(bf16[128,128]{1,0:T(8,128)(2,1)S(1)} %get-tuple-element.28), channel_id=1, source_target_pairs={{0,192},{64,256},{128,320},{192,384},{256,448},{320,0},{384,64},{4... | collective-permute-start | bytes 98312 | tf_op jit(solution)/shard_map/ppermute | solution.py:228
  41.3 4.1 %collective-permute-start.3 = (bf16[128,128]{1,0:T(8,128)(2,1)S(1)}, bf16[128,128]{1,0:T(8,128)(2,1)S(1)}, u32[]{:S(2)}, u32[]{:S(2)}) collective-permute-start(bf16[128,128]{1,0:T(8,128)(2,1)S(1)} %get-tuple-element.29), channel_id=1, source_target_pairs={{0,256},{64,320},{128,384},{192,448},{256,0},{320,64},{384,128},{4... | collective-permute-start | bytes 98312 | tf_op jit(solution)/shard_map/ppermute | solution.py:228
  45.3 4.9 %collective-permute-start.4 = (bf16[128,128]{1,0:T(8,128)(2,1)S(1)}, bf16[128,128]{1,0:T(8,128)(2,1)S(1)}, u32[]{:S(2)}, u32[]{:S(2)}) collective-permute-start(bf16[128,128]{1,0:T(8,128)(2,1)S(1)} %get-tuple-element.30), channel_id=1, source_target_pairs={{0,320},{64,384},{128,448},{192,0},{256,64},{320,128},{384,192},{4... | collective-permute-start | bytes 98312 | tf_op jit(solution)/shard_map/ppermute | solution.py:228
  50.6 11.8 %collective-permute-start.5 = (bf16[128,128]{1,0:T(8,128)(2,1)S(1)}, bf16[128,128]{1,0:T(8,128)(2,1)S(1)}, u32[]{:S(2)}, u32[]{:S(2)}) collective-permute-start(bf16[128,128]{1,0:T(8,128)(2,1)S(1)} %get-tuple-element.31), channel_id=1, source_target_pairs={{0,384},{64,448},{128,0},{192,64},{256,128},{320,192},{384,256},{4... | collective-permute-start | bytes 98312 | tf_op jit(solution)/shard_map/ppermute | solution.py:228
  62.5 2.5 %collective-permute-start.6 = (bf16[128,128]{1,0:T(8,128)(2,1)S(1)}, bf16[128,128]{1,0:T(8,128)(2,1)S(1)}, u32[]{:S(2)}, u32[]{:S(2)}) collective-permute-start(bf16[128,128]{1,0:T(8,128)(2,1)S(1)} %get-tuple-element.32), channel_id=1, source_target_pairs={{0,448},{64,0},{128,64},{192,128},{256,192},{320,256},{384,320},{4... | collective-permute-start | bytes 98312 | tf_op jit(solution)/shard_map/ppermute | solution.py:228
  66.3 2.1 %collective-permute-done.6 = bf16[128,128]{1,0:T(8,128)(2,1)S(1)} collective-permute-done((bf16[128,128]{1,0:T(8,128)(2,1)S(1)}, bf16[128,128]{1,0:T(8,128)(2,1)S(1)}, u32[]{:S(2)}, u32[]{:S(2)}) %collective-permute-start.6) | collective-permute-done | bytes 32800 | tf_op jit(solution)/shard_map/ppermute | solution.py:228
  68.4 1.9 %place.1 = bf16[64,80,128]{2,1,0:T(8,128)(2,1)} custom-call(s32[25]{0:T(128)S(1)} %copy-done.4, bf16[64,72,128]{2,1,0:T(8,128)(2,1)S(1)} %all-to-all-done.slots_ref), custom_call_target="tpu_custom_call" | custom-call | tf_op jit(solution)/shard_map/place/pallas_call | solution.py:74
  70.4 9.6 %all-to-all-start.1 = ((bf16[64,80,128]{2,1,0:T(8,128)(2,1)}), bf16[64,80,128]{2,1,0:T(8,128)(2,1)S(1)}, u32[]{:S(2)}, u32[]{:S(2)}) async-start(bf16[64,80,128]{2,1,0:T(8,128)(2,1)} %place.1), calls=%async_computation.1 | async-start | bytes 2621440 | tf_op jit(solution)/shard_map/all_to_all | solution.py:223
  80.1 2.3 %collective-permute-start.7 = (bf16[8,128,128]{2,1,0:T(8,128)(2,1)S(1)}, bf16[8,128,128]{2,1,0:T(8,128)(2,1)S(1)}, u32[]{:S(2)}, u32[]{:S(2)}) collective-permute-start(bf16[8,128,128]{2,1,0:T(8,128)(2,1)S(1)} %bitcast_dynamic-update-slice_fusion), channel_id=1, source_target_pairs={{0,2},{2,4},{4,6},{6,0},{1,3},{3,5},{5,7},{7,1},{8,10},{10,12},{12... | collective-permute-start | bytes 786440 | tf_op jit(solution)/shard_map/ppermute | solution.py:228
  82.3 4.5 %collective-permute-start.8 = (bf16[8,128,128]{2,1,0:T(8,128)(2,1)S(1)}, bf16[8,128,128]{2,1,0:T(8,128)(2,1)S(1)}, u32[]{:S(2)}, u32[]{:S(2)}) collective-permute-start(bf16[8,128,128]{2,1,0:T(8,128)(2,1)S(1)} %bitcast_dynamic-update-slice_fusion), channel_id=1, source_target_pairs={{0,4},{2,6},{4,0},{6,2},{1,5},{3,7},{5,1},{7,3},{8,12},{10,14},{12... | collective-permute-start | bytes 786440 | tf_op jit(solution)/shard_map/ppermute | solution.py:228
  88.7 2.1 %collective-permute-done.7 = bf16[8,128,128]{2,1,0:T(8,128)(2,1)S(1)} collective-permute-done((bf16[8,128,128]{2,1,0:T(8,128)(2,1)S(1)}, bf16[8,128,128]{2,1,0:T(8,128)(2,1)S(1)}, u32[]{:S(2)}, u32[]{:S(2)}) %collective-permute-start.7) | collective-permute-done | bytes 262176 | tf_op jit(solution)/shard_map/ppermute | solution.py:228
  90.9 3.5 %collective-permute-done.8 = bf16[8,128,128]{2,1,0:T(8,128)(2,1)S(1)} collective-permute-done((bf16[8,128,128]{2,1,0:T(8,128)(2,1)S(1)}, bf16[8,128,128]{2,1,0:T(8,128)(2,1)S(1)}, u32[]{:S(2)}, u32[]{:S(2)}) %collective-permute-start.8) | collective-permute-done | bytes 262176 | tf_op jit(solution)/shard_map/ppermute | solution.py:228
  94.4 3.3 %collective-permute-done.9 = bf16[8,128,128]{2,1,0:T(8,128)(2,1)S(1)} collective-permute-done((bf16[8,128,128]{2,1,0:T(8,128)(2,1)S(1)}, bf16[8,128,128]{2,1,0:T(8,128)(2,1)S(1)}, u32[]{:S(2)}, u32[]{:S(2)}) %collective-permute-start.9) | collective-permute-done | bytes 262176 | tf_op jit(solution)/shard_map/ppermute | solution.py:228
  99.8 2.6 %collective-permute-done.10.other_ref = bf16[4,8,128,128]{3,2,1,0:T(8,128)(2,1)S(1)} collective-permute-done((bf16[4,8,128,128]{3,2,1,0:T(8,128)(2,1)S(1)}, bf16[4,8,128,128]{3,2,1,0:T(8,128)(2,1)S(1)}, u32[]{:S(2)}, u32[]{:S(2)}) %collective-permute-start.10) | collective-permute-done | bytes 1048608 | tf_op jit(solution)/shard_map/ppermute | solution.py:228
  103.9 2.9 %grad_parts.1 = f32[8,448,128]{2,1,0:T(8,128)} custom-call(s32[4]{0:T(128)S(1)} %pad_add_fusion.place_ref, bf16[4,8,128,128]{3,2,1,0:T(8,128)(2,1)S(1)} %pad_maximum_fusion.own_ref, bf16[4,8,128,128]{3,2,1,0:T(8,128)(2,1)S(1)} %collective-permute-done.10.other_ref, bf16[8,2,448,128]{3,2,1,0:T(8,128)(2,1)S(1)} %bitcast.37), custom_call_target="tpu_custom_call" | custom-call | tf_op jit(solution)/shard_map/grad_parts/pallas_call | solution.py:175
  106.8 6.7 %all-to-all-done.1.state_ref = bf16[64,80,128]{2,1,0:T(8,128)(2,1)S(1)} async-done(((bf16[64,80,128]{2,1,0:T(8,128)(2,1)}), bf16[64,80,128]{2,1,0:T(8,128)(2,1)S(1)}, u32[]{:S(2)}, u32[]{:S(2)}) %all-to-all-start.1) | async-done | bytes 1310752 | tf_op jit(solution)/shard_map/all_to_all | solution.py:223
  113.7 2.1 %collective-permute-start.11 = (bf16[56,64,128]{2,1,0:T(8,128)(2,1)S(1)}, bf16[56,64,128]{2,1,0:T(8,128)(2,1)S(1)}, u32[]{:S(2)}, u32[]{:S(2)}) collective-permute-start(bf16[56,64,128]{2,1,0:T(8,128)(2,1)S(1)} %slice.3.own_ref), channel_id=1, source_target_pairs={{0,1},{1,0},{2,3},{3,2},{4,5},{5,4},{6,7},{7,6},{8,9},{9,8},{10,11... | collective-permute-start | bytes 2752520 | tf_op jit(solution)/shard_map/ppermute | solution.py:228
  115.7 2.4 %collective-permute-done.11.other_ref = bf16[56,64,128]{2,1,0:T(8,128)(2,1)S(1)} collective-permute-done((bf16[56,64,128]{2,1,0:T(8,128)(2,1)S(1)}, bf16[56,64,128]{2,1,0:T(8,128)(2,1)S(1)}, u32[]{:S(2)}, u32[]{:S(2)}) %collective-permute-start.11) | collective-permute-done | bytes 917536 | tf_op jit(solution)/shard_map/ppermute | solution.py:228
  120.0 17.9 %all_to_all.20.parts_ref = bf16[4,8,128,128]{3,2,1,0:T(8,128)(2,1)S(1)} all-to-all(bf16[4,8,128,128]{3,2,1,0:T(8,128)(2,1)S(1)} %act_sums.1), channel_id=1, replica_groups=mesh['z'=8,'y'=8,'x'=4,'c'=2] {'x'}, dimensions={0} | all-to-all | bytes 2097152 | tf_op jit(solution)/shard_map/all_to_all | solution.py:223
  138.9 5.7 %all-to-all-start.3 = ((bf16[8,128,128]{2,1,0:T(8,128)(2,1)}), bf16[8,128,128]{2,1,0:T(8,128)(2,1)S(1)}, u32[]{:S(2)}, u32[]{:S(2)}) async-start(bf16[8,128,128]{2,1,0:T(8,128)(2,1)} %act_total.1), calls=%async_computation.3 | async-start | bytes 524288 | tf_op jit(solution)/shard_map/all_to_all | solution.py:223
  144.6 11.7 %reduce-scatter.2.cloned.1.call-done = f32[1,448,128]{2,1,0:T(8,128)} async-done(((f32[8,448,128]{2,1,0:T(8,128)}), f32[1,448,128]{2,1,0:T(8,128)}) %reduce-scatter.2.cloned.1.call-update) | async-done | bytes 229392 | tf_op jit(solution)/shard_map/reduce_scatter | solution.py:244
  (46 shorter events, 18.5 us)
Async XLA Ops:
  7.2 1.3 copy-start.5
  10.8 17.3 %copy-start.2 = (bf16[16,8192]{1,0:T(8,128)(2,1)S(1)}, bf16[16,8192]{1,0:T(8,128)(2,1)}, u32[]{:S(2)}) copy-start(bf16[16,8192]{1,0:T(8,128)(2,1)} %act_ref.1) | copy-start | bytes 786436
  10.9 57.6 %copy-start.4 = (s32[25]{0:T(128)S(1)}, s32[25]{0:T(128)}, u32[]{:S(2)}) copy-start(s32[25]{0:T(128)} %offsets_ref.1) | copy-start | bytes 304
  10.9 57.6 %all-to-all-start = ((bf16[64,72,128]{2,1,0:T(8,128)(2,1)}), bf16[64,72,128]{2,1,0:T(8,128)(2,1)S(1)}, u32[]{:S(2)}, u32[]{:S(2)}) async-start(bf16[64,72,128]{2,1,0:T(8,128)(2,1)} %pack.1), calls=%async_computation | async-start | bytes 2359296 | tf_op jit(solution)/shard_map/all_to_all | solution.py:223
  27.3 70.5 %all-gather.3.cloned.1.call-start = ((), (), s32[]{:S(2)}) async-start(), calls=%async_computation.6 | async-start | bytes 1949696 | tf_op jit(solution)/shard_map/all_gather | solution.py:233
  28.8 21.8 %collective-permute-start = (bf16[128,128]{1,0:T(8,128)(2,1)S(1)}, bf16[128,128]{1,0:T(8,128)(2,1)S(1)}, u32[]{:S(2)}, u32[]{:S(2)}) collective-permute-start(bf16[128,128]{1,0:T(8,128)(2,1)S(1)} %get-tuple-element.26), channel_id=1, source_target_pairs={{0,64},{64,128},{128,192},{192,256},{256,320},{320,384},{384,448},... | collective-permute-start | bytes 98312 | tf_op jit(solution)/shard_map/ppermute | solution.py:228
  32.2 30.2 %collective-permute-start.1 = (bf16[128,128]{1,0:T(8,128)(2,1)S(1)}, bf16[128,128]{1,0:T(8,128)(2,1)S(1)}, u32[]{:S(2)}, u32[]{:S(2)}) collective-permute-start(bf16[128,128]{1,0:T(8,128)(2,1)S(1)} %get-tuple-element.27), channel_id=1, source_target_pairs={{0,128},{64,192},{128,256},{192,320},{256,384},{320,448},{384,0},{... | collective-permute-start | bytes 98312 | tf_op jit(solution)/shard_map/ppermute | solution.py:228
  36.5 28.4 %collective-permute-start.2 = (bf16[128,128]{1,0:T(8,128)(2,1)S(1)}, bf16[128,128]{1,0:T(8,128)(2,1)S(1)}, u32[]{:S(2)}, u32[]{:S(2)}) collective-permute-start(bf16[128,128]{1,0:T(8,128)(2,1)S(1)} %get-tuple-element.28), channel_id=1, source_target_pairs={{0,192},{64,256},{128,320},{192,384},{256,448},{320,0},{384,64},{4... | collective-permute-start | bytes 98312 | tf_op jit(solution)/shard_map/ppermute | solution.py:228
  41.3 25.0 %collective-permute-start.3 = (bf16[128,128]{1,0:T(8,128)(2,1)S(1)}, bf16[128,128]{1,0:T(8,128)(2,1)S(1)}, u32[]{:S(2)}, u32[]{:S(2)}) collective-permute-start(bf16[128,128]{1,0:T(8,128)(2,1)S(1)} %get-tuple-element.29), channel_id=1, source_target_pairs={{0,256},{64,320},{128,384},{192,448},{256,0},{320,64},{384,128},{4... | collective-permute-start | bytes 98312 | tf_op jit(solution)/shard_map/ppermute | solution.py:228
  45.3 20.9 %collective-permute-start.4 = (bf16[128,128]{1,0:T(8,128)(2,1)S(1)}, bf16[128,128]{1,0:T(8,128)(2,1)S(1)}, u32[]{:S(2)}, u32[]{:S(2)}) collective-permute-start(bf16[128,128]{1,0:T(8,128)(2,1)S(1)} %get-tuple-element.30), channel_id=1, source_target_pairs={{0,320},{64,384},{128,448},{192,0},{256,64},{320,128},{384,192},{4... | collective-permute-start | bytes 98312 | tf_op jit(solution)/shard_map/ppermute | solution.py:228
  50.6 15.7 %collective-permute-start.5 = (bf16[128,128]{1,0:T(8,128)(2,1)S(1)}, bf16[128,128]{1,0:T(8,128)(2,1)S(1)}, u32[]{:S(2)}, u32[]{:S(2)}) collective-permute-start(bf16[128,128]{1,0:T(8,128)(2,1)S(1)} %get-tuple-element.31), channel_id=1, source_target_pairs={{0,384},{64,448},{128,0},{192,64},{256,128},{320,192},{384,256},{4... | collective-permute-start | bytes 98312 | tf_op jit(solution)/shard_map/ppermute | solution.py:228
  62.5 6.0 %collective-permute-start.6 = (bf16[128,128]{1,0:T(8,128)(2,1)S(1)}, bf16[128,128]{1,0:T(8,128)(2,1)S(1)}, u32[]{:S(2)}, u32[]{:S(2)}) collective-permute-start(bf16[128,128]{1,0:T(8,128)(2,1)S(1)} %get-tuple-element.32), channel_id=1, source_target_pairs={{0,448},{64,0},{128,64},{192,128},{256,192},{320,256},{384,320},{4... | collective-permute-start | bytes 98312 | tf_op jit(solution)/shard_map/ppermute | solution.py:228
  70.4 43.2 %all-to-all-start.1 = ((bf16[64,80,128]{2,1,0:T(8,128)(2,1)}), bf16[64,80,128]{2,1,0:T(8,128)(2,1)S(1)}, u32[]{:S(2)}, u32[]{:S(2)}) async-start(bf16[64,80,128]{2,1,0:T(8,128)(2,1)} %place.1), calls=%async_computation.1 | async-start | bytes 2621440 | tf_op jit(solution)/shard_map/all_to_all | solution.py:223
  80.0 76.3 %reduce-scatter.2.cloned.1.call-start = ((), (), s32[]{:S(2)}) async-start(), calls=%async_computation.5 | async-start | bytes 2064384 | tf_op jit(solution)/shard_map/reduce_scatter | solution.py:244
  80.1 10.8 %collective-permute-start.7 = (bf16[8,128,128]{2,1,0:T(8,128)(2,1)S(1)}, bf16[8,128,128]{2,1,0:T(8,128)(2,1)S(1)}, u32[]{:S(2)}, u32[]{:S(2)}) collective-permute-start(bf16[8,128,128]{2,1,0:T(8,128)(2,1)S(1)} %bitcast_dynamic-update-slice_fusion), channel_id=1, source_target_pairs={{0,2},{2,4},{4,6},{6,0},{1,3},{3,5},{5,7},{7,1},{8,10},{10,12},{12... | collective-permute-start | bytes 786440 | tf_op jit(solution)/shard_map/ppermute | solution.py:228
  82.3 12.1 %collective-permute-start.8 = (bf16[8,128,128]{2,1,0:T(8,128)(2,1)S(1)}, bf16[8,128,128]{2,1,0:T(8,128)(2,1)S(1)}, u32[]{:S(2)}, u32[]{:S(2)}) collective-permute-start(bf16[8,128,128]{2,1,0:T(8,128)(2,1)S(1)} %bitcast_dynamic-update-slice_fusion), channel_id=1, source_target_pairs={{0,4},{2,6},{4,0},{6,2},{1,5},{3,7},{5,1},{7,3},{8,12},{10,14},{12... | collective-permute-start | bytes 786440 | tf_op jit(solution)/shard_map/ppermute | solution.py:228
  86.8 10.9 %collective-permute-start.9 = (bf16[8,128,128]{2,1,0:T(8,128)(2,1)S(1)}, bf16[8,128,128]{2,1,0:T(8,128)(2,1)S(1)}, u32[]{:S(2)}, u32[]{:S(2)}) collective-permute-start(bf16[8,128,128]{2,1,0:T(8,128)(2,1)S(1)} %bitcast_dynamic-update-slice_fusion), channel_id=1, source_target_pairs={{0,6},{2,0},{4,2},{6,4},{1,7},{3,1},{5,3},{7,5},{8,14},{10,8},{12,... | collective-permute-start | bytes 786440 | tf_op jit(solution)/shard_map/ppermute | solution.py:228
  97.9 4.6 %collective-permute-start.10 = (bf16[4,8,128,128]{3,2,1,0:T(8,128)(2,1)S(1)}, bf16[4,8,128,128]{3,2,1,0:T(8,128)(2,1)S(1)}, u32[]{:S(2)}, u32[]{:S(2)}) collective-permute-start(bf16[4,8,128,128]{3,2,1,0:T(8,128)(2,1)S(1)} %pad_maximum_fusion.own_ref), channel_id=1, source_target_pairs={{0,1},{1,0},{2,3},{3,2},{4,5},{5,4},{6,7},{7,6},{8,9},{9,8},{10,11... | collective-permute-start | bytes 3145736 | tf_op jit(solution)/shard_map/ppermute | solution.py:228
  102.4 1.5 copy-start
  113.6 4.6 %copy-start.1 = (bf16[7168,128]{1,0:T(8,128)(2,1)S(1)}, bf16[7168,128]{1,0:T(8,128)(2,1)}, u32[]{:S(2)}) copy-start(bf16[7168,128]{1,0:T(8,128)(2,1)} %all-gather.3.cloned.1.call-done) | copy-start | bytes 5505028
  113.7 4.5 %collective-permute-start.11 = (bf16[56,64,128]{2,1,0:T(8,128)(2,1)S(1)}, bf16[56,64,128]{2,1,0:T(8,128)(2,1)S(1)}, u32[]{:S(2)}, u32[]{:S(2)}) collective-permute-start(bf16[56,64,128]{2,1,0:T(8,128)(2,1)S(1)} %slice.3.own_ref), channel_id=1, source_target_pairs={{0,1},{1,0},{2,3},{3,2},{4,5},{5,4},{6,7},{7,6},{8,9},{9,8},{10,11... | collective-permute-start | bytes 2752520 | tf_op jit(solution)/shard_map/ppermute | solution.py:228
  138.9 19.9 %all-to-all-start.3 = ((bf16[8,128,128]{2,1,0:T(8,128)(2,1)}), bf16[8,128,128]{2,1,0:T(8,128)(2,1)S(1)}, u32[]{:S(2)}, u32[]{:S(2)}) async-start(bf16[8,128,128]{2,1,0:T(8,128)(2,1)} %act_total.1), calls=%async_computation.3 | async-start | bytes 524288 | tf_op jit(solution)/shard_map/all_to_all | solution.py:223
  156.3 0.9 copy-start.3
Sparse Core Ops, SparseCore 0:
  30.3 57.1 all-gather.2
  113.7 42.5 reduce-scatter.1

commit v8 on v7

--- a/solution.py
+++ b/solution.py
@@ -73,12 +73,10 @@
 def place(offsets, slots):
     return pl.pallas_call(
         place_kernel,
-        grid=(1,),
         in_specs=[
             pl.BlockSpec(memory_space=pltpu.SMEM),
-            pl.BlockSpec((SHARDS, 72, LANES), lambda i: (0, 0, 0)),
+            pl.BlockSpec(memory_space=pltpu.VMEM),
         ],
-        out_specs=pl.BlockSpec((GROUPS, 80, LANES), lambda i: (0, 0, 0)),
         out_shape=jax.ShapeDtypeStruct((GROUPS, 80, LANES), bf16),
         scratch_shapes=[pltpu.VMEM((GROUPS + 4, 24, LANES), f32)],
         compiler_params=PARAMS,

time: 167 us -> 167 us (level)
  no operation moved by 1% of the time
where the time goes in v8:
time: 167 us; the launch traced here: 166 us
  starting transfers between devices  80.1 us (48%)
  waiting for transfers between devices  37 us (22%)
  blocking collectives  17.9 us (11%)
  between operations  14.3 us (9%)
  Pallas kernels  11 us (7%)
  local copies, waits for them, and re-layouts  3.42 us (2%)
  other arithmetic  2.59 us (2%)
    ppermute x12, starting transfers between devices, shift(): return lax.ppermute(x, axis, [(i, (i + by) % n) for i in range(n)])  48.2 us
    all_to_all x3, starting transfers between devices, exchange(): return lax.all_to_all(x, axis, split_axis=0, concat_axis=0, tiled=True)  31.8 us
    all_to_all x1, blocking collectives, exchange(): return lax.all_to_all(x, axis, split_axis=0, concat_axis=0, tiled=True)  17.9 us
    ppermute x12, waiting for transfers between devices, shift(): return lax.ppermute(x, axis, [(i, (i + by) % n) for i in range(n)])  17.9 us
    reduce_scatter x1, waiting for transfers between devices, shards(): grad = lax.psum_scatter(parts, 'y', scatter_dimension=0)  11.7 us
    all_to_all x3, waiting for transfers between devices, exchange(): return lax.all_to_all(x, axis, split_axis=0, concat_axis=0, tiled=True)  6.7 us
  transfers between devices with their start and end apart: 17, of which 10 were waited for; matrix products, arithmetic and copies ran while one was open for 0% of the time, Pallas kernels for 6%

profile of v8, /device:TPU:30, one launch (start us, length us, event | category | flops | bytes accessed | tf_op | source)
XLA Modules:
  0.0 166.4 jit_solution(4955143930433731435)
XLA Ops:
  10.9 16.5 %all-to-all-start = ((bf16[64,72,128]{2,1,0:T(8,128)(2,1)}), bf16[64,72,128]{2,1,0:T(8,128)(2,1)S(1)}, u32[]{:S(2)}, u32[]{:S(2)}) async-start(bf16[64,72,128]{2,1,0:T(8,128)(2,1)} %pack.1), calls=%async_computation | async-start | bytes 2359296 | tf_op jit(solution)/shard_map/all_to_all | solution.py:221
  28.8 3.4 %collective-permute-start = (bf16[128,128]{1,0:T(8,128)(2,1)S(1)}, bf16[128,128]{1,0:T(8,128)(2,1)S(1)}, u32[]{:S(2)}, u32[]{:S(2)}) collective-permute-start(bf16[128,128]{1,0:T(8,128)(2,1)S(1)} %get-tuple-element.26), channel_id=1, source_target_pairs={{0,64},{64,128},{128,192},{192,256},{256,320},{320,384},{384,448},... | collective-permute-start | bytes 98312 | tf_op jit(solution)/shard_map/ppermute | solution.py:226
  32.2 4.3 %collective-permute-start.1 = (bf16[128,128]{1,0:T(8,128)(2,1)S(1)}, bf16[128,128]{1,0:T(8,128)(2,1)S(1)}, u32[]{:S(2)}, u32[]{:S(2)}) collective-permute-start(bf16[128,128]{1,0:T(8,128)(2,1)S(1)} %get-tuple-element.27), channel_id=1, source_target_pairs={{0,128},{64,192},{128,256},{192,320},{256,384},{320,448},{384,0},{... | collective-permute-start | bytes 98312 | tf_op jit(solution)/shard_map/ppermute | solution.py:226
  36.5 4.7 %collective-permute-start.2 = (bf16[128,128]{1,0:T(8,128)(2,1)S(1)}, bf16[128,128]{1,0:T(8,128)(2,1)S(1)}, u32[]{:S(2)}, u32[]{:S(2)}) collective-permute-start(bf16[128,128]{1,0:T(8,128)(2,1)S(1)} %get-tuple-element.28), channel_id=1, source_target_pairs={{0,192},{64,256},{128,320},{192,384},{256,448},{320,0},{384,64},{4... | collective-permute-start | bytes 98312 | tf_op jit(solution)/shard_map/ppermute | solution.py:226
  41.3 4.1 %collective-permute-start.3 = (bf16[128,128]{1,0:T(8,128)(2,1)S(1)}, bf16[128,128]{1,0:T(8,128)(2,1)S(1)}, u32[]{:S(2)}, u32[]{:S(2)}) collective-permute-start(bf16[128,128]{1,0:T(8,128)(2,1)S(1)} %get-tuple-element.29), channel_id=1, source_target_pairs={{0,256},{64,320},{128,384},{192,448},{256,0},{320,64},{384,128},{4... | collective-permute-start | bytes 98312 | tf_op jit(solution)/shard_map/ppermute | solution.py:226
  45.3 4.9 %collective-permute-start.4 = (bf16[128,128]{1,0:T(8,128)(2,1)S(1)}, bf16[128,128]{1,0:T(8,128)(2,1)S(1)}, u32[]{:S(2)}, u32[]{:S(2)}) collective-permute-start(bf16[128,128]{1,0:T(8,128)(2,1)S(1)} %get-tuple-element.30), channel_id=1, source_target_pairs={{0,320},{64,384},{128,448},{192,0},{256,64},{320,128},{384,192},{4... | collective-permute-start | bytes 98312 | tf_op jit(solution)/shard_map/ppermute | solution.py:226
  50.6 11.8 %collective-permute-start.5 = (bf16[128,128]{1,0:T(8,128)(2,1)S(1)}, bf16[128,128]{1,0:T(8,128)(2,1)S(1)}, u32[]{:S(2)}, u32[]{:S(2)}) collective-permute-start(bf16[128,128]{1,0:T(8,128)(2,1)S(1)} %get-tuple-element.31), channel_id=1, source_target_pairs={{0,384},{64,448},{128,0},{192,64},{256,128},{320,192},{384,256},{4... | collective-permute-start | bytes 98312 | tf_op jit(solution)/shard_map/ppermute | solution.py:226
  62.5 2.5 %collective-permute-start.6 = (bf16[128,128]{1,0:T(8,128)(2,1)S(1)}, bf16[128,128]{1,0:T(8,128)(2,1)S(1)}, u32[]{:S(2)}, u32[]{:S(2)}) collective-permute-start(bf16[128,128]{1,0:T(8,128)(2,1)S(1)} %get-tuple-element.32), channel_id=1, source_target_pairs={{0,448},{64,0},{128,64},{192,128},{256,192},{320,256},{384,320},{4... | collective-permute-start | bytes 98312 | tf_op jit(solution)/shard_map/ppermute | solution.py:226
  66.3 2.1 %collective-permute-done.6 = bf16[128,128]{1,0:T(8,128)(2,1)S(1)} collective-permute-done((bf16[128,128]{1,0:T(8,128)(2,1)S(1)}, bf16[128,128]{1,0:T(8,128)(2,1)S(1)}, u32[]{:S(2)}, u32[]{:S(2)}) %collective-permute-start.6) | collective-permute-done | bytes 32800 | tf_op jit(solution)/shard_map/ppermute | solution.py:226
  68.4 1.9 %place.1 = bf16[64,80,128]{2,1,0:T(8,128)(2,1)} custom-call(s32[25]{0:T(128)S(1)} %copy-done.4, bf16[64,72,128]{2,1,0:T(8,128)(2,1)S(1)} %all-to-all-done.slots_ref), custom_call_target="tpu_custom_call" | custom-call | tf_op jit(solution)/shard_map/place/pallas_call | solution.py:74
  70.4 9.6 %all-to-all-start.1 = ((bf16[64,80,128]{2,1,0:T(8,128)(2,1)}), bf16[64,80,128]{2,1,0:T(8,128)(2,1)S(1)}, u32[]{:S(2)}, u32[]{:S(2)}) async-start(bf16[64,80,128]{2,1,0:T(8,128)(2,1)} %place.1), calls=%async_computation.1 | async-start | bytes 2621440 | tf_op jit(solution)/shard_map/all_to_all | solution.py:221
  80.1 2.3 %collective-permute-start.7 = (bf16[8,128,128]{2,1,0:T(8,128)(2,1)S(1)}, bf16[8,128,128]{2,1,0:T(8,128)(2,1)S(1)}, u32[]{:S(2)}, u32[]{:S(2)}) collective-permute-start(bf16[8,128,128]{2,1,0:T(8,128)(2,1)S(1)} %bitcast_dynamic-update-slice_fusion), channel_id=1, source_target_pairs={{0,2},{2,4},{4,6},{6,0},{1,3},{3,5},{5,7},{7,1},{8,10},{10,12},{12... | collective-permute-start | bytes 786440 | tf_op jit(solution)/shard_map/ppermute | solution.py:226
  82.3 4.5 %collective-permute-start.8 = (bf16[8,128,128]{2,1,0:T(8,128)(2,1)S(1)}, bf16[8,128,128]{2,1,0:T(8,128)(2,1)S(1)}, u32[]{:S(2)}, u32[]{:S(2)}) collective-permute-start(bf16[8,128,128]{2,1,0:T(8,128)(2,1)S(1)} %bitcast_dynamic-update-slice_fusion), channel_id=1, source_target_pairs={{0,4},{2,6},{4,0},{6,2},{1,5},{3,7},{5,1},{7,3},{8,12},{10,14},{12... | collective-permute-start | bytes 786440 | tf_op jit(solution)/shard_map/ppermute | solution.py:226
  88.7 2.1 %collective-permute-done.7 = bf16[8,128,128]{2,1,0:T(8,128)(2,1)S(1)} collective-permute-done((bf16[8,128,128]{2,1,0:T(8,128)(2,1)S(1)}, bf16[8,128,128]{2,1,0:T(8,128)(2,1)S(1)}, u32[]{:S(2)}, u32[]{:S(2)}) %collective-permute-start.7) | collective-permute-done | bytes 262176 | tf_op jit(solution)/shard_map/ppermute | solution.py:226
  90.9 3.5 %collective-permute-done.8 = bf16[8,128,128]{2,1,0:T(8,128)(2,1)S(1)} collective-permute-done((bf16[8,128,128]{2,1,0:T(8,128)(2,1)S(1)}, bf16[8,128,128]{2,1,0:T(8,128)(2,1)S(1)}, u32[]{:S(2)}, u32[]{:S(2)}) %collective-permute-start.8) | collective-permute-done | bytes 262176 | tf_op jit(solution)/shard_map/ppermute | solution.py:226
  94.4 3.3 %collective-permute-done.9 = bf16[8,128,128]{2,1,0:T(8,128)(2,1)S(1)} collective-permute-done((bf16[8,128,128]{2,1,0:T(8,128)(2,1)S(1)}, bf16[8,128,128]{2,1,0:T(8,128)(2,1)S(1)}, u32[]{:S(2)}, u32[]{:S(2)}) %collective-permute-start.9) | collective-permute-done | bytes 262176 | tf_op jit(solution)/shard_map/ppermute | solution.py:226
  99.8 2.6 %collective-permute-done.10.other_ref = bf16[4,8,128,128]{3,2,1,0:T(8,128)(2,1)S(1)} collective-permute-done((bf16[4,8,128,128]{3,2,1,0:T(8,128)(2,1)S(1)}, bf16[4,8,128,128]{3,2,1,0:T(8,128)(2,1)S(1)}, u32[]{:S(2)}, u32[]{:S(2)}) %collective-permute-start.10) | collective-permute-done | bytes 1048608 | tf_op jit(solution)/shard_map/ppermute | solution.py:226
  103.9 2.9 %grad_parts.1 = f32[8,448,128]{2,1,0:T(8,128)} custom-call(s32[4]{0:T(128)S(1)} %pad_add_fusion.place_ref, bf16[4,8,128,128]{3,2,1,0:T(8,128)(2,1)S(1)} %pad_maximum_fusion.own_ref, bf16[4,8,128,128]{3,2,1,0:T(8,128)(2,1)S(1)} %collective-permute-done.10.other_ref, bf16[8,2,448,128]{3,2,1,0:T(8,128)(2,1)S(1)} %bitcast.37), custom_call_target="tpu_custom_call" | custom-call | tf_op jit(solution)/shard_map/grad_parts/pallas_call | solution.py:173
  106.8 6.7 %all-to-all-done.1.state_ref = bf16[64,80,128]{2,1,0:T(8,128)(2,1)S(1)} async-done(((bf16[64,80,128]{2,1,0:T(8,128)(2,1)}), bf16[64,80,128]{2,1,0:T(8,128)(2,1)S(1)}, u32[]{:S(2)}, u32[]{:S(2)}) %all-to-all-start.1) | async-done | bytes 1310752 | tf_op jit(solution)/shard_map/all_to_all | solution.py:221
  113.7 2.1 %collective-permute-start.11 = (bf16[56,64,128]{2,1,0:T(8,128)(2,1)S(1)}, bf16[56,64,128]{2,1,0:T(8,128)(2,1)S(1)}, u32[]{:S(2)}, u32[]{:S(2)}) collective-permute-start(bf16[56,64,128]{2,1,0:T(8,128)(2,1)S(1)} %slice.3.own_ref), channel_id=1, source_target_pairs={{0,1},{1,0},{2,3},{3,2},{4,5},{5,4},{6,7},{7,6},{8,9},{9,8},{10,11... | collective-permute-start | bytes 2752520 | tf_op jit(solution)/shard_map/ppermute | solution.py:226
  115.7 2.4 %collective-permute-done.11.other_ref = bf16[56,64,128]{2,1,0:T(8,128)(2,1)S(1)} collective-permute-done((bf16[56,64,128]{2,1,0:T(8,128)(2,1)S(1)}, bf16[56,64,128]{2,1,0:T(8,128)(2,1)S(1)}, u32[]{:S(2)}, u32[]{:S(2)}) %collective-permute-start.11) | collective-permute-done | bytes 917536 | tf_op jit(solution)/shard_map/ppermute | solution.py:226
  120.0 17.9 %all_to_all.20.parts_ref = bf16[4,8,128,128]{3,2,1,0:T(8,128)(2,1)S(1)} all-to-all(bf16[4,8,128,128]{3,2,1,0:T(8,128)(2,1)S(1)} %act_sums.1), channel_id=1, replica_groups=mesh['z'=8,'y'=8,'x'=4,'c'=2] {'x'}, dimensions={0} | all-to-all | bytes 2097152 | tf_op jit(solution)/shard_map/all_to_all | solution.py:221
  138.9 5.7 %all-to-all-start.3 = ((bf16[8,128,128]{2,1,0:T(8,128)(2,1)}), bf16[8,128,128]{2,1,0:T(8,128)(2,1)S(1)}, u32[]{:S(2)}, u32[]{:S(2)}) async-start(bf16[8,128,128]{2,1,0:T(8,128)(2,1)} %act_total.1), calls=%async_computation.3 | async-start | bytes 524288 | tf_op jit(solution)/shard_map/all_to_all | solution.py:221
  144.6 11.7 %reduce-scatter.2.cloned.1.call-done = f32[1,448,128]{2,1,0:T(8,128)} async-done(((f32[8,448,128]{2,1,0:T(8,128)}), f32[1,448,128]{2,1,0:T(8,128)}) %reduce-scatter.2.cloned.1.call-update) | async-done | bytes 229392 | tf_op jit(solution)/shard_map/reduce_scatter | solution.py:242
  (46 shorter events, 18.5 us)
Async XLA Ops:
  7.2 1.3 copy-start.5
  10.8 17.3 %copy-start.2 = (bf16[16,8192]{1,0:T(8,128)(2,1)S(1)}, bf16[16,8192]{1,0:T(8,128)(2,1)}, u32[]{:S(2)}) copy-start(bf16[16,8192]{1,0:T(8,128)(2,1)} %act_ref.1) | copy-start | bytes 786436
  10.9 57.6 %copy-start.4 = (s32[25]{0:T(128)S(1)}, s32[25]{0:T(128)}, u32[]{:S(2)}) copy-start(s32[25]{0:T(128)} %offsets_ref.1) | copy-start | bytes 304
  10.9 57.6 %all-to-all-start = ((bf16[64,72,128]{2,1,0:T(8,128)(2,1)}), bf16[64,72,128]{2,1,0:T(8,128)(2,1)S(1)}, u32[]{:S(2)}, u32[]{:S(2)}) async-start(bf16[64,72,128]{2,1,0:T(8,128)(2,1)} %pack.1), calls=%async_computation | async-start | bytes 2359296 | tf_op jit(solution)/shard_map/all_to_all | solution.py:221
  27.3 70.5 %all-gather.3.cloned.1.call-start = ((), (), s32[]{:S(2)}) async-start(), calls=%async_computation.6 | async-start | bytes 1949696 | tf_op jit(solution)/shard_map/all_gather | solution.py:231
  28.8 21.8 %collective-permute-start = (bf16[128,128]{1,0:T(8,128)(2,1)S(1)}, bf16[128,128]{1,0:T(8,128)(2,1)S(1)}, u32[]{:S(2)}, u32[]{:S(2)}) collective-permute-start(bf16[128,128]{1,0:T(8,128)(2,1)S(1)} %get-tuple-element.26), channel_id=1, source_target_pairs={{0,64},{64,128},{128,192},{192,256},{256,320},{320,384},{384,448},... | collective-permute-start | bytes 98312 | tf_op jit(solution)/shard_map/ppermute | solution.py:226
  32.2 30.2 %collective-permute-start.1 = (bf16[128,128]{1,0:T(8,128)(2,1)S(1)}, bf16[128,128]{1,0:T(8,128)(2,1)S(1)}, u32[]{:S(2)}, u32[]{:S(2)}) collective-permute-start(bf16[128,128]{1,0:T(8,128)(2,1)S(1)} %get-tuple-element.27), channel_id=1, source_target_pairs={{0,128},{64,192},{128,256},{192,320},{256,384},{320,448},{384,0},{... | collective-permute-start | bytes 98312 | tf_op jit(solution)/shard_map/ppermute | solution.py:226
  36.5 28.4 %collective-permute-start.2 = (bf16[128,128]{1,0:T(8,128)(2,1)S(1)}, bf16[128,128]{1,0:T(8,128)(2,1)S(1)}, u32[]{:S(2)}, u32[]{:S(2)}) collective-permute-start(bf16[128,128]{1,0:T(8,128)(2,1)S(1)} %get-tuple-element.28), channel_id=1, source_target_pairs={{0,192},{64,256},{128,320},{192,384},{256,448},{320,0},{384,64},{4... | collective-permute-start | bytes 98312 | tf_op jit(solution)/shard_map/ppermute | solution.py:226
  41.3 25.0 %collective-permute-start.3 = (bf16[128,128]{1,0:T(8,128)(2,1)S(1)}, bf16[128,128]{1,0:T(8,128)(2,1)S(1)}, u32[]{:S(2)}, u32[]{:S(2)}) collective-permute-start(bf16[128,128]{1,0:T(8,128)(2,1)S(1)} %get-tuple-element.29), channel_id=1, source_target_pairs={{0,256},{64,320},{128,384},{192,448},{256,0},{320,64},{384,128},{4... | collective-permute-start | bytes 98312 | tf_op jit(solution)/shard_map/ppermute | solution.py:226
  45.3 20.9 %collective-permute-start.4 = (bf16[128,128]{1,0:T(8,128)(2,1)S(1)}, bf16[128,128]{1,0:T(8,128)(2,1)S(1)}, u32[]{:S(2)}, u32[]{:S(2)}) collective-permute-start(bf16[128,128]{1,0:T(8,128)(2,1)S(1)} %get-tuple-element.30), channel_id=1, source_target_pairs={{0,320},{64,384},{128,448},{192,0},{256,64},{320,128},{384,192},{4... | collective-permute-start | bytes 98312 | tf_op jit(solution)/shard_map/ppermute | solution.py:226
  50.6 15.7 %collective-permute-start.5 = (bf16[128,128]{1,0:T(8,128)(2,1)S(1)}, bf16[128,128]{1,0:T(8,128)(2,1)S(1)}, u32[]{:S(2)}, u32[]{:S(2)}) collective-permute-start(bf16[128,128]{1,0:T(8,128)(2,1)S(1)} %get-tuple-element.31), channel_id=1, source_target_pairs={{0,384},{64,448},{128,0},{192,64},{256,128},{320,192},{384,256},{4... | collective-permute-start | bytes 98312 | tf_op jit(solution)/shard_map/ppermute | solution.py:226
  62.5 6.0 %collective-permute-start.6 = (bf16[128,128]{1,0:T(8,128)(2,1)S(1)}, bf16[128,128]{1,0:T(8,128)(2,1)S(1)}, u32[]{:S(2)}, u32[]{:S(2)}) collective-permute-start(bf16[128,128]{1,0:T(8,128)(2,1)S(1)} %get-tuple-element.32), channel_id=1, source_target_pairs={{0,448},{64,0},{128,64},{192,128},{256,192},{320,256},{384,320},{4... | collective-permute-start | bytes 98312 | tf_op jit(solution)/shard_map/ppermute | solution.py:226
  70.4 43.2 %all-to-all-start.1 = ((bf16[64,80,128]{2,1,0:T(8,128)(2,1)}), bf16[64,80,128]{2,1,0:T(8,128)(2,1)S(1)}, u32[]{:S(2)}, u32[]{:S(2)}) async-start(bf16[64,80,128]{2,1,0:T(8,128)(2,1)} %place.1), calls=%async_computation.1 | async-start | bytes 2621440 | tf_op jit(solution)/shard_map/all_to_all | solution.py:221
  80.0 76.3 %reduce-scatter.2.cloned.1.call-start = ((), (), s32[]{:S(2)}) async-start(), calls=%async_computation.5 | async-start | bytes 2064384 | tf_op jit(solution)/shard_map/reduce_scatter | solution.py:242
  80.1 10.8 %collective-permute-start.7 = (bf16[8,128,128]{2,1,0:T(8,128)(2,1)S(1)}, bf16[8,128,128]{2,1,0:T(8,128)(2,1)S(1)}, u32[]{:S(2)}, u32[]{:S(2)}) collective-permute-start(bf16[8,128,128]{2,1,0:T(8,128)(2,1)S(1)} %bitcast_dynamic-update-slice_fusion), channel_id=1, source_target_pairs={{0,2},{2,4},{4,6},{6,0},{1,3},{3,5},{5,7},{7,1},{8,10},{10,12},{12... | collective-permute-start | bytes 786440 | tf_op jit(solution)/shard_map/ppermute | solution.py:226
  82.3 12.1 %collective-permute-start.8 = (bf16[8,128,128]{2,1,0:T(8,128)(2,1)S(1)}, bf16[8,128,128]{2,1,0:T(8,128)(2,1)S(1)}, u32[]{:S(2)}, u32[]{:S(2)}) collective-permute-start(bf16[8,128,128]{2,1,0:T(8,128)(2,1)S(1)} %bitcast_dynamic-update-slice_fusion), channel_id=1, source_target_pairs={{0,4},{2,6},{4,0},{6,2},{1,5},{3,7},{5,1},{7,3},{8,12},{10,14},{12... | collective-permute-start | bytes 786440 | tf_op jit(solution)/shard_map/ppermute | solution.py:226
  86.8 10.9 %collective-permute-start.9 = (bf16[8,128,128]{2,1,0:T(8,128)(2,1)S(1)}, bf16[8,128,128]{2,1,0:T(8,128)(2,1)S(1)}, u32[]{:S(2)}, u32[]{:S(2)}) collective-permute-start(bf16[8,128,128]{2,1,0:T(8,128)(2,1)S(1)} %bitcast_dynamic-update-slice_fusion), channel_id=1, source_target_pairs={{0,6},{2,0},{4,2},{6,4},{1,7},{3,1},{5,3},{7,5},{8,14},{10,8},{12,... | collective-permute-start | bytes 786440 | tf_op jit(solution)/shard_map/ppermute | solution.py:226
  97.9 4.6 %collective-permute-start.10 = (bf16[4,8,128,128]{3,2,1,0:T(8,128)(2,1)S(1)}, bf16[4,8,128,128]{3,2,1,0:T(8,128)(2,1)S(1)}, u32[]{:S(2)}, u32[]{:S(2)}) collective-permute-start(bf16[4,8,128,128]{3,2,1,0:T(8,128)(2,1)S(1)} %pad_maximum_fusion.own_ref), channel_id=1, source_target_pairs={{0,1},{1,0},{2,3},{3,2},{4,5},{5,4},{6,7},{7,6},{8,9},{9,8},{10,11... | collective-permute-start | bytes 3145736 | tf_op jit(solution)/shard_map/ppermute | solution.py:226
  102.4 1.5 copy-start
  113.6 4.6 %copy-start.1 = (bf16[7168,128]{1,0:T(8,128)(2,1)S(1)}, bf16[7168,128]{1,0:T(8,128)(2,1)}, u32[]{:S(2)}) copy-start(bf16[7168,128]{1,0:T(8,128)(2,1)} %all-gather.3.cloned.1.call-done) | copy-start | bytes 5505028
  113.7 4.5 %collective-permute-start.11 = (bf16[56,64,128]{2,1,0:T(8,128)(2,1)S(1)}, bf16[56,64,128]{2,1,0:T(8,128)(2,1)S(1)}, u32[]{:S(2)}, u32[]{:S(2)}) collective-permute-start(bf16[56,64,128]{2,1,0:T(8,128)(2,1)S(1)} %slice.3.own_ref), channel_id=1, source_target_pairs={{0,1},{1,0},{2,3},{3,2},{4,5},{5,4},{6,7},{7,6},{8,9},{9,8},{10,11... | collective-permute-start | bytes 2752520 | tf_op jit(solution)/shard_map/ppermute | solution.py:226
  138.9 19.9 %all-to-all-start.3 = ((bf16[8,128,128]{2,1,0:T(8,128)(2,1)}), bf16[8,128,128]{2,1,0:T(8,128)(2,1)S(1)}, u32[]{:S(2)}, u32[]{:S(2)}) async-start(bf16[8,128,128]{2,1,0:T(8,128)(2,1)} %act_total.1), calls=%async_computation.3 | async-start | bytes 524288 | tf_op jit(solution)/shard_map/all_to_all | solution.py:221
  156.3 0.9 copy-start.3
Sparse Core Ops, SparseCore 0:
  30.3 57.1 all-gather.2
  113.7 42.5 reduce-scatter.1

commit v9 on v8

--- a/solution.py
+++ b/solution.py
@@ -229,8 +229,8 @@
 def shards(old_weight, old_first, old_second, old_offsets, activations, upstream):
     here = jnp.stack([lax.axis_index(a) for a in ("z", "y", "x", "c")])
     up = lax.all_gather(upstream.T, ("z", "c"), axis=0).reshape(SIDE, 2, COLS, LANES)
-    halves = [t.T.astype(bf16) for t in (old_weight, old_first, old_second)]
-    got = exchange(pack(*halves), ("z", "y"))
+    blocks = pack(old_weight.T, old_first.T.astype(bf16), old_second.T.astype(bf16))
+    got = exchange(blocks, ("z", "y"))
     sent = send_blocks(here, activations)
     act = jnp.stack([sent[0]] + [shift(sent[s], "z", s) for s in range(1, SIDE)])
     got, act = lax.optimization_barrier((got, act))

time: 167 us -> 166 us (level)
  no operation moved by 1% of the time
where the time goes in v9:
time: 166 us; the launch traced here: 165 us
  starting transfers between devices  80.1 us (48%)
  waiting for transfers between devices  37 us (22%)
  blocking collectives  17.9 us (11%)
  between operations  14.3 us (9%)
  Pallas kernels  11 us (7%)
  local copies, waits for them, and re-layouts  3.39 us (2%)
    ppermute x12, starting transfers between devices, shift(): return lax.ppermute(x, axis, [(i, (i + by) % n) for i in range(n)])  48.2 us
    all_to_all x3, starting transfers between devices, exchange(): return lax.all_to_all(x, axis, split_axis=0, concat_axis=0, tiled=True)  31.8 us
    all_to_all x1, blocking collectives, exchange(): return lax.all_to_all(x, axis, split_axis=0, concat_axis=0, tiled=True)  17.9 us
    ppermute x12, waiting for transfers between devices, shift(): return lax.ppermute(x, axis, [(i, (i + by) % n) for i in range(n)])  17.9 us
    reduce_scatter x1, waiting for transfers between devices, shards(): grad = lax.psum_scatter(parts, 'y', scatter_dimension=0)  11.7 us
    all_to_all x3, waiting for transfers between devices, exchange(): return lax.all_to_all(x, axis, split_axis=0, concat_axis=0, tiled=True)  6.7 us
  transfers between devices with their start and end apart: 17, of which 10 were waited for; matrix products, arithmetic and copies ran while one was open for 0% of the time, Pallas kernels for 6%

profile of v9, /device:TPU:30, one launch (start us, length us, event | category | flops | bytes accessed | tf_op | source)
XLA Modules:
  0.0 165.4 jit_solution(12071129285418240977)
XLA Ops:
  9.8 16.5 %all-to-all-start = ((bf16[64,72,128]{2,1,0:T(8,128)(2,1)}), bf16[64,72,128]{2,1,0:T(8,128)(2,1)S(1)}, u32[]{:S(2)}, u32[]{:S(2)}) async-start(bf16[64,72,128]{2,1,0:T(8,128)(2,1)} %pack.1), calls=%async_computation | async-start | bytes 2359296 | tf_op jit(solution)/shard_map/all_to_all | solution.py:221
  27.8 3.4 %collective-permute-start = (bf16[128,128]{1,0:T(8,128)(2,1)S(1)}, bf16[128,128]{1,0:T(8,128)(2,1)S(1)}, u32[]{:S(2)}, u32[]{:S(2)}) collective-permute-start(bf16[128,128]{1,0:T(8,128)(2,1)S(1)} %get-tuple-element.26), channel_id=1, source_target_pairs={{0,64},{64,128},{128,192},{192,256},{256,320},{320,384},{384,448},... | collective-permute-start | bytes 98312 | tf_op jit(solution)/shard_map/ppermute | solution.py:226
  31.2 4.3 %collective-permute-start.1 = (bf16[128,128]{1,0:T(8,128)(2,1)S(1)}, bf16[128,128]{1,0:T(8,128)(2,1)S(1)}, u32[]{:S(2)}, u32[]{:S(2)}) collective-permute-start(bf16[128,128]{1,0:T(8,128)(2,1)S(1)} %get-tuple-element.27), channel_id=1, source_target_pairs={{0,128},{64,192},{128,256},{192,320},{256,384},{320,448},{384,0},{... | collective-permute-start | bytes 98312 | tf_op jit(solution)/shard_map/ppermute | solution.py:226
  35.5 4.7 %collective-permute-start.2 = (bf16[128,128]{1,0:T(8,128)(2,1)S(1)}, bf16[128,128]{1,0:T(8,128)(2,1)S(1)}, u32[]{:S(2)}, u32[]{:S(2)}) collective-permute-start(bf16[128,128]{1,0:T(8,128)(2,1)S(1)} %get-tuple-element.28), channel_id=1, source_target_pairs={{0,192},{64,256},{128,320},{192,384},{256,448},{320,0},{384,64},{4... | collective-permute-start | bytes 98312 | tf_op jit(solution)/shard_map/ppermute | solution.py:226
  40.3 4.1 %collective-permute-start.3 = (bf16[128,128]{1,0:T(8,128)(2,1)S(1)}, bf16[128,128]{1,0:T(8,128)(2,1)S(1)}, u32[]{:S(2)}, u32[]{:S(2)}) collective-permute-start(bf16[128,128]{1,0:T(8,128)(2,1)S(1)} %get-tuple-element.29), channel_id=1, source_target_pairs={{0,256},{64,320},{128,384},{192,448},{256,0},{320,64},{384,128},{4... | collective-permute-start | bytes 98312 | tf_op jit(solution)/shard_map/ppermute | solution.py:226
  44.3 4.9 %collective-permute-start.4 = (bf16[128,128]{1,0:T(8,128)(2,1)S(1)}, bf16[128,128]{1,0:T(8,128)(2,1)S(1)}, u32[]{:S(2)}, u32[]{:S(2)}) collective-permute-start(bf16[128,128]{1,0:T(8,128)(2,1)S(1)} %get-tuple-element.30), channel_id=1, source_target_pairs={{0,320},{64,384},{128,448},{192,0},{256,64},{320,128},{384,192},{4... | collective-permute-start | bytes 98312 | tf_op jit(solution)/shard_map/ppermute | solution.py:226
  49.6 11.8 %collective-permute-start.5 = (bf16[128,128]{1,0:T(8,128)(2,1)S(1)}, bf16[128,128]{1,0:T(8,128)(2,1)S(1)}, u32[]{:S(2)}, u32[]{:S(2)}) collective-permute-start(bf16[128,128]{1,0:T(8,128)(2,1)S(1)} %get-tuple-element.31), channel_id=1, source_target_pairs={{0,384},{64,448},{128,0},{192,64},{256,128},{320,192},{384,256},{4... | collective-permute-start | bytes 98312 | tf_op jit(solution)/shard_map/ppermute | solution.py:226
  61.4 2.5 %collective-permute-start.6 = (bf16[128,128]{1,0:T(8,128)(2,1)S(1)}, bf16[128,128]{1,0:T(8,128)(2,1)S(1)}, u32[]{:S(2)}, u32[]{:S(2)}) collective-permute-start(bf16[128,128]{1,0:T(8,128)(2,1)S(1)} %get-tuple-element.32), channel_id=1, source_target_pairs={{0,448},{64,0},{128,64},{192,128},{256,192},{320,256},{384,320},{4... | collective-permute-start | bytes 98312 | tf_op jit(solution)/shard_map/ppermute | solution.py:226
  65.3 2.1 %collective-permute-done.6 = bf16[128,128]{1,0:T(8,128)(2,1)S(1)} collective-permute-done((bf16[128,128]{1,0:T(8,128)(2,1)S(1)}, bf16[128,128]{1,0:T(8,128)(2,1)S(1)}, u32[]{:S(2)}, u32[]{:S(2)}) %collective-permute-start.6) | collective-permute-done | bytes 32800 | tf_op jit(solution)/shard_map/ppermute | solution.py:226
  67.4 1.9 %place.1 = bf16[64,80,128]{2,1,0:T(8,128)(2,1)} custom-call(s32[25]{0:T(128)S(1)} %copy-done.5, bf16[64,72,128]{2,1,0:T(8,128)(2,1)S(1)} %all-to-all-done.slots_ref), custom_call_target="tpu_custom_call" | custom-call | tf_op jit(solution)/shard_map/place/pallas_call | solution.py:74
  69.4 9.6 %all-to-all-start.1 = ((bf16[64,80,128]{2,1,0:T(8,128)(2,1)}), bf16[64,80,128]{2,1,0:T(8,128)(2,1)S(1)}, u32[]{:S(2)}, u32[]{:S(2)}) async-start(bf16[64,80,128]{2,1,0:T(8,128)(2,1)} %place.1), calls=%async_computation.1 | async-start | bytes 2621440 | tf_op jit(solution)/shard_map/all_to_all | solution.py:221
  79.0 2.3 %collective-permute-start.7 = (bf16[8,128,128]{2,1,0:T(8,128)(2,1)S(1)}, bf16[8,128,128]{2,1,0:T(8,128)(2,1)S(1)}, u32[]{:S(2)}, u32[]{:S(2)}) collective-permute-start(bf16[8,128,128]{2,1,0:T(8,128)(2,1)S(1)} %bitcast_dynamic-update-slice_fusion), channel_id=1, source_target_pairs={{0,2},{2,4},{4,6},{6,0},{1,3},{3,5},{5,7},{7,1},{8,10},{10,12},{12... | collective-permute-start | bytes 786440 | tf_op jit(solution)/shard_map/ppermute | solution.py:226
  81.3 4.5 %collective-permute-start.8 = (bf16[8,128,128]{2,1,0:T(8,128)(2,1)S(1)}, bf16[8,128,128]{2,1,0:T(8,128)(2,1)S(1)}, u32[]{:S(2)}, u32[]{:S(2)}) collective-permute-start(bf16[8,128,128]{2,1,0:T(8,128)(2,1)S(1)} %bitcast_dynamic-update-slice_fusion), channel_id=1, source_target_pairs={{0,4},{2,6},{4,0},{6,2},{1,5},{3,7},{5,1},{7,3},{8,12},{10,14},{12... | collective-permute-start | bytes 786440 | tf_op jit(solution)/shard_map/ppermute | solution.py:226
  87.7 2.1 %collective-permute-done.7 = bf16[8,128,128]{2,1,0:T(8,128)(2,1)S(1)} collective-permute-done((bf16[8,128,128]{2,1,0:T(8,128)(2,1)S(1)}, bf16[8,128,128]{2,1,0:T(8,128)(2,1)S(1)}, u32[]{:S(2)}, u32[]{:S(2)}) %collective-permute-start.7) | collective-permute-done | bytes 262176 | tf_op jit(solution)/shard_map/ppermute | solution.py:226
  89.8 3.5 %collective-permute-done.8 = bf16[8,128,128]{2,1,0:T(8,128)(2,1)S(1)} collective-permute-done((bf16[8,128,128]{2,1,0:T(8,128)(2,1)S(1)}, bf16[8,128,128]{2,1,0:T(8,128)(2,1)S(1)}, u32[]{:S(2)}, u32[]{:S(2)}) %collective-permute-start.8) | collective-permute-done | bytes 262176 | tf_op jit(solution)/shard_map/ppermute | solution.py:226
  93.4 3.3 %collective-permute-done.9 = bf16[8,128,128]{2,1,0:T(8,128)(2,1)S(1)} collective-permute-done((bf16[8,128,128]{2,1,0:T(8,128)(2,1)S(1)}, bf16[8,128,128]{2,1,0:T(8,128)(2,1)S(1)}, u32[]{:S(2)}, u32[]{:S(2)}) %collective-permute-start.9) | collective-permute-done | bytes 262176 | tf_op jit(solution)/shard_map/ppermute | solution.py:226
  98.8 2.6 %collective-permute-done.10.other_ref = bf16[4,8,128,128]{3,2,1,0:T(8,128)(2,1)S(1)} collective-permute-done((bf16[4,8,128,128]{3,2,1,0:T(8,128)(2,1)S(1)}, bf16[4,8,128,128]{3,2,1,0:T(8,128)(2,1)S(1)}, u32[]{:S(2)}, u32[]{:S(2)}) %collective-permute-start.10) | collective-permute-done | bytes 1048608 | tf_op jit(solution)/shard_map/ppermute | solution.py:226
  102.9 2.9 %grad_parts.1 = f32[8,448,128]{2,1,0:T(8,128)} custom-call(s32[4]{0:T(128)S(1)} %pad_add_fusion.place_ref, bf16[4,8,128,128]{3,2,1,0:T(8,128)(2,1)S(1)} %pad_maximum_fusion.own_ref, bf16[4,8,128,128]{3,2,1,0:T(8,128)(2,1)S(1)} %collective-permute-done.10.other_ref, bf16[8,2,448,128]{3,2,1,0:T(8,128)(2,1)S(1)} %bitcast.36), custom_call_target="tpu_custom_call" | custom-call | tf_op jit(solution)/shard_map/grad_parts/pallas_call | solution.py:173
  105.8 6.7 %all-to-all-done.1.state_ref = bf16[64,80,128]{2,1,0:T(8,128)(2,1)S(1)} async-done(((bf16[64,80,128]{2,1,0:T(8,128)(2,1)}), bf16[64,80,128]{2,1,0:T(8,128)(2,1)S(1)}, u32[]{:S(2)}, u32[]{:S(2)}) %all-to-all-start.1) | async-done | bytes 1310752 | tf_op jit(solution)/shard_map/all_to_all | solution.py:221
  112.7 2.1 %collective-permute-start.11 = (bf16[56,64,128]{2,1,0:T(8,128)(2,1)S(1)}, bf16[56,64,128]{2,1,0:T(8,128)(2,1)S(1)}, u32[]{:S(2)}, u32[]{:S(2)}) collective-permute-start(bf16[56,64,128]{2,1,0:T(8,128)(2,1)S(1)} %slice.3.own_ref), channel_id=1, source_target_pairs={{0,1},{1,0},{2,3},{3,2},{4,5},{5,4},{6,7},{7,6},{8,9},{9,8},{10,11... | collective-permute-start | bytes 2752520 | tf_op jit(solution)/shard_map/ppermute | solution.py:226
  114.7 2.4 %collective-permute-done.11.other_ref = bf16[56,64,128]{2,1,0:T(8,128)(2,1)S(1)} collective-permute-done((bf16[56,64,128]{2,1,0:T(8,128)(2,1)S(1)}, bf16[56,64,128]{2,1,0:T(8,128)(2,1)S(1)}, u32[]{:S(2)}, u32[]{:S(2)}) %collective-permute-start.11) | collective-permute-done | bytes 917536 | tf_op jit(solution)/shard_map/ppermute | solution.py:226
  119.0 17.9 %all_to_all.20.parts_ref = bf16[4,8,128,128]{3,2,1,0:T(8,128)(2,1)S(1)} all-to-all(bf16[4,8,128,128]{3,2,1,0:T(8,128)(2,1)S(1)} %act_sums.1), channel_id=1, replica_groups=mesh['z'=8,'y'=8,'x'=4,'c'=2] {'x'}, dimensions={0} | all-to-all | bytes 2097152 | tf_op jit(solution)/shard_map/all_to_all | solution.py:221
  137.9 5.7 %all-to-all-start.3 = ((bf16[8,128,128]{2,1,0:T(8,128)(2,1)}), bf16[8,128,128]{2,1,0:T(8,128)(2,1)S(1)}, u32[]{:S(2)}, u32[]{:S(2)}) async-start(bf16[8,128,128]{2,1,0:T(8,128)(2,1)} %act_total.1), calls=%async_computation.3 | async-start | bytes 524288 | tf_op jit(solution)/shard_map/all_to_all | solution.py:221
  143.6 11.7 %reduce-scatter.2.cloned.1.call-done = f32[1,448,128]{2,1,0:T(8,128)} async-done(((f32[8,448,128]{2,1,0:T(8,128)}), f32[1,448,128]{2,1,0:T(8,128)}) %reduce-scatter.2.cloned.1.call-update) | async-done | bytes 229392 | tf_op jit(solution)/shard_map/reduce_scatter | solution.py:242
  (45 shorter events, 17.5 us)
Async XLA Ops:
  7.2 1.5 copy-start.2
  9.8 17.3 %copy-start.3 = (bf16[16,8192]{1,0:T(8,128)(2,1)S(1)}, bf16[16,8192]{1,0:T(8,128)(2,1)}, u32[]{:S(2)}) copy-start(bf16[16,8192]{1,0:T(8,128)(2,1)} %act_ref.1) | copy-start | bytes 786436
  9.8 57.6 %copy-start.5 = (s32[25]{0:T(128)S(1)}, s32[25]{0:T(128)}, u32[]{:S(2)}) copy-start(s32[25]{0:T(128)} %offsets_ref.1) | copy-start | bytes 304
  9.8 57.6 %all-to-all-start = ((bf16[64,72,128]{2,1,0:T(8,128)(2,1)}), bf16[64,72,128]{2,1,0:T(8,128)(2,1)S(1)}, u32[]{:S(2)}, u32[]{:S(2)}) async-start(bf16[64,72,128]{2,1,0:T(8,128)(2,1)} %pack.1), calls=%async_computation | async-start | bytes 2359296 | tf_op jit(solution)/shard_map/all_to_all | solution.py:221
  26.3 70.5 %all-gather.3.cloned.1.call-start = ((), (), s32[]{:S(2)}) async-start(), calls=%async_computation.6 | async-start | bytes 1949696 | tf_op jit(solution)/shard_map/all_gather | solution.py:231
  27.8 21.8 %collective-permute-start = (bf16[128,128]{1,0:T(8,128)(2,1)S(1)}, bf16[128,128]{1,0:T(8,128)(2,1)S(1)}, u32[]{:S(2)}, u32[]{:S(2)}) collective-permute-start(bf16[128,128]{1,0:T(8,128)(2,1)S(1)} %get-tuple-element.26), channel_id=1, source_target_pairs={{0,64},{64,128},{128,192},{192,256},{256,320},{320,384},{384,448},... | collective-permute-start | bytes 98312 | tf_op jit(solution)/shard_map/ppermute | solution.py:226
  31.2 30.2 %collective-permute-start.1 = (bf16[128,128]{1,0:T(8,128)(2,1)S(1)}, bf16[128,128]{1,0:T(8,128)(2,1)S(1)}, u32[]{:S(2)}, u32[]{:S(2)}) collective-permute-start(bf16[128,128]{1,0:T(8,128)(2,1)S(1)} %get-tuple-element.27), channel_id=1, source_target_pairs={{0,128},{64,192},{128,256},{192,320},{256,384},{320,448},{384,0},{... | collective-permute-start | bytes 98312 | tf_op jit(solution)/shard_map/ppermute | solution.py:226
  35.5 28.4 %collective-permute-start.2 = (bf16[128,128]{1,0:T(8,128)(2,1)S(1)}, bf16[128,128]{1,0:T(8,128)(2,1)S(1)}, u32[]{:S(2)}, u32[]{:S(2)}) collective-permute-start(bf16[128,128]{1,0:T(8,128)(2,1)S(1)} %get-tuple-element.28), channel_id=1, source_target_pairs={{0,192},{64,256},{128,320},{192,384},{256,448},{320,0},{384,64},{4... | collective-permute-start | bytes 98312 | tf_op jit(solution)/shard_map/ppermute | solution.py:226
  40.3 25.0 %collective-permute-start.3 = (bf16[128,128]{1,0:T(8,128)(2,1)S(1)}, bf16[128,128]{1,0:T(8,128)(2,1)S(1)}, u32[]{:S(2)}, u32[]{:S(2)}) collective-permute-start(bf16[128,128]{1,0:T(8,128)(2,1)S(1)} %get-tuple-element.29), channel_id=1, source_target_pairs={{0,256},{64,320},{128,384},{192,448},{256,0},{320,64},{384,128},{4... | collective-permute-start | bytes 98312 | tf_op jit(solution)/shard_map/ppermute | solution.py:226
  44.3 20.9 %collective-permute-start.4 = (bf16[128,128]{1,0:T(8,128)(2,1)S(1)}, bf16[128,128]{1,0:T(8,128)(2,1)S(1)}, u32[]{:S(2)}, u32[]{:S(2)}) collective-permute-start(bf16[128,128]{1,0:T(8,128)(2,1)S(1)} %get-tuple-element.30), channel_id=1, source_target_pairs={{0,320},{64,384},{128,448},{192,0},{256,64},{320,128},{384,192},{4... | collective-permute-start | bytes 98312 | tf_op jit(solution)/shard_map/ppermute | solution.py:226
  49.6 15.7 %collective-permute-start.5 = (bf16[128,128]{1,0:T(8,128)(2,1)S(1)}, bf16[128,128]{1,0:T(8,128)(2,1)S(1)}, u32[]{:S(2)}, u32[]{:S(2)}) collective-permute-start(bf16[128,128]{1,0:T(8,128)(2,1)S(1)} %get-tuple-element.31), channel_id=1, source_target_pairs={{0,384},{64,448},{128,0},{192,64},{256,128},{320,192},{384,256},{4... | collective-permute-start | bytes 98312 | tf_op jit(solution)/shard_map/ppermute | solution.py:226
  61.4 6.0 %collective-permute-start.6 = (bf16[128,128]{1,0:T(8,128)(2,1)S(1)}, bf16[128,128]{1,0:T(8,128)(2,1)S(1)}, u32[]{:S(2)}, u32[]{:S(2)}) collective-permute-start(bf16[128,128]{1,0:T(8,128)(2,1)S(1)} %get-tuple-element.32), channel_id=1, source_target_pairs={{0,448},{64,0},{128,64},{192,128},{256,192},{320,256},{384,320},{4... | collective-permute-start | bytes 98312 | tf_op jit(solution)/shard_map/ppermute | solution.py:226
  69.4 43.2 %all-to-all-start.1 = ((bf16[64,80,128]{2,1,0:T(8,128)(2,1)}), bf16[64,80,128]{2,1,0:T(8,128)(2,1)S(1)}, u32[]{:S(2)}, u32[]{:S(2)}) async-start(bf16[64,80,128]{2,1,0:T(8,128)(2,1)} %place.1), calls=%async_computation.1 | async-start | bytes 2621440 | tf_op jit(solution)/shard_map/all_to_all | solution.py:221
  79.0 76.3 %reduce-scatter.2.cloned.1.call-start = ((), (), s32[]{:S(2)}) async-start(), calls=%async_computation.5 | async-start | bytes 2064384 | tf_op jit(solution)/shard_map/reduce_scatter | solution.py:242
  79.0 10.8 %collective-permute-start.7 = (bf16[8,128,128]{2,1,0:T(8,128)(2,1)S(1)}, bf16[8,128,128]{2,1,0:T(8,128)(2,1)S(1)}, u32[]{:S(2)}, u32[]{:S(2)}) collective-permute-start(bf16[8,128,128]{2,1,0:T(8,128)(2,1)S(1)} %bitcast_dynamic-update-slice_fusion), channel_id=1, source_target_pairs={{0,2},{2,4},{4,6},{6,0},{1,3},{3,5},{5,7},{7,1},{8,10},{10,12},{12... | collective-permute-start | bytes 786440 | tf_op jit(solution)/shard_map/ppermute | solution.py:226
  81.3 12.1 %collective-permute-start.8 = (bf16[8,128,128]{2,1,0:T(8,128)(2,1)S(1)}, bf16[8,128,128]{2,1,0:T(8,128)(2,1)S(1)}, u32[]{:S(2)}, u32[]{:S(2)}) collective-permute-start(bf16[8,128,128]{2,1,0:T(8,128)(2,1)S(1)} %bitcast_dynamic-update-slice_fusion), channel_id=1, source_target_pairs={{0,4},{2,6},{4,0},{6,2},{1,5},{3,7},{5,1},{7,3},{8,12},{10,14},{12... | collective-permute-start | bytes 786440 | tf_op jit(solution)/shard_map/ppermute | solution.py:226
  85.8 10.9 %collective-permute-start.9 = (bf16[8,128,128]{2,1,0:T(8,128)(2,1)S(1)}, bf16[8,128,128]{2,1,0:T(8,128)(2,1)S(1)}, u32[]{:S(2)}, u32[]{:S(2)}) collective-permute-start(bf16[8,128,128]{2,1,0:T(8,128)(2,1)S(1)} %bitcast_dynamic-update-slice_fusion), channel_id=1, source_target_pairs={{0,6},{2,0},{4,2},{6,4},{1,7},{3,1},{5,3},{7,5},{8,14},{10,8},{12,... | collective-permute-start | bytes 786440 | tf_op jit(solution)/shard_map/ppermute | solution.py:226
  96.8 4.6 %collective-permute-start.10 = (bf16[4,8,128,128]{3,2,1,0:T(8,128)(2,1)S(1)}, bf16[4,8,128,128]{3,2,1,0:T(8,128)(2,1)S(1)}, u32[]{:S(2)}, u32[]{:S(2)}) collective-permute-start(bf16[4,8,128,128]{3,2,1,0:T(8,128)(2,1)S(1)} %pad_maximum_fusion.own_ref), channel_id=1, source_target_pairs={{0,1},{1,0},{2,3},{3,2},{4,5},{5,4},{6,7},{7,6},{8,9},{9,8},{10,11... | collective-permute-start | bytes 3145736 | tf_op jit(solution)/shard_map/ppermute | solution.py:226
  101.4 1.5 copy-start
  112.5 4.6 %copy-start.1 = (bf16[7168,128]{1,0:T(8,128)(2,1)S(1)}, bf16[7168,128]{1,0:T(8,128)(2,1)}, u32[]{:S(2)}) copy-start(bf16[7168,128]{1,0:T(8,128)(2,1)} %all-gather.3.cloned.1.call-done) | copy-start | bytes 5505028
  112.7 4.5 %collective-permute-start.11 = (bf16[56,64,128]{2,1,0:T(8,128)(2,1)S(1)}, bf16[56,64,128]{2,1,0:T(8,128)(2,1)S(1)}, u32[]{:S(2)}, u32[]{:S(2)}) collective-permute-start(bf16[56,64,128]{2,1,0:T(8,128)(2,1)S(1)} %slice.3.own_ref), channel_id=1, source_target_pairs={{0,1},{1,0},{2,3},{3,2},{4,5},{5,4},{6,7},{7,6},{8,9},{9,8},{10,11... | collective-permute-start | bytes 2752520 | tf_op jit(solution)/shard_map/ppermute | solution.py:226
  137.9 20.0 %all-to-all-start.3 = ((bf16[8,128,128]{2,1,0:T(8,128)(2,1)}), bf16[8,128,128]{2,1,0:T(8,128)(2,1)S(1)}, u32[]{:S(2)}, u32[]{:S(2)}) async-start(bf16[8,128,128]{2,1,0:T(8,128)(2,1)} %act_total.1), calls=%async_computation.3 | async-start | bytes 524288 | tf_op jit(solution)/shard_map/all_to_all | solution.py:221
  155.3 0.9 copy-start.4
Sparse Core Ops, SparseCore 0:
  29.3 57.1 all-gather.2
  112.7 42.5 reduce-scatter.1

commit v10 on v9

--- a/solution.py
+++ b/solution.py
@@ -53,11 +53,14 @@
 
 def place_kernel(offsets_ref, slots_ref, out_ref, rows_ref):
     lane = lax.broadcasted_iota(jnp.int32, (24, LANES), 1)
-    for k in range(SHARDS):
-        begin = offsets_ref[k]
+    begins = [offsets_ref[k] for k in range(SHARDS)]
+    rolled = [
+        pltpu.roll(slots_ref[k].astype(f32), begin % LANES, 1) for k, begin in enumerate(begins)
+    ]
+    for begin, turned in zip(begins, rolled):
         block = begin // LANES
         shift = begin % LANES
-        turned = pltpu.roll(slots_ref[k].astype(f32), shift, 1).reshape(3, 24, LANES)
+        turned = turned.reshape(3, 24, LANES)
         rows_ref[block] = jnp.where(lane >= shift, turned[0], rows_ref[block])
         rows_ref[block + 1] = jnp.where(lane >= shift, turned[1], turned[0])
         rows_ref[block + 2] = jnp.where(lane >= shift, turned[2], turned[1])

time: 166 us -> 166 us (level)
  the two profiles are of different devices: /device:TPU:30 before, /device:TPU:28 now
where the time goes in v10:
time: 166 us; the launch traced here: 165 us
  starting transfers between devices  80.3 us (48%)
  waiting for transfers between devices  37.4 us (23%)
  blocking collectives  17.3 us (10%)
  between operations  14.3 us (9%)
  Pallas kernels  11 us (7%)
  local copies, waits for them, and re-layouts  3.39 us (2%)
    ppermute x12, starting transfers between devices, shift(): return lax.ppermute(x, axis, [(i, (i + by) % n) for i in range(n)])  48.3 us
    all_to_all x3, starting transfers between devices, exchange(): return lax.all_to_all(x, axis, split_axis=0, concat_axis=0, tiled=True)  31.8 us
    ppermute x12, waiting for transfers between devices, shift(): return lax.ppermute(x, axis, [(i, (i + by) % n) for i in range(n)])  17.4 us
    all_to_all x1, blocking collectives, exchange(): return lax.all_to_all(x, axis, split_axis=0, concat_axis=0, tiled=True)  17.3 us
    reduce_scatter x1, waiting for transfers between devices, shards(): grad = lax.psum_scatter(parts, 'y', scatter_dimension=0)  12.2 us
    all_to_all x3, waiting for transfers between devices, exchange(): return lax.all_to_all(x, axis, split_axis=0, concat_axis=0, tiled=True)  7.03 us
  transfers between devices with their start and end apart: 17, of which 10 were waited for; matrix products, arithmetic and copies ran while one was open for 0% of the time, Pallas kernels for 6%

profile of v10, /device:TPU:28, one launch (start us, length us, event | category | flops | bytes accessed | tf_op | source)
XLA Modules:
  0.0 165.2 jit_solution(14337742834344300385)
XLA Ops:
  9.8 16.5 %all-to-all-start = ((bf16[64,72,128]{2,1,0:T(8,128)(2,1)}), bf16[64,72,128]{2,1,0:T(8,128)(2,1)S(1)}, u32[]{:S(2)}, u32[]{:S(2)}) async-start(bf16[64,72,128]{2,1,0:T(8,128)(2,1)} %pack.1), calls=%async_computation | async-start | bytes 2359296 | tf_op jit(solution)/shard_map/all_to_all | solution.py:224
  27.8 3.4 %collective-permute-start = (bf16[128,128]{1,0:T(8,128)(2,1)S(1)}, bf16[128,128]{1,0:T(8,128)(2,1)S(1)}, u32[]{:S(2)}, u32[]{:S(2)}) collective-permute-start(bf16[128,128]{1,0:T(8,128)(2,1)S(1)} %get-tuple-element.26), channel_id=1, source_target_pairs={{0,64},{64,128},{128,192},{192,256},{256,320},{320,384},{384,448},... | collective-permute-start | bytes 98312 | tf_op jit(solution)/shard_map/ppermute | solution.py:229
  31.2 4.3 %collective-permute-start.1 = (bf16[128,128]{1,0:T(8,128)(2,1)S(1)}, bf16[128,128]{1,0:T(8,128)(2,1)S(1)}, u32[]{:S(2)}, u32[]{:S(2)}) collective-permute-start(bf16[128,128]{1,0:T(8,128)(2,1)S(1)} %get-tuple-element.27), channel_id=1, source_target_pairs={{0,128},{64,192},{128,256},{192,320},{256,384},{320,448},{384,0},{... | collective-permute-start | bytes 98312 | tf_op jit(solution)/shard_map/ppermute | solution.py:229
  35.5 4.7 %collective-permute-start.2 = (bf16[128,128]{1,0:T(8,128)(2,1)S(1)}, bf16[128,128]{1,0:T(8,128)(2,1)S(1)}, u32[]{:S(2)}, u32[]{:S(2)}) collective-permute-start(bf16[128,128]{1,0:T(8,128)(2,1)S(1)} %get-tuple-element.28), channel_id=1, source_target_pairs={{0,192},{64,256},{128,320},{192,384},{256,448},{320,0},{384,64},{4... | collective-permute-start | bytes 98312 | tf_op jit(solution)/shard_map/ppermute | solution.py:229
  40.3 4.1 %collective-permute-start.3 = (bf16[128,128]{1,0:T(8,128)(2,1)S(1)}, bf16[128,128]{1,0:T(8,128)(2,1)S(1)}, u32[]{:S(2)}, u32[]{:S(2)}) collective-permute-start(bf16[128,128]{1,0:T(8,128)(2,1)S(1)} %get-tuple-element.29), channel_id=1, source_target_pairs={{0,256},{64,320},{128,384},{192,448},{256,0},{320,64},{384,128},{4... | collective-permute-start | bytes 98312 | tf_op jit(solution)/shard_map/ppermute | solution.py:229
  44.3 4.9 %collective-permute-start.4 = (bf16[128,128]{1,0:T(8,128)(2,1)S(1)}, bf16[128,128]{1,0:T(8,128)(2,1)S(1)}, u32[]{:S(2)}, u32[]{:S(2)}) collective-permute-start(bf16[128,128]{1,0:T(8,128)(2,1)S(1)} %get-tuple-element.30), channel_id=1, source_target_pairs={{0,320},{64,384},{128,448},{192,0},{256,64},{320,128},{384,192},{4... | collective-permute-start | bytes 98312 | tf_op jit(solution)/shard_map/ppermute | solution.py:229
  49.5 11.8 %collective-permute-start.5 = (bf16[128,128]{1,0:T(8,128)(2,1)S(1)}, bf16[128,128]{1,0:T(8,128)(2,1)S(1)}, u32[]{:S(2)}, u32[]{:S(2)}) collective-permute-start(bf16[128,128]{1,0:T(8,128)(2,1)S(1)} %get-tuple-element.31), channel_id=1, source_target_pairs={{0,384},{64,448},{128,0},{192,64},{256,128},{320,192},{384,256},{4... | collective-permute-start | bytes 98312 | tf_op jit(solution)/shard_map/ppermute | solution.py:229
  61.4 2.4 %collective-permute-start.6 = (bf16[128,128]{1,0:T(8,128)(2,1)S(1)}, bf16[128,128]{1,0:T(8,128)(2,1)S(1)}, u32[]{:S(2)}, u32[]{:S(2)}) collective-permute-start(bf16[128,128]{1,0:T(8,128)(2,1)S(1)} %get-tuple-element.32), channel_id=1, source_target_pairs={{0,448},{64,0},{128,64},{192,128},{256,192},{320,256},{384,320},{4... | collective-permute-start | bytes 98312 | tf_op jit(solution)/shard_map/ppermute | solution.py:229
  65.3 2.1 %collective-permute-done.6 = bf16[128,128]{1,0:T(8,128)(2,1)S(1)} collective-permute-done((bf16[128,128]{1,0:T(8,128)(2,1)S(1)}, bf16[128,128]{1,0:T(8,128)(2,1)S(1)}, u32[]{:S(2)}, u32[]{:S(2)}) %collective-permute-start.6) | collective-permute-done | bytes 32800 | tf_op jit(solution)/shard_map/ppermute | solution.py:229
  67.4 1.9 %place.1 = bf16[64,80,128]{2,1,0:T(8,128)(2,1)} custom-call(s32[25]{0:T(128)S(1)} %copy-done.5, bf16[64,72,128]{2,1,0:T(8,128)(2,1)S(1)} %all-to-all-done.slots_ref), custom_call_target="tpu_custom_call" | custom-call | tf_op jit(solution)/shard_map/place/pallas_call | solution.py:77
  69.3 9.6 %all-to-all-start.1 = ((bf16[64,80,128]{2,1,0:T(8,128)(2,1)}), bf16[64,80,128]{2,1,0:T(8,128)(2,1)S(1)}, u32[]{:S(2)}, u32[]{:S(2)}) async-start(bf16[64,80,128]{2,1,0:T(8,128)(2,1)} %place.1), calls=%async_computation.1 | async-start | bytes 2621440 | tf_op jit(solution)/shard_map/all_to_all | solution.py:224
  79.0 3.1 %collective-permute-start.7 = (bf16[8,128,128]{2,1,0:T(8,128)(2,1)S(1)}, bf16[8,128,128]{2,1,0:T(8,128)(2,1)S(1)}, u32[]{:S(2)}, u32[]{:S(2)}) collective-permute-start(bf16[8,128,128]{2,1,0:T(8,128)(2,1)S(1)} %bitcast_dynamic-update-slice_fusion), channel_id=1, source_target_pairs={{0,2},{2,4},{4,6},{6,0},{1,3},{3,5},{5,7},{7,1},{8,10},{10,12},{12... | collective-permute-start | bytes 786440 | tf_op jit(solution)/shard_map/ppermute | solution.py:229
  82.1 2.7 %collective-permute-start.8 = (bf16[8,128,128]{2,1,0:T(8,128)(2,1)S(1)}, bf16[8,128,128]{2,1,0:T(8,128)(2,1)S(1)}, u32[]{:S(2)}, u32[]{:S(2)}) collective-permute-start(bf16[8,128,128]{2,1,0:T(8,128)(2,1)S(1)} %bitcast_dynamic-update-slice_fusion), channel_id=1, source_target_pairs={{0,4},{2,6},{4,0},{6,2},{1,5},{3,7},{5,1},{7,3},{8,12},{10,14},{12... | collective-permute-start | bytes 786440 | tf_op jit(solution)/shard_map/ppermute | solution.py:229
  84.9 2.9 %collective-permute-start.9 = (bf16[8,128,128]{2,1,0:T(8,128)(2,1)S(1)}, bf16[8,128,128]{2,1,0:T(8,128)(2,1)S(1)}, u32[]{:S(2)}, u32[]{:S(2)}) collective-permute-start(bf16[8,128,128]{2,1,0:T(8,128)(2,1)S(1)} %bitcast_dynamic-update-slice_fusion), channel_id=1, source_target_pairs={{0,6},{2,0},{4,2},{6,4},{1,7},{3,1},{5,3},{7,5},{8,14},{10,8},{12,... | collective-permute-start | bytes 786440 | tf_op jit(solution)/shard_map/ppermute | solution.py:229
  88.8 4.1 %collective-permute-done.8 = bf16[8,128,128]{2,1,0:T(8,128)(2,1)S(1)} collective-permute-done((bf16[8,128,128]{2,1,0:T(8,128)(2,1)S(1)}, bf16[8,128,128]{2,1,0:T(8,128)(2,1)S(1)}, u32[]{:S(2)}, u32[]{:S(2)}) %collective-permute-start.8) | collective-permute-done | bytes 262176 | tf_op jit(solution)/shard_map/ppermute | solution.py:229
  92.9 3.5 %collective-permute-done.9 = bf16[8,128,128]{2,1,0:T(8,128)(2,1)S(1)} collective-permute-done((bf16[8,128,128]{2,1,0:T(8,128)(2,1)S(1)}, bf16[8,128,128]{2,1,0:T(8,128)(2,1)S(1)}, u32[]{:S(2)}, u32[]{:S(2)}) %collective-permute-start.9) | collective-permute-done | bytes 262176 | tf_op jit(solution)/shard_map/ppermute | solution.py:229
  98.5 2.6 %collective-permute-done.10.other_ref = bf16[4,8,128,128]{3,2,1,0:T(8,128)(2,1)S(1)} collective-permute-done((bf16[4,8,128,128]{3,2,1,0:T(8,128)(2,1)S(1)}, bf16[4,8,128,128]{3,2,1,0:T(8,128)(2,1)S(1)}, u32[]{:S(2)}, u32[]{:S(2)}) %collective-permute-start.10) | collective-permute-done | bytes 1048608 | tf_op jit(solution)/shard_map/ppermute | solution.py:229
  102.6 2.9 %grad_parts.1 = f32[8,448,128]{2,1,0:T(8,128)} custom-call(s32[4]{0:T(128)S(1)} %pad_add_fusion.place_ref, bf16[4,8,128,128]{3,2,1,0:T(8,128)(2,1)S(1)} %pad_maximum_fusion.own_ref, bf16[4,8,128,128]{3,2,1,0:T(8,128)(2,1)S(1)} %collective-permute-done.10.other_ref, bf16[8,2,448,128]{3,2,1,0:T(8,128)(2,1)S(1)} %bitcast.36), custom_call_target="tpu_custom_call" | custom-call | tf_op jit(solution)/shard_map/grad_parts/pallas_call | solution.py:176
  105.5 7.0 %all-to-all-done.1.state_ref = bf16[64,80,128]{2,1,0:T(8,128)(2,1)S(1)} async-done(((bf16[64,80,128]{2,1,0:T(8,128)(2,1)}), bf16[64,80,128]{2,1,0:T(8,128)(2,1)S(1)}, u32[]{:S(2)}, u32[]{:S(2)}) %all-to-all-start.1) | async-done | bytes 1310752 | tf_op jit(solution)/shard_map/all_to_all | solution.py:224
  112.7 2.1 %collective-permute-start.11 = (bf16[56,64,128]{2,1,0:T(8,128)(2,1)S(1)}, bf16[56,64,128]{2,1,0:T(8,128)(2,1)S(1)}, u32[]{:S(2)}, u32[]{:S(2)}) collective-permute-start(bf16[56,64,128]{2,1,0:T(8,128)(2,1)S(1)} %slice.3.own_ref), channel_id=1, source_target_pairs={{0,1},{1,0},{2,3},{3,2},{4,5},{5,4},{6,7},{7,6},{8,9},{9,8},{10,11... | collective-permute-start | bytes 2752520 | tf_op jit(solution)/shard_map/ppermute | solution.py:229
  114.7 2.4 %collective-permute-done.11.other_ref = bf16[56,64,128]{2,1,0:T(8,128)(2,1)S(1)} collective-permute-done((bf16[56,64,128]{2,1,0:T(8,128)(2,1)S(1)}, bf16[56,64,128]{2,1,0:T(8,128)(2,1)S(1)}, u32[]{:S(2)}, u32[]{:S(2)}) %collective-permute-start.11) | collective-permute-done | bytes 917536 | tf_op jit(solution)/shard_map/ppermute | solution.py:229
  119.0 17.3 %all_to_all.20.parts_ref = bf16[4,8,128,128]{3,2,1,0:T(8,128)(2,1)S(1)} all-to-all(bf16[4,8,128,128]{3,2,1,0:T(8,128)(2,1)S(1)} %act_sums.1), channel_id=1, replica_groups=mesh['z'=8,'y'=8,'x'=4,'c'=2] {'x'}, dimensions={0} | all-to-all | bytes 2097152 | tf_op jit(solution)/shard_map/all_to_all | solution.py:224
  137.2 5.7 %all-to-all-start.3 = ((bf16[8,128,128]{2,1,0:T(8,128)(2,1)}), bf16[8,128,128]{2,1,0:T(8,128)(2,1)S(1)}, u32[]{:S(2)}, u32[]{:S(2)}) async-start(bf16[8,128,128]{2,1,0:T(8,128)(2,1)} %act_total.1), calls=%async_computation.3 | async-start | bytes 524288 | tf_op jit(solution)/shard_map/all_to_all | solution.py:224
  142.9 12.2 %reduce-scatter.2.cloned.1.call-done = f32[1,448,128]{2,1,0:T(8,128)} async-done(((f32[8,448,128]{2,1,0:T(8,128)}), f32[1,448,128]{2,1,0:T(8,128)}) %reduce-scatter.2.cloned.1.call-update) | async-done | bytes 229392 | tf_op jit(solution)/shard_map/reduce_scatter | solution.py:245
  (45 shorter events, 16.6 us)
Async XLA Ops:
  7.2 1.5 copy-start.2
  9.8 17.3 %copy-start.3 = (bf16[16,8192]{1,0:T(8,128)(2,1)S(1)}, bf16[16,8192]{1,0:T(8,128)(2,1)}, u32[]{:S(2)}) copy-start(bf16[16,8192]{1,0:T(8,128)(2,1)} %act_ref.1) | copy-start | bytes 786436
  9.8 57.6 %copy-start.5 = (s32[25]{0:T(128)S(1)}, s32[25]{0:T(128)}, u32[]{:S(2)}) copy-start(s32[25]{0:T(128)} %offsets_ref.1) | copy-start | bytes 304
  9.8 57.6 %all-to-all-start = ((bf16[64,72,128]{2,1,0:T(8,128)(2,1)}), bf16[64,72,128]{2,1,0:T(8,128)(2,1)S(1)}, u32[]{:S(2)}, u32[]{:S(2)}) async-start(bf16[64,72,128]{2,1,0:T(8,128)(2,1)} %pack.1), calls=%async_computation | async-start | bytes 2359296 | tf_op jit(solution)/shard_map/all_to_all | solution.py:224
  26.3 70.2 %all-gather.3.cloned.1.call-start = ((), (), s32[]{:S(2)}) async-start(), calls=%async_computation.6 | async-start | bytes 1949696 | tf_op jit(solution)/shard_map/all_gather | solution.py:234
  27.8 21.8 %collective-permute-start = (bf16[128,128]{1,0:T(8,128)(2,1)S(1)}, bf16[128,128]{1,0:T(8,128)(2,1)S(1)}, u32[]{:S(2)}, u32[]{:S(2)}) collective-permute-start(bf16[128,128]{1,0:T(8,128)(2,1)S(1)} %get-tuple-element.26), channel_id=1, source_target_pairs={{0,64},{64,128},{128,192},{192,256},{256,320},{320,384},{384,448},... | collective-permute-start | bytes 98312 | tf_op jit(solution)/shard_map/ppermute | solution.py:229
  31.2 30.2 %collective-permute-start.1 = (bf16[128,128]{1,0:T(8,128)(2,1)S(1)}, bf16[128,128]{1,0:T(8,128)(2,1)S(1)}, u32[]{:S(2)}, u32[]{:S(2)}) collective-permute-start(bf16[128,128]{1,0:T(8,128)(2,1)S(1)} %get-tuple-element.27), channel_id=1, source_target_pairs={{0,128},{64,192},{128,256},{192,320},{256,384},{320,448},{384,0},{... | collective-permute-start | bytes 98312 | tf_op jit(solution)/shard_map/ppermute | solution.py:229
  35.5 28.4 %collective-permute-start.2 = (bf16[128,128]{1,0:T(8,128)(2,1)S(1)}, bf16[128,128]{1,0:T(8,128)(2,1)S(1)}, u32[]{:S(2)}, u32[]{:S(2)}) collective-permute-start(bf16[128,128]{1,0:T(8,128)(2,1)S(1)} %get-tuple-element.28), channel_id=1, source_target_pairs={{0,192},{64,256},{128,320},{192,384},{256,448},{320,0},{384,64},{4... | collective-permute-start | bytes 98312 | tf_op jit(solution)/shard_map/ppermute | solution.py:229
  40.3 25.0 %collective-permute-start.3 = (bf16[128,128]{1,0:T(8,128)(2,1)S(1)}, bf16[128,128]{1,0:T(8,128)(2,1)S(1)}, u32[]{:S(2)}, u32[]{:S(2)}) collective-permute-start(bf16[128,128]{1,0:T(8,128)(2,1)S(1)} %get-tuple-element.29), channel_id=1, source_target_pairs={{0,256},{64,320},{128,384},{192,448},{256,0},{320,64},{384,128},{4... | collective-permute-start | bytes 98312 | tf_op jit(solution)/shard_map/ppermute | solution.py:229
  44.3 20.9 %collective-permute-start.4 = (bf16[128,128]{1,0:T(8,128)(2,1)S(1)}, bf16[128,128]{1,0:T(8,128)(2,1)S(1)}, u32[]{:S(2)}, u32[]{:S(2)}) collective-permute-start(bf16[128,128]{1,0:T(8,128)(2,1)S(1)} %get-tuple-element.30), channel_id=1, source_target_pairs={{0,320},{64,384},{128,448},{192,0},{256,64},{320,128},{384,192},{4... | collective-permute-start | bytes 98312 | tf_op jit(solution)/shard_map/ppermute | solution.py:229
  49.5 15.7 %collective-permute-start.5 = (bf16[128,128]{1,0:T(8,128)(2,1)S(1)}, bf16[128,128]{1,0:T(8,128)(2,1)S(1)}, u32[]{:S(2)}, u32[]{:S(2)}) collective-permute-start(bf16[128,128]{1,0:T(8,128)(2,1)S(1)} %get-tuple-element.31), channel_id=1, source_target_pairs={{0,384},{64,448},{128,0},{192,64},{256,128},{320,192},{384,256},{4... | collective-permute-start | bytes 98312 | tf_op jit(solution)/shard_map/ppermute | solution.py:229
  61.4 6.0 %collective-permute-start.6 = (bf16[128,128]{1,0:T(8,128)(2,1)S(1)}, bf16[128,128]{1,0:T(8,128)(2,1)S(1)}, u32[]{:S(2)}, u32[]{:S(2)}) collective-permute-start(bf16[128,128]{1,0:T(8,128)(2,1)S(1)} %get-tuple-element.32), channel_id=1, source_target_pairs={{0,448},{64,0},{128,64},{192,128},{256,192},{320,256},{384,320},{4... | collective-permute-start | bytes 98312 | tf_op jit(solution)/shard_map/ppermute | solution.py:229
  69.3 43.2 %all-to-all-start.1 = ((bf16[64,80,128]{2,1,0:T(8,128)(2,1)}), bf16[64,80,128]{2,1,0:T(8,128)(2,1)S(1)}, u32[]{:S(2)}, u32[]{:S(2)}) async-start(bf16[64,80,128]{2,1,0:T(8,128)(2,1)} %place.1), calls=%async_computation.1 | async-start | bytes 2621440 | tf_op jit(solution)/shard_map/all_to_all | solution.py:224
  79.0 76.2 %reduce-scatter.2.cloned.1.call-start = ((), (), s32[]{:S(2)}) async-start(), calls=%async_computation.5 | async-start | bytes 2064384 | tf_op jit(solution)/shard_map/reduce_scatter | solution.py:245
  79.0 9.8 %collective-permute-start.7 = (bf16[8,128,128]{2,1,0:T(8,128)(2,1)S(1)}, bf16[8,128,128]{2,1,0:T(8,128)(2,1)S(1)}, u32[]{:S(2)}, u32[]{:S(2)}) collective-permute-start(bf16[8,128,128]{2,1,0:T(8,128)(2,1)S(1)} %bitcast_dynamic-update-slice_fusion), channel_id=1, source_target_pairs={{0,2},{2,4},{4,6},{6,0},{1,3},{3,5},{5,7},{7,1},{8,10},{10,12},{12... | collective-permute-start | bytes 786440 | tf_op jit(solution)/shard_map/ppermute | solution.py:229
  82.1 10.8 %collective-permute-start.8 = (bf16[8,128,128]{2,1,0:T(8,128)(2,1)S(1)}, bf16[8,128,128]{2,1,0:T(8,128)(2,1)S(1)}, u32[]{:S(2)}, u32[]{:S(2)}) collective-permute-start(bf16[8,128,128]{2,1,0:T(8,128)(2,1)S(1)} %bitcast_dynamic-update-slice_fusion), channel_id=1, source_target_pairs={{0,4},{2,6},{4,0},{6,2},{1,5},{3,7},{5,1},{7,3},{8,12},{10,14},{12... | collective-permute-start | bytes 786440 | tf_op jit(solution)/shard_map/ppermute | solution.py:229
  84.9 11.5 %collective-permute-start.9 = (bf16[8,128,128]{2,1,0:T(8,128)(2,1)S(1)}, bf16[8,128,128]{2,1,0:T(8,128)(2,1)S(1)}, u32[]{:S(2)}, u32[]{:S(2)}) collective-permute-start(bf16[8,128,128]{2,1,0:T(8,128)(2,1)S(1)} %bitcast_dynamic-update-slice_fusion), channel_id=1, source_target_pairs={{0,6},{2,0},{4,2},{6,4},{1,7},{3,1},{5,3},{7,5},{8,14},{10,8},{12,... | collective-permute-start | bytes 786440 | tf_op jit(solution)/shard_map/ppermute | solution.py:229
  96.5 4.6 %collective-permute-start.10 = (bf16[4,8,128,128]{3,2,1,0:T(8,128)(2,1)S(1)}, bf16[4,8,128,128]{3,2,1,0:T(8,128)(2,1)S(1)}, u32[]{:S(2)}, u32[]{:S(2)}) collective-permute-start(bf16[4,8,128,128]{3,2,1,0:T(8,128)(2,1)S(1)} %pad_maximum_fusion.own_ref), channel_id=1, source_target_pairs={{0,1},{1,0},{2,3},{3,2},{4,5},{5,4},{6,7},{7,6},{8,9},{9,8},{10,11... | collective-permute-start | bytes 3145736 | tf_op jit(solution)/shard_map/ppermute | solution.py:229
  101.1 1.5 copy-start
  112.6 4.6 %copy-start.1 = (bf16[7168,128]{1,0:T(8,128)(2,1)S(1)}, bf16[7168,128]{1,0:T(8,128)(2,1)}, u32[]{:S(2)}) copy-start(bf16[7168,128]{1,0:T(8,128)(2,1)} %all-gather.3.cloned.1.call-done) | copy-start | bytes 5505028
  112.7 4.5 %collective-permute-start.11 = (bf16[56,64,128]{2,1,0:T(8,128)(2,1)S(1)}, bf16[56,64,128]{2,1,0:T(8,128)(2,1)S(1)}, u32[]{:S(2)}, u32[]{:S(2)}) collective-permute-start(bf16[56,64,128]{2,1,0:T(8,128)(2,1)S(1)} %slice.3.own_ref), channel_id=1, source_target_pairs={{0,1},{1,0},{2,3},{3,2},{4,5},{5,4},{6,7},{7,6},{8,9},{9,8},{10,11... | collective-permute-start | bytes 2752520 | tf_op jit(solution)/shard_map/ppermute | solution.py:229
  137.2 20.5 %all-to-all-start.3 = ((bf16[8,128,128]{2,1,0:T(8,128)(2,1)}), bf16[8,128,128]{2,1,0:T(8,128)(2,1)S(1)}, u32[]{:S(2)}, u32[]{:S(2)}) async-start(bf16[8,128,128]{2,1,0:T(8,128)(2,1)} %act_total.1), calls=%async_computation.3 | async-start | bytes 524288 | tf_op jit(solution)/shard_map/all_to_all | solution.py:224
  155.2 0.9 copy-start.4
Sparse Core Ops, SparseCore 0:
  29.3 57.3 all-gather.2
  112.7 42.4 reduce-scatter.1
